TPU v7x, 32 devices: a whole 2x2x4 slice. The times are simulated.
32 devices in a mesh: expert: 8 (over y, x, core), wshard: 4 (over z).
Axes of the slice: x: 2, y: 2, z: 4, core: 2. Of those that a mesh axis runs over, the one named last changes fastest.
Arguments:
- hidden_in: bfloat16 [2, 8, 256, 2048], P(None, 'expert', 'wshard'), may hold values from -6 to 6
- doc_ids: int32 [2, 8, 256], P(None, 'expert'), may hold values from 0 to 2, as said below
- routes: int32 [2, 8, 256, 8], P(None, 'expert', 'wshard'), may hold values from 0 to 15, all different within a row; in each aligned block of 64 rows (0 to 63, 64 to 127, ..., all dimensions but the last counted through in order) at most 36 rows name the same one
- attn_gain: float32 [2048], replicated, may hold values from 0.1 to 1.9
- q_gain: float32 [2048], replicated, may hold values from 0.1 to 1.9
- k_gain: float32 [2048], replicated, may hold values from 0.1 to 1.9
- ffn_gain: float32 [2048], replicated, may hold values from 0.1 to 1.9
- w_qkv: bfloat16 [2048, 6144], P('wshard'), may hold values from -0.125 to 0.125
- w_out: bfloat16 [2048, 2048], P('wshard'), may hold values from -0.5 to 0.5
- w_router: bfloat16 [2048, 16], P('wshard'), may hold values from -0.0625 to 0.0625
- w_gate_up: bfloat16 [16, 2048, 2048], P('expert', 'wshard'), may hold values from -0.125 to 0.125
- w_down: bfloat16 [16, 1024, 2048], P('expert', None, 'wshard'), may hold values from -6 to 6
- cotangent: bfloat16 [2, 8, 256, 2048], P(None, 'expert', 'wshard'), may hold values from -6 to 6
Outputs:
- hidden_out: bfloat16 [2, 8, 256, 2048], P(None, 'expert', 'wshard')
- grad_in: bfloat16 [2, 8, 256, 2048], P(None, 'expert', 'wshard')
- grad_attn_gain: float32 [2048], P(('expert', 'wshard'))
- grad_q_gain: float32 [2048], P(('expert', 'wshard'))
- grad_k_gain: float32 [2048], P(('expert', 'wshard'))
- grad_ffn_gain: float32 [2048], P(('expert', 'wshard'))
- grad_qkv: float32 [2048, 6144], P(('expert', 'wshard'))
- grad_out_proj: float32 [2048, 2048], P(('expert', 'wshard'))
- grad_router: float32 [2048, 16], P(('expert', 'wshard'))
- grad_gate_up: float32 [16, 2048, 2048], P('expert', 'wshard')
- grad_down: float32 [16, 1024, 2048], P('expert', None, 'wshard')
Inputs may be any that keep to these rules, and one draw needn't show every extreme that they name: `doc_ids`: along a sequence the numbers never fall and take 0, 1 and 2: document 0 ends within the first 32 positions, document 2 begins within the last 32 positions. `routes`: each row names 8 different experts. In each aligned block of 64 rows (one device's rows of one micro-batch) no expert is named by more than 36 rows, and in some blocks one is named by exactly 36.
All inputs are finite; a program needn't handle non-finite values.
Results may differ from a plain program's by a relative error of at most 0.02.
Values may be sent and summed in bfloat16 or wider, within the bound.
No kernel may reach another device: no remote copies, remote signals or barrier semaphores. Data moves between devices by JAX's collectives and lax.ppermute only.
A program may use at most 384 MiB of HBM per device.

v0:
```python
import jax
import jax.numpy as jnp
from jax import lax
from jax.sharding import PartitionSpec as P

HEADS = 16


EPS = 1e-05
THETA = 10000.0


def rms_scale(values):
    return lax.rsqrt(jnp.mean(values * values, axis=-1, keepdims=True) + EPS)


def rotary_tables(positions, head_size):
    half = head_size // 2
    freq = THETA ** (-(jnp.arange(half, dtype=jnp.float32) * 2.0 / head_size))
    angle = positions.astype(jnp.float32)[:, None] * freq[None, :]
    return (jnp.cos(angle)[:, None, :], jnp.sin(angle)[:, None, :])


def rotate(values, cosine, sine):
    half = values.shape[-1] // 2
    first = values[..., :half]
    second = values[..., half:]
    return jnp.concatenate(
        [first * cosine - second * sine, second * cosine + first * sine], axis=-1
    )


def rotate_back(grads, cosine, sine):
    half = grads.shape[-1] // 2
    first = grads[..., :half]
    second = grads[..., half:]
    return jnp.concatenate(
        [first * cosine + second * sine, second * cosine - first * sine], axis=-1
    )


def norm_back(values, scale, gain, grads):
    weighted = gain * grads
    inner = jnp.mean(values * weighted, axis=-1, keepdims=True)
    value_grad = scale * weighted - values * scale * scale * scale * inner
    return (value_grad, jnp.sum(grads * values * scale, axis=0))


def silu_parts(gate):
    sigma = jax.nn.sigmoid(gate)
    return (gate * sigma, sigma * (1.0 + gate * (1.0 - sigma)))


def local(
    hidden_in,
    doc_ids,
    routes,
    attn_gain,
    q_gain,
    k_gain,
    ffn_gain,
    w_qkv,
    w_out,
    w_router,
    w_gate_up,
    w_down,
    cotangent,
):
    micro_count = hidden_in.shape[0]
    tok_rows = hidden_in.shape[2]
    width = hidden_in.shape[3]
    top_count = routes.shape[3]
    heads = HEADS
    head_size = width // heads
    expert_count = w_router.shape[1]
    local_experts = w_gate_up.shape[0]
    hidden_units = w_down.shape[1]
    capacity = (tok_rows * top_count * 9 + 8 * expert_count - 1) // (8 * expert_count)
    slots = expert_count * capacity
    seq_len = doc_ids.shape[2]
    shard = lax.axis_index("wshard")
    key_pos = jnp.arange(seq_len, dtype=jnp.int32)
    query_pos = shard * tok_rows + jnp.arange(tok_rows, dtype=jnp.int32)
    cosine, sine = rotary_tables(query_pos, head_size)
    causal = key_pos[None, :] <= query_pos[:, None]
    scale = head_size ** (-0.5)
    expert_ids = jnp.arange(expert_count, dtype=jnp.int32)
    expert_up, expert_down = (
        lax.all_gather(w_gate_up, "wshard", axis=1, tiled=True),
        lax.all_gather(w_down, "wshard", axis=2, tiled=True),
    )
    mixer_totals = (
        jnp.zeros((width, 3 * width), jnp.float32),
        jnp.zeros((width, width), jnp.float32),
        jnp.zeros((width, expert_count), jnp.float32),
        jnp.zeros((width,), jnp.float32),
        jnp.zeros((width,), jnp.float32),
        jnp.zeros((width,), jnp.float32),
        jnp.zeros((width,), jnp.float32),
    )
    expert_totals = (
        jnp.zeros((local_experts, width, 2 * hidden_units), jnp.float32),
        jnp.zeros((local_experts, hidden_units, width), jnp.float32),
    )
    outputs_list = []
    input_grads = []
    for micro in range(micro_count):
        full_qkv, full_out, full_router = (
            lax.all_gather(w_qkv, "wshard", axis=0, tiled=True),
            lax.all_gather(w_out, "wshard", axis=0, tiled=True),
            lax.all_gather(w_router, "wshard", axis=0, tiled=True),
        )
        tokens = hidden_in[micro, 0].astype(jnp.float32)
        doc_row = doc_ids[micro, 0]
        query_doc = lax.dynamic_slice_in_dim(doc_row, shard * tok_rows, tok_rows)
        allowed = causal & (doc_row[None, :] == query_doc[:, None])
        choose = routes[micro, 0]
        scale_one = rms_scale(tokens)
        normed = (tokens * scale_one * attn_gain).astype(jnp.bfloat16)
        projected = jnp.dot(normed, full_qkv, preferred_element_type=jnp.float32)
        query_raw = projected[:, :width]
        key_raw = projected[:, width : 2 * width]
        value_raw = projected[:, 2 * width :]
        query_scale = rms_scale(query_raw)
        key_scale = rms_scale(key_raw)
        query_rot = rotate(
            (query_raw * query_scale * q_gain).reshape(tok_rows, heads, head_size), cosine, sine
        ).astype(jnp.bfloat16)
        key_rot = rotate(
            (key_raw * key_scale * k_gain).reshape(tok_rows, heads, head_size), cosine, sine
        ).astype(jnp.bfloat16)
        value_low = value_raw.astype(jnp.bfloat16)
        keys_all, values_all = (
            lax.all_gather(key_rot.reshape(tok_rows, width), "wshard", axis=0, tiled=True),
            lax.all_gather(value_low, "wshard", axis=0, tiled=True),
        )
        keys_all = keys_all.reshape(seq_len, heads, head_size)
        values_all = values_all.reshape(seq_len, heads, head_size)
        scores = (
            jnp.einsum("qhd,khd->hqk", query_rot, keys_all, preferred_element_type=jnp.float32)
            * scale
        )
        scores = jnp.where(allowed[None], scores, -1e30)
        peak = jnp.max(scores, axis=-1, keepdims=True)
        expo = jnp.exp(scores - peak)
        total = jnp.sum(expo, axis=-1, keepdims=True)
        log_total = peak + jnp.log(total)
        probs_low = (expo / total).astype(jnp.bfloat16)
        attended = jnp.einsum(
            "hqk,khd->qhd", probs_low, values_all, preferred_element_type=jnp.float32
        )
        attended = attended.reshape(tok_rows, width).astype(jnp.bfloat16)
        resid = tokens + jnp.dot(attended, full_out, preferred_element_type=jnp.float32)
        scale_two = rms_scale(resid)
        ffn_in = (resid * scale_two * ffn_gain).astype(jnp.bfloat16)
        logits = jnp.dot(ffn_in, full_router, preferred_element_type=jnp.float32)
        gate_all = jax.nn.softmax(logits, axis=-1)
        expert_hot = choose[:, :, None] == expert_ids[None, None, :]
        gates = jnp.sum(jnp.where(expert_hot, gate_all[:, None, :], 0.0), axis=-1)
        flat_ids = choose.reshape(-1)
        flat_hot = (flat_ids[:, None] == expert_ids[None, :]).astype(jnp.int32)
        rank = jnp.sum((jnp.cumsum(flat_hot, axis=0) - flat_hot) * flat_hot, axis=1)
        slot = flat_ids * capacity + rank
        assign = (
            jnp.zeros((slots,), jnp.int32)
            .at[slot]
            .set(jnp.arange(tok_rows * top_count, dtype=jnp.int32))
        )
        filled = jnp.zeros((slots,), jnp.bool_).at[slot].set(True)
        send = jnp.where(filled[:, None], ffn_in[assign // top_count], jnp.zeros((), jnp.bfloat16))
        rows = lax.all_to_all(
            send.reshape(expert_count, capacity, width),
            "expert",
            split_axis=0,
            concat_axis=1,
            tiled=True,
        )
        gate_up = jnp.einsum("erd,edf->erf", rows, expert_up, preferred_element_type=jnp.float32)
        gate_part = gate_up[..., :hidden_units]
        up_part = gate_up[..., hidden_units:]
        silu_value, silu_slope = silu_parts(gate_part)
        activated = (silu_value * up_part).astype(jnp.bfloat16)
        expert_out = jnp.einsum(
            "erf,efd->erd", activated, expert_down, preferred_element_type=jnp.float32
        ).astype(jnp.bfloat16)
        returned = lax.all_to_all(
            expert_out, "expert", split_axis=1, concat_axis=0, tiled=True
        ).reshape(slots, width)
        picked = returned[slot].reshape(tok_rows, top_count, width).astype(jnp.float32)
        mixture = jnp.einsum("tk,tkd->td", gates, picked)
        outputs_list.append((resid + mixture).astype(jnp.bfloat16))
        upstream = cotangent[micro, 0].astype(jnp.float32)
        gate_grad = jnp.einsum("tkd,td->tk", picked, upstream)
        slot_grads = (
            (gates[:, :, None] * upstream[:, None, :])
            .astype(jnp.bfloat16)
            .reshape(tok_rows * top_count, width)
        )
        send_back = jnp.where(filled[:, None], slot_grads[assign], jnp.zeros((), jnp.bfloat16))
        row_grads = lax.all_to_all(
            send_back.reshape(expert_count, capacity, width),
            "expert",
            split_axis=0,
            concat_axis=1,
            tiled=True,
        )
        down_grad = jnp.einsum(
            "erf,erd->efd", activated, row_grads, preferred_element_type=jnp.float32
        )
        act_grad = jnp.einsum(
            "erd,efd->erf", row_grads, expert_down, preferred_element_type=jnp.float32
        )
        gate_up_grad = jnp.concatenate(
            [act_grad * up_part * silu_slope, act_grad * silu_value], axis=-1
        ).astype(jnp.bfloat16)
        up_grad = jnp.einsum("erd,erf->edf", rows, gate_up_grad, preferred_element_type=jnp.float32)
        input_rows = jnp.einsum(
            "erf,edf->erd", gate_up_grad, expert_up, preferred_element_type=jnp.float32
        ).astype(jnp.bfloat16)
        returned_grads = lax.all_to_all(
            input_rows, "expert", split_axis=1, concat_axis=0, tiled=True
        ).reshape(slots, width)
        ffn_grad = jnp.sum(
            returned_grads[slot].reshape(tok_rows, top_count, width).astype(jnp.float32), axis=1
        )
        gate_total = jnp.sum(jnp.where(expert_hot, gate_grad[:, :, None], 0.0), axis=1)
        logit_grad = gate_all * (
            gate_total - jnp.sum(gate_all * gate_total, axis=-1, keepdims=True)
        )
        logit_grad = logit_grad.astype(jnp.bfloat16)
        router_grad = jnp.dot(ffn_in.T, logit_grad, preferred_element_type=jnp.float32)
        ffn_grad = ffn_grad + jnp.dot(logit_grad, full_router.T, preferred_element_type=jnp.float32)
        resid_grad, ffn_gain_grad = norm_back(resid, scale_two, ffn_gain, ffn_grad)
        resid_grad = resid_grad + upstream
        branch_grad = resid_grad.astype(jnp.bfloat16)
        out_grad = jnp.dot(attended.T, branch_grad, preferred_element_type=jnp.float32)
        attended_grad = jnp.dot(branch_grad, full_out.T, preferred_element_type=jnp.float32).astype(
            jnp.bfloat16
        )
        attended_grad = attended_grad.reshape(tok_rows, heads, head_size)
        again = (
            jnp.einsum("qhd,khd->hqk", query_rot, keys_all, preferred_element_type=jnp.float32)
            * scale
        )
        probs_again = jnp.where(allowed[None], jnp.exp(again - log_total), 0.0)
        prob_grad = jnp.einsum(
            "qhd,khd->hqk", attended_grad, values_all, preferred_element_type=jnp.float32
        )
        inner = jnp.sum(probs_again * prob_grad, axis=-1, keepdims=True)
        score_grad = (probs_again * (prob_grad - inner)).astype(jnp.bfloat16)
        query_grad = (
            jnp.einsum("hqk,khd->qhd", score_grad, keys_all, preferred_element_type=jnp.float32)
            * scale
        )
        key_part = (
            jnp.einsum("hqk,qhd->khd", score_grad, query_rot, preferred_element_type=jnp.float32)
            * scale
        )
        value_part = jnp.einsum(
            "hqk,qhd->khd",
            probs_again.astype(jnp.bfloat16),
            attended_grad,
            preferred_element_type=jnp.float32,
        )
        key_grad, value_grad = (
            lax.psum_scatter(
                key_part.reshape(seq_len, width).astype(jnp.bfloat16),
                "wshard",
                scatter_dimension=0,
                tiled=True,
            ).astype(jnp.float32),
            lax.psum_scatter(
                value_part.reshape(seq_len, width).astype(jnp.bfloat16),
                "wshard",
                scatter_dimension=0,
                tiled=True,
            ).astype(jnp.float32),
        )
        query_norm_grad = rotate_back(query_grad, cosine, sine).reshape(tok_rows, width)
        key_norm_grad = rotate_back(
            key_grad.reshape(tok_rows, heads, head_size), cosine, sine
        ).reshape(tok_rows, width)
        query_in_grad, q_gain_grad = norm_back(query_raw, query_scale, q_gain, query_norm_grad)
        key_in_grad, k_gain_grad = norm_back(key_raw, key_scale, k_gain, key_norm_grad)
        proj_grad = jnp.concatenate([query_in_grad, key_in_grad, value_grad], axis=-1).astype(
            jnp.bfloat16
        )
        qkv_grad = jnp.dot(normed.T, proj_grad, preferred_element_type=jnp.float32)
        normed_grad = jnp.dot(proj_grad, full_qkv.T, preferred_element_type=jnp.float32)
        token_grad, attn_gain_grad = norm_back(tokens, scale_one, attn_gain, normed_grad)
        input_grads.append((token_grad + resid_grad).astype(jnp.bfloat16))
        shares = (
            qkv_grad,
            out_grad,
            router_grad,
            attn_gain_grad,
            q_gain_grad,
            k_gain_grad,
            ffn_gain_grad,
        )
        expert_shares = (up_grad, down_grad)
        mixer_totals = jax.tree.map(jnp.add, mixer_totals, shares)
        expert_totals = jax.tree.map(jnp.add, expert_totals, expert_shares)
    total_qkv, total_out, total_router, total_attn, total_query, total_key, total_ffn = mixer_totals
    total_up, total_down = expert_totals
    final_mixer = (
        lax.psum_scatter(total_qkv, ("expert", "wshard"), scatter_dimension=0, tiled=True),
        lax.psum_scatter(total_out, ("expert", "wshard"), scatter_dimension=0, tiled=True),
        lax.psum_scatter(total_router, ("expert", "wshard"), scatter_dimension=0, tiled=True),
        lax.psum_scatter(total_attn, ("expert", "wshard"), scatter_dimension=0, tiled=True),
        lax.psum_scatter(total_query, ("expert", "wshard"), scatter_dimension=0, tiled=True),
        lax.psum_scatter(total_key, ("expert", "wshard"), scatter_dimension=0, tiled=True),
        lax.psum_scatter(total_ffn, ("expert", "wshard"), scatter_dimension=0, tiled=True),
    )
    final_expert = (
        lax.psum_scatter(
            total_up.astype(jnp.bfloat16), "wshard", scatter_dimension=1, tiled=True
        ).astype(jnp.float32),
        lax.psum_scatter(
            total_down.astype(jnp.bfloat16), "wshard", scatter_dimension=2, tiled=True
        ).astype(jnp.float32),
    )
    hidden_out = jnp.stack(outputs_list)[:, None]
    grad_in = jnp.stack(input_grads)[:, None]
    return (
        hidden_out,
        grad_in,
        final_mixer[3],
        final_mixer[4],
        final_mixer[5],
        final_mixer[6],
        final_mixer[0],
        final_mixer[1],
        final_mixer[2],
        final_expert[0],
        final_expert[1],
    )


def solution(mesh):
    in_specs = (
        P(None, "expert", "wshard", None),
        P(None, "expert", None),
        P(None, "expert", "wshard", None),
        P(),
        P(),
        P(),
        P(),
        P("wshard", None),
        P("wshard", None),
        P("wshard", None),
        P("expert", "wshard", None),
        P("expert", None, "wshard"),
        P(None, "expert", "wshard", None),
    )
    out_specs = (
        P(None, "expert", "wshard", None),
        P(None, "expert", "wshard", None),
        P(("expert", "wshard")),
        P(("expert", "wshard")),
        P(("expert", "wshard")),
        P(("expert", "wshard")),
        P(("expert", "wshard"), None),
        P(("expert", "wshard"), None),
        P(("expert", "wshard"), None),
        P("expert", "wshard", None),
        P("expert", None, "wshard"),
    )
    return jax.shard_map(local, mesh=mesh, in_specs=in_specs, out_specs=out_specs, check_vma=False)
```

profile of v0, /device:TPU:0, one launch (start us, length us, event | category | flops | bytes accessed | tf_op | source)
XLA Modules:
  0.0 3020.0 jit_solution(15646015796822386503)
XLA Ops:
  8.7 428.9 %all-gather.9.cloned.1.call-done = bf16[2048,6144]{1,0:T(8,128)(2,1)} async-done(((bf16[512,6144]{1,0:T(8,128)(2,1)}), bf16[2048,6144]{1,0:T(8,128)(2,1)}) %all-gather.9.cloned.1.call-update) | async-done | bytes 25165840 | tf_op jit(solution)/shard_map/all_gather | solution.py:109
  448.4 10.9 fusion.129
  475.3 15.6 all-gather.13.cloned.1.call-done
  493.4 27.2 all-gather.11.cloned.1.call-done
  522.4 148.8 %all-gather.15.cloned.1.call-done = bf16[2048,2048]{1,0:T(8,128)(2,1)} async-done(((bf16[512,2048]{1,0:T(8,128)(2,1)}), bf16[2048,2048]{1,0:T(8,128)(2,1)}) %all-gather.15.cloned.1.call-update) | async-done | bytes 8388624 | tf_op jit(solution)/shard_map/all_gather | solution.py:110
  686.9 35.7 %all_to_all.132 = bf16[16,36,2048]{2,1,0:T(8,128)(2,1)S(1)} all-to-all(bf16[16,36,2048]{2,1,0:T(8,128)(2,1)S(1)} %broadcast_select_fusion.3), channel_id=1, replica_groups=mesh['expert'=8,'wshard'=4] {'expert'}, dimensions={0} | all-to-all | bytes 4718592 | tf_op jit(solution)/shard_map/all_to_all | solution.py:171
  726.4 231.4 %all-gather.17.cloned.1.call-done = bf16[2,2048,2048]{2,1,0:T(8,128)(2,1)} async-done(((bf16[2,512,2048]{2,1,0:T(8,128)(2,1)}), bf16[2,2048,2048]{2,1,0:T(8,128)(2,1)}) %all-gather.17.cloned.1.call-update) | async-done | bytes 16777232 | tf_op jit(solution)/shard_map/all_gather | solution.py:89
  957.8 11.5 fusion.24
  972.2 134.8 %all-gather.19.cloned.1.call-done = bf16[2,1024,2048]{2,1,0:T(8,128)(2,1)} async-done(((bf16[2,1024,512]{2,1,0:T(8,128)(2,1)}), bf16[2,1024,2048]{2,1,0:T(8,128)(2,1)}) %all-gather.19.cloned.1.call-update) | async-done | bytes 8388624 | tf_op jit(solution)/shard_map/all_gather | solution.py:90
  1121.6 13.4 all_gather.34
  1136.5 14.6 all-to-all-done.1
  1189.7 24.6 all-to-all-done.4
  1218.5 11.4 multiply_convert_fusion.3
  1230.0 18.1 convolution_convert_fusion.1
  1271.2 14.8 all-to-all-done.5
  1307.9 34.9 %all_to_all.133 = bf16[16,36,2048]{2,1,0:T(8,128)(2,1)S(1)} all-to-all(bf16[16,36,2048]{2,1,0:T(8,128)(2,1)S(1)} %broadcast_select_fusion.1), channel_id=1, replica_groups=mesh['expert'=8,'wshard'=4] {'expert'}, dimensions={0} | all-to-all | bytes 4718592 | tf_op jit(solution)/shard_map/all_to_all | solution.py:171
  1370.0 28.5 all-to-all-done.3
  1417.7 35.5 %all_to_all.134 = bf16[16,36,2048]{2,1,0:T(8,128)(2,1)S(1)} all-to-all(bf16[16,36,2048]{2,1,0:T(8,128)(2,1)S(1)} %broadcast_select_fusion), channel_id=1, replica_groups=mesh['expert'=8,'wshard'=4] {'expert'}, dimensions={0} | all-to-all | bytes 4718592 | tf_op jit(solution)/shard_map/all_to_all | solution.py:200
  1487.2 22.6 all-to-all-done.7
  1568.2 11.8 add_convert_fusion.1
  1581.7 17.9 fusion.22
  1599.6 20.0 add_convert_fusion
  1644.5 20.8 fusion.99
  1665.3 32.0 %convolution_add_fusion = f32[2048,6144]{1,0:T(8,128)} fusion(f32[2048,6144]{1,0:T(8,128)} %fusion.99, bf16[64,2048]{1,0:T(8,128)(2,1)} %reduce-scatter.18.cloned.1.call-done, bf16[64,2048]{1,0:T(8,128)(2,1)S(1)} %copy-done.40, bf16[64,2048]{1,0:T(8,128)(2,1)S(1)} %copy-done.39, f32[64]{0:T(128)S(1)} %copy-done.83, f32[2048]{0:T(1024)S(1)} %copy-done.57, ...), kind=kOutput, calls=%fused_computation.13 | convolution fusion | flops 1626079232 | bytes 101720576 | tf_op jit(solution)/shard_map/dot_general | solution.py:288
  1697.4 82.9 %reduce-scatter.28.cloned.1.call-done = f32[64,16]{1,0:T(8,128)} async-done(((f32[2048,16]{1,0:T(8,128)}), f32[64,16]{1,0:T(8,128)}) %reduce-scatter.28.cloned.1.call-update) | async-done | bytes 4112
  1782.7 13.3 fusion.98
  1796.0 12.7 fusion.67
  1808.7 42.3 %all-reduce.4 = (f32[2048]{0:T(1024)S(1)}, f32[2048]{0:T(1024)S(1)}, f32[2048]{0:T(1024)S(1)}, f32[2048]{0:T(1024)S(1)}) all-reduce(f32[2048]{0:T(1024)S(1)} %add.319, f32[2048]{0:T(1024)S(1)} %add.320, f32[2048]{0:T(1024)S(1)} %add.321, f32[2048]{0:T(1024)S(1)} %add.322), channel_id=6, replica_groups=mesh['expert'=8,'wshard'=4] {'expert','wshard'}, use_global_device_ids=true, to_apply=%region_50.51.clone | all-reduce | flops 8192 | bytes 65536
  1854.6 71.2 %reduce-scatter.26.cloned.1.call-done = bf16[2,1024,512]{2,1,0:T(8,128)(2,1)} async-done(((bf16[2,1024,2048]{2,1,0:T(8,128)(2,1)}), bf16[2,1024,512]{2,1,0:T(8,128)(2,1)}) %reduce-scatter.26.cloned.1.call-update) | async-done | bytes 2097168 | tf_op jit(solution)/shard_map/reduce_scatter | solution.py:319
  1929.9 279.2 %reduce-scatter.24.cloned.1.call-done = bf16[2,512,2048]{2,1,0:T(8,128)(2,1)} async-done(((bf16[2,2048,2048]{2,1,0:T(8,128)(2,1)}), bf16[2,512,2048]{2,1,0:T(8,128)(2,1)}) %reduce-scatter.24.cloned.1.call-update) | async-done | bytes 4194320 | tf_op jit(solution)/shard_map/reduce_scatter | solution.py:316
  2215.7 361.0 %reduce-scatter.22.cloned.1.call-done = f32[64,2048]{1,0:T(8,128)} async-done(((f32[2048,2048]{1,0:T(8,128)}), f32[64,2048]{1,0:T(8,128)}) %reduce-scatter.22.cloned.1.call-update) | async-done | bytes 524304 | tf_op jit(solution)/shard_map/reduce_scatter | solution.py:308
  2576.8 436.4 %reduce-scatter.20.cloned.1.call-done = f32[64,6144]{1,0:T(8,128)} async-done(((f32[2048,6144]{1,0:T(8,128)}), f32[64,6144]{1,0:T(8,128)}) %reduce-scatter.20.cloned.1.call-update) | async-done | bytes 1572880 | tf_op jit(solution)/shard_map/reduce_scatter | solution.py:307
  (506 shorter events, 338.8 us)
Async XLA Ops:
  7.2 430.3 %copy-start.56 = (f32[2048]{0:T(1024)S(1)}, f32[2048]{0:T(1024)}, u32[]{:S(2)}) copy-start(f32[2048]{0:T(1024)} %param.16) | copy-start | bytes 24580
  7.2 430.3 %all-gather.9.cloned.1.call-start = ((), (), s32[]{:S(2)}) async-start(), calls=%async_computation.17 | async-start | bytes 31457280 | tf_op jit(solution)/shard_map/all_gather | solution.py:109
  7.9 483.0 %all-gather.13.cloned.1.call-start = ((), (), s32[]{:S(2)}) async-start(), calls=%async_computation.19 | async-start | bytes 1310720 | tf_op jit(solution)/shard_map/all_gather | solution.py:134
  8.4 439.6 %copy-start.82 = (f32[64]{0:T(128)}, f32[64]{0:T(128)S(1)}, u32[]{:S(2)}) copy-start(f32[64]{0:T(128)S(1)} %get-tuple-element.197) | copy-start | bytes 772
  8.4 439.9 %copy-start.88 = (f32[64]{0:T(128)}, f32[64]{0:T(128)S(1)}, u32[]{:S(2)}) copy-start(f32[64]{0:T(128)S(1)} %get-tuple-element.198) | copy-start | bytes 772
  8.7 452.8 %copy-start.71 = (f32[64,64]{1,0:T(8,128)}, f32[64,64]{1,0:T(8,128)S(1)}, u32[]{:S(2)}) copy-start(f32[64,64]{1,0:T(8,128)S(1)} %get-tuple-element.174) | copy-start | bytes 49156
  8.7 452.8 %copy-start.73 = (f32[64,64]{1,0:T(8,128)}, f32[64,64]{1,0:T(8,128)S(1)}, u32[]{:S(2)}) copy-start(f32[64,64]{1,0:T(8,128)S(1)} %get-tuple-element.175) | copy-start | bytes 49156
  464.7 55.9 %all-gather.11.cloned.1.call-start = ((), (), s32[]{:S(2)}) async-start(), calls=%async_computation.18 | async-start | bytes 1310720 | tf_op jit(solution)/shard_map/all_gather | solution.py:135
  465.5 205.7 %all-gather.15.cloned.1.call-start = ((), (), s32[]{:S(2)}) async-start(), calls=%async_computation.20 | async-start | bytes 10485760 | tf_op jit(solution)/shard_map/all_gather | solution.py:110
  466.2 491.6 %all-gather.17.cloned.1.call-start = ((), (), s32[]{:S(2)}) async-start(), calls=%async_computation.21 | async-start | bytes 20971520 | tf_op jit(solution)/shard_map/all_gather | solution.py:89
  466.7 640.3 %all-gather.19.cloned.1.call-start = ((), (), s32[]{:S(2)}) async-start(), calls=%async_computation.22 | async-start | bytes 10485760 | tf_op jit(solution)/shard_map/all_gather | solution.py:90
  522.4 153.9 %copy-start.48 = (bf16[16,8,8,128]{3,2,1,0:T(8,128)(2,1)}, bf16[16,8,8,128]{3,2,1,0:T(8,128)(2,1)S(1)}, u32[]{:S(2)}) copy-start(bf16[16,8,8,128]{3,2,1,0:T(8,128)(2,1)S(1)} %fusion.30) | copy-start | bytes 786436
  522.4 153.9 %copy-start.75 = (f32[2048]{0:T(1024)S(1)}, f32[2048]{0:T(1024)}, u32[]{:S(2)}) copy-start(f32[2048]{0:T(1024)} %param.19) | copy-start | bytes 24580
  676.5 459.7 %copy-start = (bf16[64,2048]{1,0:T(8,128)(2,1)}, bf16[64,2048]{1,0:T(8,128)(2,1)S(1)}, u32[]{:S(2)}) copy-start(bf16[64,2048]{1,0:T(8,128)(2,1)S(1)} %multiply_convert_fusion.11) | copy-start | bytes 786436
  972.2 141.0 %copy-start.8 = (bf16[2,288,1024]{2,1,0:T(8,128)(2,1)}, bf16[2,288,1024]{2,1,0:T(8,128)(2,1)S(1)}, u32[]{:S(2)}) copy-start(bf16[2,288,1024]{2,1,0:T(8,128)(2,1)S(1)} %multiply_convert_fusion.5) | copy-start | bytes 3538948
  1117.1 34.0 %all-to-all-start.1 = ((bf16[2,288,2048]{2,0,1:T(2,128)(2,1)}), bf16[2,288,2048]{2,0,1:T(2,128)(2,1)}, u32[]{:S(2)}, u32[]{:S(2)}) async-start(bf16[2,288,2048]{2,0,1:T(2,128)(2,1)} %copy.224), calls=%async_computation.1 | async-start | bytes 4718592 | tf_op jit(solution)/shard_map/all_to_all | solution.py:186
  1177.5 36.8 %all-to-all-start.4 = ((bf16[16,36,2048]{2,1,0:T(8,128)(2,1)}), bf16[16,36,2048]{2,1,0:T(8,128)(2,1)}, u32[]{:S(2)}, u32[]{:S(2)}) async-start(bf16[16,36,2048]{2,1,0:T(8,128)(2,1)} %broadcast_select_fusion.2), calls=%async_computation.4 | async-start | bytes 5242880 | tf_op jit(solution)/shard_map/all_to_all | solution.py:200
  1182.0 77.7 %all-gather.23.cloned.1.call-start = ((), (), s32[]{:S(2)}) async-start(), calls=%async_computation.24 | async-start | bytes 1310720 | tf_op jit(solution)/shard_map/all_gather | solution.py:134
  1183.0 80.4 %all-gather.21.cloned.1.call-start = ((), (), s32[]{:S(2)}) async-start(), calls=%async_computation.23 | async-start | bytes 1310720 | tf_op jit(solution)/shard_map/all_gather | solution.py:135
  1251.9 34.1 %all-to-all-start.5 = ((bf16[2,288,2048]{2,0,1:T(2,128)(2,1)}), bf16[2,288,2048]{2,0,1:T(2,128)(2,1)}, u32[]{:S(2)}, u32[]{:S(2)}) async-start(bf16[2,288,2048]{2,0,1:T(2,128)(2,1)} %copy.248), calls=%async_computation.5 | async-start | bytes 4718592 | tf_op jit(solution)/shard_map/all_to_all | solution.py:220
  1365.3 33.1 %all-to-all-start.3 = ((bf16[2,288,2048]{2,0,1:T(2,128)(2,1)}), bf16[2,288,2048]{2,0,1:T(2,128)(2,1)S(1)}, u32[]{:S(2)}, u32[]{:S(2)}) async-start(bf16[2,288,2048]{2,0,1:T(2,128)(2,1)} %copy.242), calls=%async_computation.3 | async-start | bytes 4718592 | tf_op jit(solution)/shard_map/all_to_all | solution.py:186
  1476.7 33.1 %all-to-all-start.7 = ((bf16[2,288,2048]{2,0,1:T(2,128)(2,1)}), bf16[2,288,2048]{2,0,1:T(2,128)(2,1)S(1)}, u32[]{:S(2)}, u32[]{:S(2)}) async-start(bf16[2,288,2048]{2,0,1:T(2,128)(2,1)} %copy.264), calls=%async_computation.9 | async-start | bytes 4718592 | tf_op jit(solution)/shard_map/all_to_all | solution.py:220
  1480.5 155.7 %reduce-scatter.12.cloned.1.call-start = ((), (), s32[]{:S(2)}) async-start(), calls=%async_computation.25 | async-start | bytes 1310720 | tf_op jit(solution)/shard_map/reduce_scatter | solution.py:266
  1535.5 101.8 %reduce-scatter.16.cloned.1.call-start = ((), (), s32[]{:S(2)}) async-start(), calls=%async_computation.27 | async-start | bytes 1310720 | tf_op jit(solution)/shard_map/reduce_scatter | solution.py:266
  1548.0 96.5 %reduce-scatter.14.cloned.1.call-start = ((), (), s32[]{:S(2)}) async-start(), calls=%async_computation.26 | async-start | bytes 1310720 | tf_op jit(solution)/shard_map/reduce_scatter | solution.py:272
  1551.9 113.4 %reduce-scatter.18.cloned.1.call-start = ((), (), s32[]{:S(2)}) async-start(), calls=%async_computation.28 | async-start | bytes 1310720 | tf_op jit(solution)/shard_map/reduce_scatter | solution.py:272
  1555.9 224.5 %reduce-scatter.28.cloned.1.call-start = ((), (), s32[]{:S(2)}) async-start(), calls=%async_computation.33 | async-start | bytes 1081344
  1568.1 357.6 %reduce-scatter.26.cloned.1.call-start = ((), (), s32[]{:S(2)}) async-start(), calls=%async_computation.32 | async-start | bytes 10485760 | tf_op jit(solution)/shard_map/reduce_scatter | solution.py:319
  1580.0 629.1 %reduce-scatter.24.cloned.1.call-start = ((), (), s32[]{:S(2)}) async-start(), calls=%async_computation.31 | async-start | bytes 20971520 | tf_op jit(solution)/shard_map/reduce_scatter | solution.py:316
  1619.6 957.1 %reduce-scatter.22.cloned.1.call-start = ((), (), s32[]{:S(2)}) async-start(), calls=%async_computation.30 | async-start | bytes 17301504 | tf_op jit(solution)/shard_map/reduce_scatter | solution.py:308
  1631.3 1381.9 %reduce-scatter.20.cloned.1.call-start = ((), (), s32[]{:S(2)}) async-start(), calls=%async_computation.29 | async-start | bytes 51904512 | tf_op jit(solution)/shard_map/reduce_scatter | solution.py:307
  1697.4 84.4 %copy-start.68 = (bf16[1,64,2048]{2,1,0:T(8,128)(2,1)S(1)}, bf16[1,64,2048]{2,1,0:T(8,128)(2,1)}, u32[]{:S(2)}) copy-start(bf16[1,64,2048]{2,1,0:T(8,128)(2,1)} %get-tuple-element.126) | copy-start | bytes 786436
  (115 other events, 1339.6 us)
Sparse Core Ops, SparseCore 0:
  9.6 427.8 all-gather.8
  464.9 26.0 all-gather.12
  493.1 27.5 all-gather.10
  522.1 149.1 all-gather.14
  672.7 285.0 all-gather.16
  959.2 147.7 all-gather.18
  1185.0 26.5 all-gather.22
  1213.8 27.4 all-gather.20
  1535.6 23.5 reduce-scatter.11
  1561.5 25.7 reduce-scatter.15
  1589.6 25.7 reduce-scatter.13
  1617.7 25.7 reduce-scatter.17
  1646.3 133.9 reduce-scatter.27
  1783.2 142.4 reduce-scatter.25
  1928.0 280.9 reduce-scatter.23
  2211.8 364.9 reduce-scatter.21
  2583.6 429.5 reduce-scatter.19
where the time goes:
time: 3030 us; the launch traced here: 3020 us
  waiting for transfers between devices  2330 us (77%)
  matrix products  304 us (10%)
  blocking collectives  162 us (5%)
  local copies, waits for them, and re-layouts  141 us (5%)
  other arithmetic  48.7 us (2%)
    reduce_scatter x1, waiting for transfers between devices, local(): lax.psum_scatter(total_qkv, ('expert', 'wshard'), scatter_dimension=0, ti...  436 us
    all_gather x1, waiting for transfers between devices, local(): lax.all_gather(w_qkv, 'wshard', axis=0, tiled=True)  429 us
    reduce_scatter x1, waiting for transfers between devices, local(): lax.psum_scatter(total_out, ('expert', 'wshard'), scatter_dimension=0, ti...  361 us
    reduce_scatter x1, waiting for transfers between devices, local(): lax.psum_scatter(total_up.astype(jnp.bfloat16), 'wshard', scatter_dimensi...  279 us
    all_gather x1, waiting for transfers between devices, local(): lax.all_gather(w_gate_up, 'wshard', axis=1, tiled=True)  231 us
    all_gather x1, waiting for transfers between devices, local(): lax.all_gather(w_out, 'wshard', axis=0, tiled=True)  149 us
    all_gather x1, waiting for transfers between devices, local(): lax.all_gather(w_down, 'wshard', axis=2, tiled=True)  135 us
    unnamed x18, waiting for transfers between devices  85.4 us
  transfers between devices with their start and end apart: 22, of which 16 were waited for; matrix products, arithmetic and copies ran while one was open for 10% of the time, Pallas kernels for 0%

commit v1 on v0

v1 whole, which is shorter than its diff:
```python
import jax
import jax.numpy as jnp
from jax import lax
from jax.sharding import PartitionSpec as P

HEADS = 16
EPS = 1e-05
THETA = 10000.0
AXES = ("expert", "wshard")
LOW = jnp.bfloat16
F32 = jnp.float32


def rms_scale(values):
    return lax.rsqrt(jnp.mean(values * values, axis=-1, keepdims=True) + EPS)


def rotate(values, cosine, sine):
    half = values.shape[-1] // 2
    first = values[..., :half]
    second = values[..., half:]
    return jnp.concatenate(
        [first * cosine - second * sine, second * cosine + first * sine], axis=-1
    )


def norm_back(values, scale, gain, grads, inner):
    weighted = gain * grads
    return scale * weighted - values * scale * scale * scale * inner


def dot(a, b, dims):
    return lax.dot_general(a, b, (dims, ((), ())), preferred_element_type=F32)


def mm(a, b):
    return dot(a, b, ((1,), (0,)))


def mm_t(a, b):
    return dot(a, b, ((1,), (1,)))


def t_mm(a, b):
    return dot(a, b, ((0,), (0,)))


def build(n_e, n_w):
    bits = [1 << b for b in range(n_e.bit_length() - 1)]
    plane = bits[1:]
    nd = len(plane)

    def swap(x, d):
        return lax.ppermute(x, "expert", [(i, i ^ d) for i in range(n_e)])

    def shift(x, s):
        return lax.ppermute(x, "wshard", [(j, (j + s) % n_w) for j in range(n_w)])

    def joint(x, pairs):
        return lax.ppermute(x, AXES, pairs)

    def line_gather(x):
        return [x] + [shift(x, n_w - r) for r in range(1, n_w)]

    def line_scatter(blocks):
        total = blocks[0].astype(F32)
        for r in range(1, n_w):
            total = total + shift(blocks[r], r).astype(F32)
        return total

    def line_sum(x, shard):
        x = jnp.roll(x.reshape(2, n_w, -1), shard, axis=1)
        return jnp.roll(lax.psum(x, "wshard"), -shard, axis=1)

    def part_of(r):
        return r * nd // n_w

    def order(r):
        p = part_of(r)
        return [plane[(s + p) % nd] for s in range(nd)]

    def plane_gather(blocks):
        groups = [{(r, 0): b for r, b in enumerate(blocks)}]
        held = dict(groups[0])
        for step in range(nd):
            got = {}
            for (r, m), b in held.items():
                d = order(r)[step]
                got[(r, m | d)] = swap(b, d)
            held.update(got)
            groups.append(got)
        return groups

    def plane_scatter(parts):
        parts = dict(parts)
        for step in reversed(range(nd)):
            for r in range(n_w):
                d = order(r)[step]
                for r2, m in sorted(k for k in parts if k[0] == r and k[1] & d):
                    got = swap(parts.pop((r, m)), d).astype(F32)
                    keep = parts[(r, m ^ d)].astype(F32)
                    parts[(r, m ^ d)] = (keep + got).astype(LOW)
        return [parts[(r, 0)] for r in range(n_w)]

    def hyper_scatter(x, me, dims, kind):
        x = x.reshape((2,) * len(bits) + x.shape[1:])
        left = list(reversed(bits))
        for d in dims:
            at = left.index(d)
            bit = (me // d) % 2
            send = lax.dynamic_index_in_dim(x, 1 - bit, at, keepdims=False).astype(kind)
            keep = lax.dynamic_index_in_dim(x, bit, at, keepdims=False)
            x = (keep.astype(F32) + swap(send, d).astype(F32)).astype(kind)
            left.pop(at)
        return x

    def local(
        hidden_in,
        doc_ids,
        routes,
        attn_gain,
        q_gain,
        k_gain,
        ffn_gain,
        w_qkv,
        w_out,
        w_router,
        w_gate_up,
        w_down,
        cotangent,
    ):
        micro = hidden_in.shape[0]
        rows = hidden_in.shape[2]
        width = hidden_in.shape[3]
        heads = HEADS
        head = width // heads
        my_heads = heads // n_w
        cols = width // n_w
        experts = w_router.shape[1]
        local_experts = w_gate_up.shape[0]
        units = w_down.shape[1]
        own = micro * rows
        seq = n_w * rows
        me = lax.axis_index("expert")
        shard = lax.axis_index("wshard")
        core = me % 2
        my_expert = (me // 2) * n_w + shard
        scale = head ** (-0.5)

        piece = width // n_w // n_e
        mine = lax.dynamic_slice_in_dim(w_qkv, me * piece, piece, 0)
        mine = mine.reshape(piece, 3, n_w, cols)

        def columns_for(target):
            return lax.dynamic_index_in_dim(mine, target % n_w, 2, keepdims=False)

        bank = jnp.zeros((n_w, piece, 3, cols), LOW)
        for s in range(n_w):
            got = columns_for(shard + s)
            if s:
                got = shift(got, s)
            bank = lax.dynamic_update_index_in_dim(bank, got, (shard - s + n_w) % n_w, 0)
        bank = bank.reshape(n_w, piece, 3 * cols)
        w_heads = jnp.zeros((n_w, n_e, piece, 3 * cols), LOW)
        half = piece // 2
        for p in range(2):
            dims = plane[p:] + plane[:p] + [1]
            held = {0: bank[:, p * half : (p + 1) * half]}
            for d in dims:
                held.update({m | d: swap(b, d) for m, b in list(held.items())})
            for m, b in held.items():
                w_heads = lax.dynamic_update_slice(
                    w_heads, b[:, None], (0, jnp.bitwise_xor(me, m), p * half, 0)
                )
        w_heads = w_heads.reshape(width, 3 * cols)

        tokens = hidden_in.reshape(own, width).astype(F32)
        scale_one = rms_scale(tokens)
        normed = (tokens * scale_one * attn_gain).astype(LOW)
        normed_all = jnp.concatenate(line_gather(normed), 0)

        router = lax.all_gather(w_router, "wshard", axis=0, tiled=True)
        all_routes = lax.all_gather(routes.reshape(own, -1), AXES, axis=0, tiled=False)

        half_rows = w_gate_up.shape[1] // 2
        half_units = units // 2

        def expert_pairs(s, h):
            out = []
            for c in range(n_e // 2):
                for w in range(n_w):
                    t = (w + s) % n_w
                    src = ((2 * c + t // local_experts) * n_w + w, (2 * c + h) * n_w + t)
                    if src[0] != src[1]:
                        out.append(src)
            return out

        holder = shard // local_experts
        up_own, down_own = [], []
        for s in range(n_w):
            target = (shard + s) % n_w
            j = jnp.clip(target - local_experts * core, 0, local_experts - 1)
            up_got = jnp.zeros((half_rows, 2 * units), LOW)
            down_got = jnp.zeros((half_units, cols), LOW)
            up_src = lax.dynamic_index_in_dim(w_gate_up, j, 0, keepdims=False)
            down_src = lax.dynamic_index_in_dim(w_down, j, 0, keepdims=False)
            for h in range(2):
                up_h = up_src[h * half_rows : (h + 1) * half_rows]
                down_h = down_src[h * half_units : (h + 1) * half_units]
                up_in = joint(up_h, expert_pairs(s, h))
                down_in = joint(down_h, expert_pairs(s, h))
                if s == 0:
                    up_in = jnp.where(holder == h, up_h, up_in)
                    down_in = jnp.where(holder == h, down_h, down_in)
                up_got = jnp.where(core == h, up_in, up_got)
                down_got = jnp.where(core == h, down_in, down_got)
            up_own.append(up_got)
            down_own.append(down_got)
        w_up = jnp.zeros((n_w, 2, half_rows, 2 * units), LOW)
        w_dn = jnp.zeros((2, half_units, n_w, cols), LOW)
        for s in range(n_w):
            w = (shard - s + n_w) % n_w
            for which, up_b, down_b in (
                (core, up_own[s], down_own[s]),
                (1 - core, swap(up_own[s], 1), swap(down_own[s], 1)),
            ):
                w_up = lax.dynamic_update_slice(w_up, up_b[None, None], (w, which, 0, 0))
                w_dn = lax.dynamic_update_slice(w_dn, down_b[None, :, None], (which, 0, w, 0))
        w_up = w_up.reshape(width, 2 * units)
        w_dn = w_dn.reshape(units, width)

        projected = mm(normed_all, w_heads)
        raw = projected.reshape(n_w, micro, rows, 3, my_heads, head)
        squares = jnp.sum(projected.reshape(-1, 3, cols)[:, :2] ** 2, axis=-1).T
        scales = lax.rsqrt(line_sum(squares, shard) / width + EPS)
        scales = scales.reshape(2, n_w, micro, rows, 1, 1)
        gain_q = lax.dynamic_slice_in_dim(q_gain, shard * cols, cols).reshape(my_heads, head)
        gain_k = lax.dynamic_slice_in_dim(k_gain, shard * cols, cols).reshape(my_heads, head)
        block_at = (shard + jnp.arange(n_w, dtype=jnp.int32)) % n_w
        positions = (
            block_at[:, None] * rows + jnp.arange(rows, dtype=jnp.int32)[None, :]
        )
        freq = THETA ** (-(jnp.arange(head // 2, dtype=F32) * 2.0 / head))
        angle = positions.astype(F32)[:, None, :, None, None] * freq
        cosine, sine = jnp.cos(angle), jnp.sin(angle)
        q_raw, k_raw, v_raw = raw[..., 0, :, :], raw[..., 1, :, :], raw[..., 2, :, :]
        queries = rotate(q_raw * scales[0] * gain_q, cosine, sine).astype(LOW)
        keys = rotate(k_raw * scales[1] * gain_k, cosine, sine).astype(LOW)
        values = v_raw.astype(LOW)

        def by_head(x):
            return x.transpose(1, 3, 0, 2, 4).reshape(micro * my_heads, seq, head)

        def by_token(x):
            x = x.reshape(micro, my_heads, n_w, rows, head)
            return x.transpose(2, 0, 3, 1, 4)

        q_h, k_h, v_h = by_head(queries), by_head(keys), by_head(values)
        flat_pos = positions.reshape(seq)
        docs = jnp.take(doc_ids[:, 0], flat_pos, axis=1)
        allowed = (flat_pos[None, :] <= flat_pos[:, None])[None] & (
            docs[:, :, None] == docs[:, None, :]
        )
        allowed = jnp.repeat(allowed, my_heads, axis=0)
        scores = jnp.einsum("bqd,bkd->bqk", q_h, k_h, preferred_element_type=F32) * scale
        scores = jnp.where(allowed, scores, -1e30)
        peak = jnp.max(scores, axis=-1, keepdims=True)
        expo = jnp.exp(scores - peak)
        probs = expo / jnp.sum(expo, axis=-1, keepdims=True)
        probs_low = probs.astype(LOW)
        attended = jnp.einsum("bqk,bkd->bqd", probs_low, v_h, preferred_element_type=F32)
        attended = by_token(attended.astype(LOW)).reshape(n_w * own, cols)
        branch = mm(attended, w_out).astype(LOW).reshape(n_w, own, width)
        resid = tokens + line_scatter([branch[r] for r in range(n_w)])

        scale_two = rms_scale(resid)
        ffn_in = (resid * scale_two * ffn_gain).astype(LOW)
        upstream = cotangent.reshape(own, width)
        x_groups = plane_gather(line_gather(ffn_in))
        dy_groups = plane_gather(line_gather(upstream))
        used = jnp.any(all_routes == my_expert, axis=-1)

        mix_parts, back_parts = {}, {}
        grad_up = jnp.zeros((width, 2 * units), F32)
        grad_dn = jnp.zeros((units, width), F32)
        grad_router = jnp.zeros((width, experts), F32)
        hot = jnp.arange(experts, dtype=jnp.int32)[None, :] == my_expert
        for x_group, dy_group in zip(x_groups, dy_groups):
            names = list(x_group)
            x = jnp.concatenate([x_group[n] for n in names], 0)
            dy = jnp.concatenate([dy_group[n] for n in names], 0)
            owner = jnp.stack(
                [jnp.bitwise_xor(me, m) * n_w + (shard + r) % n_w for r, m in names]
            )
            mask = jnp.take(used, owner, axis=0).reshape(-1, 1)
            gate_all = jax.nn.softmax(mm(x, router), axis=-1)
            gate = jnp.sum(jnp.where(hot, gate_all, 0.0), axis=-1, keepdims=True)
            gate = jnp.where(mask, gate, 0.0)
            gate_up = mm(x, w_up)
            g, u = gate_up[:, :units], gate_up[:, units:]
            sigma = jax.nn.sigmoid(g)
            silu = g * sigma
            act = (silu * u).astype(LOW).astype(F32)
            lifted = mm_t(dy, w_dn)
            dgate = jnp.sum(act * lifted, axis=-1, keepdims=True)
            act_gated = (act * gate).astype(LOW)
            dact = lifted * gate
            dgu = jnp.concatenate(
                [dact * u * (sigma * (1.0 + g * (1.0 - sigma))), dact * silu], axis=-1
            ).astype(LOW)
            dlogits = (dgate * gate * (jnp.where(hot, 1.0, 0.0) - gate_all)).astype(LOW)
            mix = mm(act_gated, w_dn).astype(LOW)
            back = (mm_t(dgu, w_up) + mm_t(dlogits, router)).astype(LOW)
            for at, name in enumerate(names):
                mix_parts[name] = mix[at * own : (at + 1) * own]
                back_parts[name] = back[at * own : (at + 1) * own]
            grad_up = grad_up + t_mm(x, dgu)
            grad_dn = grad_dn + t_mm(act_gated, dy)
            grad_router = grad_router + t_mm(x, dlogits)
        dffn = line_scatter(plane_scatter(back_parts))
        mixture = line_scatter(plane_scatter(mix_parts))
        hidden_out = (resid + mixture).astype(LOW)

        def pair_sum(x, axis):
            send = lax.dynamic_index_in_dim(x, 1 - core, axis, keepdims=False).astype(LOW)
            keep = lax.dynamic_index_in_dim(x, core, axis, keepdims=False)
            return (keep + swap(send, 1).astype(F32)).astype(LOW)

        up_sum = pair_sum(grad_up.reshape(n_w, 2, half_rows, 2 * units), 1)
        dn_sum = pair_sum(grad_dn.reshape(2, half_units, n_w, cols), 0)

        def grad_pairs(s, h):
            out = []
            for c in range(n_e // 2):
                for w in range(n_w):
                    pair = (
                        (2 * c + h) * n_w + w,
                        (2 * c + w // local_experts) * n_w + (w + s) % n_w,
                    )
                    if pair[0] != pair[1]:
                        out.append(pair)
            return out

        up_out = [[0.0, 0.0] for j in range(local_experts)]
        dn_out = [[0.0, 0.0] for j in range(local_experts)]
        for s in range(n_w):
            target = (shard + s) % n_w
            up_send = lax.dynamic_index_in_dim(up_sum, target, 0, keepdims=False)
            dn_send = lax.dynamic_index_in_dim(dn_sum, target, 1, keepdims=False)
            for h in range(2):
                up_in = joint(up_send, grad_pairs(s, h))
                dn_in = joint(dn_send, grad_pairs(s, h))
                if s == 0:
                    kept = (core == h) & (holder == core)
                    up_in = jnp.where(kept, up_send, up_in)
                    dn_in = jnp.where(kept, dn_send, dn_in)
                for j in range(local_experts):
                    right = (shard - local_experts * core - j - s) % n_w == 0
                    up_out[j][h] = jnp.where(right, up_in.astype(F32), up_out[j][h])
                    dn_out[j][h] = jnp.where(right, dn_in.astype(F32), dn_out[j][h])
        out_gate_up = jnp.stack([jnp.concatenate(u, 0) for u in up_out])
        out_down = jnp.stack([jnp.concatenate(d, 0) for d in dn_out])

        upstream = upstream.astype(F32)
        weighted = ffn_gain * dffn
        inner = jnp.mean(resid * weighted, axis=-1, keepdims=True)
        dresid = upstream + norm_back(resid, scale_two, ffn_gain, dffn, inner)
        grad_ffn_gain = jnp.sum(dffn * resid * scale_two, axis=0)
        dbranch = jnp.concatenate(line_gather(dresid.astype(LOW)), 0)
        grad_out = t_mm(attended, dbranch)
        dattended = mm_t(dbranch, w_out).astype(LOW)
        datt_h = by_head(dattended.reshape(n_w, micro, rows, my_heads, head))
        dprobs = jnp.einsum("bqd,bkd->bqk", datt_h, v_h, preferred_element_type=F32)
        probs = jnp.where(allowed, probs, 0.0)
        dscores = probs * (dprobs - jnp.sum(probs * dprobs, axis=-1, keepdims=True))
        dscores = dscores.astype(LOW)
        dq = jnp.einsum("bqk,bkd->bqd", dscores, k_h, preferred_element_type=F32) * scale
        dk = jnp.einsum("bqk,bqd->bkd", dscores, q_h, preferred_element_type=F32) * scale
        dv = jnp.einsum("bqk,bqd->bkd", probs_low, datt_h, preferred_element_type=F32)
        dq = rotate(by_token(dq), cosine, -sine)
        dk = rotate(by_token(dk), cosine, -sine)
        dv = by_token(dv)
        inners = jnp.stack(
            [
                jnp.sum(q_raw * gain_q * dq, axis=(-2, -1)),
                jnp.sum(k_raw * gain_k * dk, axis=(-2, -1)),
            ]
        )
        inners = line_sum(inners, shard) / width
        inners = inners.reshape(2, n_w, micro, rows, 1, 1)
        dq_raw = norm_back(q_raw, scales[0], gain_q, dq, inners[0])
        dk_raw = norm_back(k_raw, scales[1], gain_k, dk, inners[1])
        grad_q = jnp.sum(dq * q_raw * scales[0], axis=(0, 1, 2)).reshape(cols)
        grad_k = jnp.sum(dk * k_raw * scales[1], axis=(0, 1, 2)).reshape(cols)
        dproj = jnp.stack([dq_raw, dk_raw, dv], axis=3).astype(LOW)
        dproj = dproj.reshape(n_w * own, 3 * cols)
        dnormed = mm_t(dproj, w_heads).astype(LOW).reshape(n_w, own, width)
        dnormed = line_scatter([dnormed[r] for r in range(n_w)])
        inner = jnp.mean(tokens * (attn_gain * dnormed), axis=-1, keepdims=True)
        dx = norm_back(tokens, scale_one, attn_gain, dnormed, inner)
        grad_in = (dresid + dx).astype(LOW)
        grad_attn_gain = jnp.sum(dnormed * tokens * scale_one, axis=0)
        grad_qkv = t_mm(normed_all, dproj)

        small = width // (n_e * n_w)
        core_first = [1] + plane
        qkv = hyper_scatter(grad_qkv.reshape(n_e, n_w * small, 3 * cols), me, core_first, LOW)
        qkv = qkv.reshape(n_w, small, 3, cols)
        out_qkv = jnp.zeros((small, 3, n_w, cols), F32)
        for s in range(n_w):
            got = lax.dynamic_index_in_dim(qkv, (shard + s) % n_w, 0, keepdims=False)
            if s:
                got = shift(got, s)
            out_qkv = lax.dynamic_update_index_in_dim(
                out_qkv, got.astype(F32), (shard - s + n_w) % n_w, 2
            )
        out_qkv = out_qkv.reshape(small, 3 * width)
        to_rows = [
            (i * n_w + w, w * n_e + i) for i in range(n_e) for w in range(n_w)
        ]
        out_rows = hyper_scatter(grad_out.reshape(n_e, small, width), me, core_first, LOW)
        out_rows = joint(out_rows, to_rows).astype(F32)
        gains = jnp.stack([grad_q, grad_k]).reshape(2, n_e, small).transpose(1, 0, 2)
        gains = joint(hyper_scatter(gains, me, core_first, F32), to_rows)
        pack = jnp.concatenate([grad_router.T, grad_attn_gain[None], grad_ffn_gain[None]], 0)
        pack = pack.reshape(experts + 2, n_e, n_w * small).transpose(1, 0, 2)
        pack = hyper_scatter(pack, me, core_first, F32)
        pack = pack.reshape(experts + 2, n_w, small)
        total = 0.0
        for s in range(n_w):
            got = lax.dynamic_index_in_dim(pack, (shard + s) % n_w, 1, keepdims=False)
            total = total + (shift(got, s) if s else got)
        return (
            hidden_out.reshape(micro, 1, rows, width),
            grad_in.reshape(micro, 1, rows, width),
            total[experts],
            gains[0],
            gains[1],
            total[experts + 1],
            out_qkv,
            out_rows,
            total[:experts].T,
            out_gate_up,
            out_down,
        )

    return local


def solution(mesh):
    in_specs = (
        P(None, "expert", "wshard", None),
        P(None, "expert", None),
        P(None, "expert", "wshard", None),
        P(),
        P(),
        P(),
        P(),
        P("wshard", None),
        P("wshard", None),
        P("wshard", None),
        P("expert", "wshard", None),
        P("expert", None, "wshard"),
        P(None, "expert", "wshard", None),
    )
    out_specs = (
        P(None, "expert", "wshard", None),
        P(None, "expert", "wshard", None),
        P(("expert", "wshard")),
        P(("expert", "wshard")),
        P(("expert", "wshard")),
        P(("expert", "wshard")),
        P(("expert", "wshard"), None),
        P(("expert", "wshard"), None),
        P(("expert", "wshard"), None),
        P("expert", "wshard", None),
        P("expert", None, "wshard"),
    )
    local = build(mesh.shape["expert"], mesh.shape["wshard"])
    return jax.shard_map(local, mesh=mesh, in_specs=in_specs, out_specs=out_specs, check_vma=False)
```

time: 3030 us -> 1620 us (0.53)
  waiting for transfers between devices: 2330 us -> 425 us
  starting transfers between devices: 22.9 us -> 357 us
  local copies, waits for them, and re-layouts: 141 us -> 376 us
  matrix products: 304 us -> 207 us
  other arithmetic: 48.7 us -> 104 us
  blocking collectives: 162 us -> 119 us
    reduce_scatter x8 -> x0, waiting for transfers between devices: 1150 us -> none  [the longest x1 436 us: local(): lax.psum_scatter(total_qkv, ('expert', 'wshard'), scatter_dimension=0, ti...]
    all_gather x8 -> x0, waiting for transfers between devices: 987 us -> none  [the longest x1 429 us: local(): lax.all_gather(w_qkv, 'wshard', axis=0, tiled=True)]
    ppermute x0 -> x151, waiting for transfers between devices: none -> 425 us  [the longest x33 203 us: shift(): return lax.ppermute(x, 'wshard', [(j, (j + s) % n_w) for j in range(n_w)])]
    ppermute x0 -> x151, starting transfers between devices: none -> 357 us  [the longest x84 128 us: swap(): return lax.ppermute(x, 'expert', [(i, i ^ d) for i in range(n_e)])]
    dynamic_update_slice x0 -> x36, local copies, waits for them, and re-layouts: none -> 207 us  [the longest x8 155 us: local(): lax.dynamic_update_slice(w_dn, down_b[None, :, None], (which, 0, w, 0))]
    all_to_all x3 -> x0, blocking collectives: 106 us -> none  [the longest x2 70.6 us: local(): lax.all_to_all(send.reshape(expert_count, capacity, width), 'expert', spl...]
    all_to_all x5 -> x0, waiting for transfers between devices: 105 us -> none  [the longest x2 43.1 us: local(): lax.all_to_all(expert_out, 'expert', split_axis=1, concat_axis=0, tiled=T...]
    dot_general x46 -> x39, matrix products: 304 us -> 207 us  [the longest x33 196 us: dot(): return lax.dot_general(a, b, (dims, ((), ())), preferred_element_type=F32)]
  transfers between devices with their start and end apart: 22 -> 151, of which waited for: 16 -> 41; matrix products, arithmetic and copies ran while one was open for 10% -> 35% of each run, Pallas kernels for 0% -> 0%
where the time goes in v1:
time: 1620 us; the launch traced here: 1590 us
  waiting for transfers between devices  425 us (26%)
  local copies, waits for them, and re-layouts  376 us (23%)
  starting transfers between devices  357 us (22%)
  matrix products  207 us (13%)
  blocking collectives  119 us (7%)
  other arithmetic  104 us (6%)
    ppermute x33, waiting for transfers between devices, shift(): return lax.ppermute(x, 'wshard', [(j, (j + s) % n_w) for j in range(n_w)])  203 us
    dot_general x33, matrix products, dot(): return lax.dot_general(a, b, (dims, ((), ())), preferred_element_type=F32)  196 us
    dynamic_update_slice x8, local copies, waits for them, and re-layouts, local(): lax.dynamic_update_slice(w_dn, down_b[None, :, None], (which, 0, w, 0))  155 us
    ppermute x84, waiting for transfers between devices, swap(): return lax.ppermute(x, 'expert', [(i, i ^ d) for i in range(n_e)])  143 us
    ppermute x84, starting transfers between devices, swap(): return lax.ppermute(x, 'expert', [(i, i ^ d) for i in range(n_e)])  128 us
    ppermute x33, starting transfers between devices, shift(): return lax.ppermute(x, 'wshard', [(j, (j + s) % n_w) for j in range(n_w)])  125 us
    ppermute x34, starting transfers between devices, joint(): return lax.ppermute(x, AXES, pairs)  104 us
    ppermute x34, waiting for transfers between devices, joint(): return lax.ppermute(x, AXES, pairs)  78.6 us
  transfers between devices with their start and end apart: 151, of which 41 were waited for; matrix products, arithmetic and copies ran while one was open for 35% of the time, Pallas kernels for 0%

profile of v1, /device:TPU:0, one launch (start us, length us, event | category | flops | bytes accessed | tf_op | source)
XLA Modules:
  0.0 1592.4 jit_solution(14936476159306368017)
XLA Ops:
  27.8 20.7 %all_gather.7 = bf16[2048,16]{0,1:T(8,128)(2,1)S(1)} all-gather(bf16[512,16]{0,1:T(8,128)(2,1)S(1)} %copy-done.109), channel_id=1, replica_groups=mesh['expert'=8,'wshard'=4] {'wshard'}, dimensions={0}, use_global_device_ids=true | all-gather | bytes 81920 | tf_op jit(solution)/shard_map/all_gather | solution.py:182
  48.5 66.1 %all_gather.6 = s32[32,128,8]{1,2,0:T(8,128)S(1)} all-gather(s32[1,128,8]{1,2,0:T(8,128)S(1)} %all_gather_reshape.3), channel_id=1, replica_groups=mesh['expert'=8,'wshard'=4] {'expert','wshard'}, dimensions={0}, use_global_device_ids=true | all-gather | bytes 135168 | tf_op jit(solution)/shard_map/all_gather | solution.py:183
  159.1 21.9 %collective-permute-done.45 = bf16[512,512]{1,0:T(8,128)(2,1)S(1)} collective-permute-done((bf16[512,512]{1,0:T(8,128)(2,1)S(1)}, bf16[512,512]{1,0:T(8,128)(2,1)S(1)}, u32[]{:S(2)}, u32[]{:S(2)}) %collective-permute-start.45) | collective-permute-done | bytes 524320 | tf_op jit(solution)/shard_map/ppermute | solution.py:60
  180.9 28.9 %collective-permute-start = (bf16[128,2048]{1,0:T(8,128)(2,1)}, bf16[128,2048]{1,0:T(8,128)(2,1)S(1)}, u32[]{:S(2)}, u32[]{:S(2)}) collective-permute-start(bf16[128,2048]{1,0:T(8,128)(2,1)} %fusion.48), channel_id=1, source_target_pairs={{0,3},{1,0},{2,1},{3,2},{4,7},{5,4},{6,5},{7,6},{8,11},{9,8},{10,9... | collective-permute-start | bytes 1572872 | tf_op jit(solution)/shard_map/ppermute | solution.py:57
  231.5 19.3 %dynamic_update_slice.150 = bf16[2,512,4,512]{3,2,1,0:T(4,128)(2,1)} dynamic-update-slice(bf16[2,512,4,512]{3,2,1,0:T(4,128)(2,1)} %broadcast_in_dim.319, bf16[1,512,1,512]{3,2,1,0:T(2,128)(2,1)} %copy.433, s32[]{:T(128)S(6)} %select_n.848, s32[]{:T(128)} %constant.563.clone.1, s32[]{:T(128)S(6)} %select_n.821, s32[]{:T(128)} %constant.563.clone.1) | dynamic-update-slice | bytes 1048580 | tf_op jit(solution)/shard_map/dynamic_update_slice | solution.py:228
  281.8 29.0 %collective-permute-done.78 = bf16[128,2048]{1,0:T(8,128)(2,1)} collective-permute-done((bf16[128,2048]{1,0:T(8,128)(2,1)}, bf16[128,2048]{1,0:T(8,128)(2,1)}, u32[]{:S(2)}, u32[]{:S(2)}) %collective-permute-start.78) | collective-permute-done | bytes 524320 | tf_op jit(solution)/shard_map/ppermute | solution.py:57
  350.8 19.6 %dynamic_update_slice.151 = bf16[2,512,4,512]{3,2,1,0:T(4,128)(2,1)} dynamic-update-slice(bf16[2,512,4,512]{3,2,1,0:T(4,128)(2,1)} %dynamic_update_slice.150, bf16[1,512,1,512]{3,2,1,0:T(2,128)(2,1)} %copy.434, s32[]{:T(128)S(6)} %select_n.849, s32[]{:T(128)} %constant.563.clone.1, s32[]{:T(128)S(6)} %select_n.821, s32[]{:T(128)} %constant.563.clone.1) | dynamic-update-slice | bytes 1048580 | tf_op jit(solution)/shard_map/dynamic_update_slice | solution.py:228
  370.5 19.3 %dynamic_update_slice.152 = bf16[2,512,4,512]{3,2,1,0:T(4,128)(2,1)} dynamic-update-slice(bf16[2,512,4,512]{3,2,1,0:T(4,128)(2,1)} %dynamic_update_slice.151, bf16[1,512,1,512]{3,2,1,0:T(2,128)(2,1)} %copy.435, s32[]{:T(128)S(6)} %select_n.848, s32[]{:T(128)} %constant.563.clone.1, s32[]{:T(128)S(6)} %select_n.825, s32[]{:T(128)} %constant.563.clone.1) | dynamic-update-slice | bytes 1048580 | tf_op jit(solution)/shard_map/dynamic_update_slice | solution.py:228
  389.7 19.3 %dynamic_update_slice.153 = bf16[2,512,4,512]{3,2,1,0:T(4,128)(2,1)} dynamic-update-slice(bf16[2,512,4,512]{3,2,1,0:T(4,128)(2,1)} %dynamic_update_slice.152, bf16[1,512,1,512]{3,2,1,0:T(2,128)(2,1)} %copy.436, s32[]{:T(128)S(6)} %select_n.849, s32[]{:T(128)} %constant.563.clone.1, s32[]{:T(128)S(6)} %select_n.825, s32[]{:T(128)} %constant.563.clone.1) | dynamic-update-slice | bytes 1048580 | tf_op jit(solution)/shard_map/dynamic_update_slice | solution.py:228
  409.0 19.3 %dynamic_update_slice.154 = bf16[2,512,4,512]{3,2,1,0:T(4,128)(2,1)} dynamic-update-slice(bf16[2,512,4,512]{3,2,1,0:T(4,128)(2,1)} %dynamic_update_slice.153, bf16[1,512,1,512]{3,2,1,0:T(2,128)(2,1)} %copy.437, s32[]{:T(128)S(6)} %select_n.848, s32[]{:T(128)} %constant.563.clone.1, s32[]{:T(128)S(6)} %select_n.827, s32[]{:T(128)} %constant.563.clone.1) | dynamic-update-slice | bytes 1048580 | tf_op jit(solution)/shard_map/dynamic_update_slice | solution.py:228
  428.3 19.3 %dynamic_update_slice.155 = bf16[2,512,4,512]{3,2,1,0:T(4,128)(2,1)} dynamic-update-slice(bf16[2,512,4,512]{3,2,1,0:T(4,128)(2,1)} %dynamic_update_slice.154, bf16[1,512,1,512]{3,2,1,0:T(2,128)(2,1)} %copy.438, s32[]{:T(128)S(6)} %select_n.849, s32[]{:T(128)} %constant.563.clone.1, s32[]{:T(128)S(6)} %select_n.827, s32[]{:T(128)} %constant.563.clone.1) | dynamic-update-slice | bytes 1048580 | tf_op jit(solution)/shard_map/dynamic_update_slice | solution.py:228
  447.5 19.3 %dynamic_update_slice.156 = bf16[2,512,4,512]{3,2,1,0:T(4,128)(2,1)} dynamic-update-slice(bf16[2,512,4,512]{3,2,1,0:T(4,128)(2,1)} %dynamic_update_slice.155, bf16[1,512,1,512]{3,2,1,0:T(2,128)(2,1)} %copy.439, s32[]{:T(128)S(6)} %select_n.848, s32[]{:T(128)} %constant.563.clone.1, s32[]{:T(128)S(6)} %select_n.823, s32[]{:T(128)} %constant.563.clone.1) | dynamic-update-slice | bytes 1048580 | tf_op jit(solution)/shard_map/dynamic_update_slice | solution.py:228
  466.8 19.3 %dynamic_update_slice.157 = bf16[2,512,4,512]{3,2,1,0:T(4,128)(2,1)} dynamic-update-slice(bf16[2,512,4,512]{3,2,1,0:T(4,128)(2,1)} %dynamic_update_slice.156, bf16[1,512,1,512]{3,2,1,0:T(2,128)(2,1)} %copy.440, s32[]{:T(128)S(6)} %select_n.849, s32[]{:T(128)} %constant.563.clone.1, s32[]{:T(128)S(6)} %select_n.823, s32[]{:T(128)} %constant.563.clone.1) | dynamic-update-slice | bytes 1048580 | tf_op jit(solution)/shard_map/dynamic_update_slice | solution.py:228
  581.7 49.2 %collective-permute-start.30 = (bf16[256,2048]{1,0:T(8,128)(2,1)}, bf16[256,2048]{1,0:T(8,128)(2,1)S(1)}, u32[]{:S(2)}, u32[]{:S(2)}) collective-permute-start(bf16[256,2048]{1,0:T(8,128)(2,1)} %get-tuple-element.162), channel_id=1, source_target_pairs={{0,1},{5,2},{6,3},{3,0},{8,9},{13,10},{14,11},{11,8},{16,17},{21,1... | collective-permute-start | bytes 3145736 | tf_op jit(solution)/shard_map/ppermute | solution.py:60
  665.4 38.3 %collective-permute-done.24 = bf16[128,2048]{1,0:T(8,128)(2,1)S(1)} collective-permute-done((bf16[128,2048]{1,0:T(8,128)(2,1)S(1)}, bf16[128,2048]{1,0:T(8,128)(2,1)S(1)}, u32[]{:S(2)}, u32[]{:S(2)}) %collective-permute-start.24) | collective-permute-done | bytes 524320 | tf_op jit(solution)/shard_map/ppermute | solution.py:57
  735.2 11.7 collective-permute-done.33
  841.4 15.6 add_convert_fusion
  937.9 20.4 %add_add_fusion = f32[2048,2048]{1,0:T(8,128)} fusion(f32[2048,2048]{1,0:T(8,128)} %fusion.25, f32[2048,2048]{1,0:T(8,128)} %fusion.24, bf16[1024,2048]{1,0:T(8,128)(2,1)S(1)} %constant_dynamic-update-slice_fusion, bf16[1024,1024]{1,0:T(8,128)(2,1)S(1)} %copy-done.41, bf16[1024,1024]{1,0:T(8,128)(2,1)S(1)} %copy-done.40), kind=kOutput, calls=%fused_computation.5 | convolution fusion | flops 8606711808 | bytes 58720256 | tf_op jit(solution)/shard_map/dot_general | solution.py:33
  1004.4 21.8 %collective-permute-start.97 = (bf16[128,2048]{1,0:T(8,128)(2,1)S(1)}, bf16[128,2048]{1,0:T(8,128)(2,1)S(1)}, u32[]{:S(2)}, u32[]{:S(2)}) collective-permute-start(bf16[128,2048]{1,0:T(8,128)(2,1)S(1)} %get-tuple-element.181), channel_id=1, source_target_pairs={{0,8},{4,12},{8,0},{12,4},{16,24},{20,28},{24,16},{28,20},{1,9},{5... | collective-permute-start | bytes 1572872 | tf_op jit(solution)/shard_map/ppermute | solution.py:54
  1026.3 11.2 collective-permute-start.105
  1052.3 11.0 collective-permute-done.101
  1077.6 16.0 %collective-permute-start.106 = (bf16[128,2048]{1,0:T(8,128)(2,1)S(1)}, bf16[128,2048]{1,0:T(8,128)(2,1)S(1)}, u32[]{:S(2)}, u32[]{:S(2)}) collective-permute-start(bf16[128,2048]{1,0:T(8,128)(2,1)S(1)} %get-tuple-element.183), channel_id=1, source_target_pairs={{0,3},{1,0},{2,1},{3,2},{4,7},{5,4},{6,5},{7,6},{8,11},{9,8},{10,9... | collective-permute-start | bytes 1572872 | tf_op jit(solution)/shard_map/ppermute | solution.py:57
  1110.2 44.1 %collective-permute-done.102 = bf16[128,2048]{1,0:T(8,128)(2,1)S(1)} collective-permute-done((bf16[128,2048]{1,0:T(8,128)(2,1)S(1)}, bf16[128,2048]{1,0:T(8,128)(2,1)S(1)}, u32[]{:S(2)}, u32[]{:S(2)}) %collective-permute-start.102) | collective-permute-done | bytes 524320 | tf_op jit(solution)/shard_map/ppermute | solution.py:57
  1155.3 18.3 %collective-permute-done.72 = bf16[128,2048]{1,0:T(8,128)(2,1)S(1)} collective-permute-done((bf16[128,2048]{1,0:T(8,128)(2,1)S(1)}, bf16[128,2048]{1,0:T(8,128)(2,1)S(1)}, u32[]{:S(2)}, u32[]{:S(2)}) %collective-permute-start.72) | collective-permute-done | bytes 524320 | tf_op jit(solution)/shard_map/ppermute | solution.py:57
  1184.7 10.9 add_add_fusion.1
  1236.9 24.1 %psum.15 = f32[2,4,128]{2,1,0:T(4,128)S(1)} all-reduce(f32[2,4,128]{2,1,0:T(4,128)S(1)} %fusion.91), channel_id=1, replica_groups=mesh['expert'=8,'wshard'=4] {'wshard'}, use_global_device_ids=true, to_apply=%region_23.26 | all-reduce | flops 1024 | bytes 8192 | tf_op jit(solution)/shard_map/psum | solution.py:73
  1313.2 20.2 %collective-permute-done.111 = bf16[128,2048]{1,0:T(8,128)(2,1)} collective-permute-done((bf16[128,2048]{1,0:T(8,128)(2,1)}, bf16[128,2048]{1,0:T(8,128)(2,1)}, u32[]{:S(2)}, u32[]{:S(2)}) %collective-permute-start.111) | collective-permute-done | bytes 524320 | tf_op jit(solution)/shard_map/ppermute | solution.py:57
  1381.2 17.6 %collective-permute-start.118 = (f32[18,64]{1,0:T(8,128)S(1)}, f32[18,64]{1,0:T(8,128)S(1)}, u32[]{:S(2)}, u32[]{:S(2)}) collective-permute-start(f32[18,64]{1,0:T(8,128)S(1)} %bitcast.614), channel_id=1, source_target_pairs={{0,3},{1,0},{2,1},{3,2},{4,7},{5,4},{6,5},{7,6},{8,11},{9,8},{10,9... | collective-permute-start | bytes 13832 | tf_op jit(solution)/shard_map/ppermute | solution.py:57
  1423.6 30.4 %collective-permute-done.116 = f32[18,64]{1,0:T(8,128)S(1)} collective-permute-done((f32[18,64]{1,0:T(8,128)S(1)}, f32[18,64]{1,0:T(8,128)S(1)}, u32[]{:S(2)}, u32[]{:S(2)}) %collective-permute-start.116) | collective-permute-done | bytes 4640 | tf_op jit(solution)/shard_map/ppermute | solution.py:57
  1464.4 21.1 %collective-permute-start.125 = (bf16[256,1536]{1,0:T(8,128)(2,1)S(1)}, bf16[256,1536]{1,0:T(8,128)(2,1)S(1)}, u32[]{:S(2)}, u32[]{:S(2)}) collective-permute-start(bf16[256,1536]{1,0:T(8,128)(2,1)S(1)} %dynamic-slice_bitcast_fusion.13), channel_id=1, source_target_pairs={{0,16},{4,20},{8,24},{12,28},{16,0},{20,4},{24,8},{28,12},{1,17},{... | collective-permute-start | bytes 2359304 | tf_op jit(solution)/shard_map/ppermute | solution.py:54
  1485.5 25.0 %collective-permute-done.138 = bf16[256,2048]{1,0:T(8,128)(2,1)} collective-permute-done((bf16[256,2048]{1,0:T(8,128)(2,1)S(1)}, bf16[256,2048]{1,0:T(8,128)(2,1)}, u32[]{:S(2)}, u32[]{:S(2)}) %collective-permute-start.138) | collective-permute-done | bytes 1048608 | tf_op jit(solution)/shard_map/ppermute | solution.py:60
  1531.4 21.0 %collective-permute-start.127 = (bf16[64,3,512]{2,0,1:T(8,128)(2,1)S(1)}, bf16[64,3,512]{2,0,1:T(8,128)(2,1)}, u32[]{:S(2)}, u32[]{:S(2)}) collective-permute-start(bf16[64,3,512]{2,0,1:T(8,128)(2,1)S(1)} %bitcast.604), channel_id=1, source_target_pairs={{0,2},{1,3},{2,0},{3,1},{4,6},{5,7},{6,4},{7,5},{8,10},{9,11},{10,... | collective-permute-start | bytes 589832 | tf_op jit(solution)/shard_map/ppermute | solution.py:57
  (839 shorter events, 839.1 us)
Async XLA Ops:
  8.4 120.4 %collective-permute-start.3 = (bf16[64,3,512]{2,0,1:T(8,128)(2,1)}, bf16[64,3,512]{2,0,1:T(8,128)(2,1)}, u32[]{:S(2)}, u32[]{:S(2)}) collective-permute-start(bf16[64,3,512]{2,0,1:T(8,128)(2,1)} %bitcast.537), channel_id=1, source_target_pairs={{0,1},{1,2},{2,3},{3,0},{4,5},{5,6},{6,7},{7,4},{8,9},{9,10},{10,1... | collective-permute-start | bytes 589832 | tf_op jit(solution)/shard_map/ppermute | solution.py:57
  12.1 120.6 %collective-permute-start.4 = (bf16[64,3,512]{2,0,1:T(8,128)(2,1)}, bf16[64,3,512]{2,0,1:T(8,128)(2,1)}, u32[]{:S(2)}, u32[]{:S(2)}) collective-permute-start(bf16[64,3,512]{2,0,1:T(8,128)(2,1)} %bitcast.536), channel_id=1, source_target_pairs={{0,2},{1,3},{2,0},{3,1},{4,6},{5,7},{6,4},{7,5},{8,10},{9,11},{10,... | collective-permute-start | bytes 589832 | tf_op jit(solution)/shard_map/ppermute | solution.py:57
  15.4 121.2 %collective-permute-start.5 = (bf16[64,3,512]{2,0,1:T(8,128)(2,1)}, bf16[64,3,512]{2,0,1:T(8,128)(2,1)S(1)}, u32[]{:S(2)}, u32[]{:S(2)}) collective-permute-start(bf16[64,3,512]{2,0,1:T(8,128)(2,1)} %bitcast.535), channel_id=1, source_target_pairs={{0,3},{1,0},{2,1},{3,2},{4,7},{5,4},{6,5},{7,6},{8,11},{9,8},{10,9... | collective-permute-start | bytes 589832 | tf_op jit(solution)/shard_map/ppermute | solution.py:57
  18.0 199.7 %collective-permute-start.2 = (bf16[128,2048]{1,0:T(8,128)(2,1)}, bf16[128,2048]{1,0:T(8,128)(2,1)}, u32[]{:S(2)}, u32[]{:S(2)}) collective-permute-start(bf16[128,2048]{1,0:T(8,128)(2,1)} %fusion.48), channel_id=1, source_target_pairs={{0,1},{1,2},{2,3},{3,0},{4,5},{5,6},{6,7},{7,4},{8,9},{9,10},{10,1... | collective-permute-start | bytes 1572872 | tf_op jit(solution)/shard_map/ppermute | solution.py:57
  23.0 120.8 %collective-permute-start.39 = (bf16[512,512]{1,0:T(8,128)(2,1)}, bf16[512,512]{1,0:T(8,128)(2,1)}, u32[]{:S(2)}, u32[]{:S(2)}) collective-permute-start(bf16[512,512]{1,0:T(8,128)(2,1)} %get-tuple-element.198), channel_id=1, source_target_pairs={{6,2},{7,3},{14,10},{15,11},{22,18},{23,19},{30,26},{31,27}} | collective-permute-start | bytes 1572872 | tf_op jit(solution)/shard_map/ppermute | solution.py:60
  147.2 62.7 %collective-permute-start.47 = (bf16[512,512]{1,0:T(8,128)(2,1)S(1)}, bf16[512,512]{1,0:T(8,128)(2,1)S(1)}, u32[]{:S(2)}, u32[]{:S(2)}) collective-permute-start(bf16[512,512]{1,0:T(8,128)(2,1)S(1)} %copy-done.72), channel_id=1, source_target_pairs={{4,7},{1,4},{2,5},{7,6},{12,15},{9,12},{10,13},{15,14},{20,23},{17... | collective-permute-start | bytes 1572872 | tf_op jit(solution)/shard_map/ppermute | solution.py:60
  152.3 65.5 %collective-permute-start.1 = (bf16[128,2048]{1,0:T(8,128)(2,1)}, bf16[128,2048]{1,0:T(8,128)(2,1)S(1)}, u32[]{:S(2)}, u32[]{:S(2)}) collective-permute-start(bf16[128,2048]{1,0:T(8,128)(2,1)} %fusion.48), channel_id=1, source_target_pairs={{0,2},{1,3},{2,0},{3,1},{4,6},{5,7},{6,4},{7,5},{8,10},{9,11},{10,... | collective-permute-start | bytes 1572872 | tf_op jit(solution)/shard_map/ppermute | solution.py:57
  217.9 93.5 %collective-permute-start.27 = (bf16[256,2048]{1,0:T(8,128)(2,1)}, bf16[256,2048]{1,0:T(8,128)(2,1)}, u32[]{:S(2)}, u32[]{:S(2)}) collective-permute-start(bf16[256,2048]{1,0:T(8,128)(2,1)} %get-tuple-element.163), channel_id=1, source_target_pairs={{6,2},{7,3},{14,10},{15,11},{22,18},{23,19},{30,26},{31,27}} | collective-permute-start | bytes 3145736 | tf_op jit(solution)/shard_map/ppermute | solution.py:60
  219.5 93.3 %collective-permute-start.26 = (bf16[256,2048]{1,0:T(8,128)(2,1)}, bf16[256,2048]{1,0:T(8,128)(2,1)}, u32[]{:S(2)}, u32[]{:S(2)}) collective-permute-start(bf16[256,2048]{1,0:T(8,128)(2,1)} %get-tuple-element.161), channel_id=1, source_target_pairs={{0,4},{1,5},{8,12},{9,13},{16,20},{17,21},{24,28},{25,29}} | collective-permute-start | bytes 3145736 | tf_op jit(solution)/shard_map/ppermute | solution.py:60
  338.1 153.6 %collective-permute-start.86 = (bf16[128,2048]{1,0:T(8,128)(2,1)}, bf16[128,2048]{1,0:T(8,128)(2,1)}, u32[]{:S(2)}, u32[]{:S(2)}) collective-permute-start(bf16[128,2048]{1,0:T(8,128)(2,1)} %collective-permute-done.77), channel_id=1, source_target_pairs={{0,8},{4,12},{8,0},{12,4},{16,24},{20,28},{24,16},{28,20},{1,9},{5... | collective-permute-start | bytes 1572872 | tf_op jit(solution)/shard_map/ppermute | solution.py:54
  340.0 151.7 %collective-permute-start.13 = (bf16[4,32,1536]{2,1,0:T(8,128)(2,1)}, bf16[4,32,1536]{2,1,0:T(8,128)(2,1)}, u32[]{:S(2)}, u32[]{:S(2)}) collective-permute-start(bf16[4,32,1536]{2,1,0:T(8,128)(2,1)} %get-tuple-element.219), channel_id=1, source_target_pairs={{0,16},{4,20},{8,24},{12,28},{16,0},{20,4},{24,8},{28,12},{1,17},{... | collective-permute-start | bytes 1179656 | tf_op jit(solution)/shard_map/ppermute | solution.py:54
  340.7 154.0 %collective-permute-start.88 = (bf16[128,2048]{1,0:T(8,128)(2,1)}, bf16[128,2048]{1,0:T(8,128)(2,1)}, u32[]{:S(2)}, u32[]{:S(2)}) collective-permute-start(bf16[128,2048]{1,0:T(8,128)(2,1)} %collective-permute-done.78), channel_id=1, source_target_pairs={{0,16},{4,20},{8,24},{12,28},{16,0},{20,4},{24,8},{28,12},{1,17},{... | collective-permute-start | bytes 1572872 | tf_op jit(solution)/shard_map/ppermute | solution.py:54
  342.2 161.3 %collective-permute-start.90 = (bf16[128,2048]{1,0:T(8,128)(2,1)}, bf16[128,2048]{1,0:T(8,128)(2,1)}, u32[]{:S(2)}, u32[]{:S(2)}) collective-permute-start(bf16[128,2048]{1,0:T(8,128)(2,1)} %collective-permute-done.79), channel_id=1, source_target_pairs={{0,16},{4,20},{8,24},{12,28},{16,0},{20,4},{24,8},{28,12},{1,17},{... | collective-permute-start | bytes 1572872 | tf_op jit(solution)/shard_map/ppermute | solution.py:54
  348.7 147.3 %collective-permute-start.14 = (bf16[4,32,1536]{2,1,0:T(8,128)(2,1)}, bf16[4,32,1536]{2,1,0:T(8,128)(2,1)}, u32[]{:S(2)}, u32[]{:S(2)}) collective-permute-start(bf16[4,32,1536]{2,1,0:T(8,128)(2,1)} %get-tuple-element.219), channel_id=1, source_target_pairs={{0,8},{4,12},{8,0},{12,4},{16,24},{20,28},{24,16},{28,20},{1,9},{5... | collective-permute-start | bytes 1179656 | tf_op jit(solution)/shard_map/ppermute | solution.py:54
  505.1 66.3 %collective-permute-start.87 = (bf16[128,2048]{1,0:T(8,128)(2,1)}, bf16[128,2048]{1,0:T(8,128)(2,1)}, u32[]{:S(2)}, u32[]{:S(2)}) collective-permute-start(bf16[128,2048]{1,0:T(8,128)(2,1)} %collective-permute-done.86), channel_id=1, source_target_pairs={{0,16},{4,20},{8,24},{12,28},{16,0},{20,4},{24,8},{28,12},{1,17},{... | collective-permute-start | bytes 1572872 | tf_op jit(solution)/shard_map/ppermute | solution.py:54
  512.4 60.9 %collective-permute-start.89 = (bf16[128,2048]{1,0:T(8,128)(2,1)}, bf16[128,2048]{1,0:T(8,128)(2,1)}, u32[]{:S(2)}, u32[]{:S(2)}) collective-permute-start(bf16[128,2048]{1,0:T(8,128)(2,1)} %collective-permute-done.88), channel_id=1, source_target_pairs={{0,8},{4,12},{8,0},{12,4},{16,24},{20,28},{24,16},{28,20},{1,9},{5... | collective-permute-start | bytes 1572872 | tf_op jit(solution)/shard_map/ppermute | solution.py:54
  515.0 61.6 %collective-permute-start.91 = (bf16[128,2048]{1,0:T(8,128)(2,1)}, bf16[128,2048]{1,0:T(8,128)(2,1)}, u32[]{:S(2)}, u32[]{:S(2)}) collective-permute-start(bf16[128,2048]{1,0:T(8,128)(2,1)} %collective-permute-done.90), channel_id=1, source_target_pairs={{0,8},{4,12},{8,0},{12,4},{16,24},{20,28},{24,16},{28,20},{1,9},{5... | collective-permute-start | bytes 1572872 | tf_op jit(solution)/shard_map/ppermute | solution.py:54
  569.0 66.9 %collective-permute-start.21 = (bf16[128,2048]{1,0:T(8,128)(2,1)}, bf16[128,2048]{1,0:T(8,128)(2,1)}, u32[]{:S(2)}, u32[]{:S(2)}) collective-permute-start(bf16[128,2048]{1,0:T(8,128)(2,1)} %get-tuple-element.202), channel_id=1, source_target_pairs={{0,2},{1,3},{2,0},{3,1},{4,6},{5,7},{6,4},{7,5},{8,10},{9,11},{10,... | collective-permute-start | bytes 1572872 | tf_op jit(solution)/shard_map/ppermute | solution.py:57
  571.4 65.2 %collective-permute-start.20 = (bf16[128,2048]{1,0:T(8,128)(2,1)}, bf16[128,2048]{1,0:T(8,128)(2,1)S(1)}, u32[]{:S(2)}, u32[]{:S(2)}) collective-permute-start(bf16[128,2048]{1,0:T(8,128)(2,1)} %get-tuple-element.200), channel_id=1, source_target_pairs={{0,1},{1,2},{2,3},{3,0},{4,5},{5,6},{6,7},{7,4},{8,9},{9,10},{10,1... | collective-permute-start | bytes 1572872 | tf_op jit(solution)/shard_map/ppermute | solution.py:57
  573.3 68.3 %collective-permute-start.29 = (bf16[256,2048]{1,0:T(8,128)(2,1)}, bf16[256,2048]{1,0:T(8,128)(2,1)S(1)}, u32[]{:S(2)}, u32[]{:S(2)}) collective-permute-start(bf16[256,2048]{1,0:T(8,128)(2,1)} %get-tuple-element.160), channel_id=1, source_target_pairs={{0,5},{5,6},{6,7},{3,4},{8,13},{13,14},{14,15},{11,12},{16,21},{21... | collective-permute-start | bytes 3145736 | tf_op jit(solution)/shard_map/ppermute | solution.py:60
  576.6 64.0 %collective-permute-start.28 = (bf16[256,2048]{1,0:T(8,128)(2,1)}, bf16[256,2048]{1,0:T(8,128)(2,1)S(1)}, u32[]{:S(2)}, u32[]{:S(2)}) collective-permute-start(bf16[256,2048]{1,0:T(8,128)(2,1)} %get-tuple-element.124), channel_id=1, source_target_pairs={{0,4},{4,0},{8,12},{12,8},{16,20},{20,16},{24,28},{28,24},{1,5},{5... | collective-permute-start | bytes 3145736 | tf_op jit(solution)/shard_map/ppermute | solution.py:54
  581.7 70.6 %collective-permute-start.30 = (bf16[256,2048]{1,0:T(8,128)(2,1)}, bf16[256,2048]{1,0:T(8,128)(2,1)S(1)}, u32[]{:S(2)}, u32[]{:S(2)}) collective-permute-start(bf16[256,2048]{1,0:T(8,128)(2,1)} %get-tuple-element.162), channel_id=1, source_target_pairs={{0,1},{5,2},{6,3},{3,0},{8,9},{13,10},{14,11},{11,8},{16,17},{21,1... | collective-permute-start | bytes 3145736 | tf_op jit(solution)/shard_map/ppermute | solution.py:60
  635.9 98.9 %collective-permute-start.32 = (bf16[256,2048]{1,0:T(8,128)(2,1)}, bf16[256,2048]{1,0:T(8,128)(2,1)S(1)}, u32[]{:S(2)}, u32[]{:S(2)}) collective-permute-start(bf16[256,2048]{1,0:T(8,128)(2,1)} %get-tuple-element.159), channel_id=1, source_target_pairs={{4,6},{5,7},{2,4},{3,5},{12,14},{13,15},{10,12},{11,13},{20,22},{2... | collective-permute-start | bytes 3145736 | tf_op jit(solution)/shard_map/ppermute | solution.py:60
  639.6 66.9 %collective-permute-start.50 = (bf16[128,2048]{1,0:T(8,128)(2,1)S(1)}, bf16[128,2048]{1,0:T(8,128)(2,1)S(1)}, u32[]{:S(2)}, u32[]{:S(2)}) collective-permute-start(bf16[128,2048]{1,0:T(8,128)(2,1)S(1)} %multiply_convert_fusion.10), channel_id=1, source_target_pairs={{0,16},{4,20},{8,24},{12,28},{16,0},{20,4},{24,8},{28,12},{1,17},{... | collective-permute-start | bytes 1572872 | tf_op jit(solution)/shard_map/ppermute | solution.py:54
  641.6 62.1 %collective-permute-start.24 = (bf16[128,2048]{1,0:T(8,128)(2,1)S(1)}, bf16[128,2048]{1,0:T(8,128)(2,1)S(1)}, u32[]{:S(2)}, u32[]{:S(2)}) collective-permute-start(bf16[128,2048]{1,0:T(8,128)(2,1)S(1)} %multiply_convert_fusion.10), channel_id=1, source_target_pairs={{0,2},{1,3},{2,0},{3,1},{4,6},{5,7},{6,4},{7,5},{8,10},{9,11},{10,... | collective-permute-start | bytes 1572872 | tf_op jit(solution)/shard_map/ppermute | solution.py:57
  861.5 116.7 %collective-permute-start.93 = (bf16[128,2048]{1,0:T(8,128)(2,1)}, bf16[128,2048]{1,0:T(8,128)(2,1)}, u32[]{:S(2)}, u32[]{:S(2)}) collective-permute-start(bf16[128,2048]{1,0:T(8,128)(2,1)} %get-tuple-element.148), channel_id=1, source_target_pairs={{0,16},{4,20},{8,24},{12,28},{16,0},{20,4},{24,8},{28,12},{1,17},{... | collective-permute-start | bytes 1572872 | tf_op jit(solution)/shard_map/ppermute | solution.py:54
  891.9 86.8 %collective-permute-start.104 = (bf16[128,2048]{1,0:T(8,128)(2,1)}, bf16[128,2048]{1,0:T(8,128)(2,1)}, u32[]{:S(2)}, u32[]{:S(2)}) collective-permute-start(bf16[128,2048]{1,0:T(8,128)(2,1)} %get-tuple-element.142), channel_id=1, source_target_pairs={{0,8},{4,12},{8,0},{12,4},{16,24},{20,28},{24,16},{28,20},{1,9},{5... | collective-permute-start | bytes 1572872 | tf_op jit(solution)/shard_map/ppermute | solution.py:54
  892.3 87.4 %collective-permute-start.100 = (bf16[128,2048]{1,0:T(8,128)(2,1)}, bf16[128,2048]{1,0:T(8,128)(2,1)}, u32[]{:S(2)}, u32[]{:S(2)}) collective-permute-start(bf16[128,2048]{1,0:T(8,128)(2,1)} %get-tuple-element.144), channel_id=1, source_target_pairs={{0,8},{4,12},{8,0},{12,4},{16,24},{20,28},{24,16},{28,20},{1,9},{5... | collective-permute-start | bytes 1572872 | tf_op jit(solution)/shard_map/ppermute | solution.py:54
  894.0 87.5 %collective-permute-start.96 = (bf16[128,2048]{1,0:T(8,128)(2,1)}, bf16[128,2048]{1,0:T(8,128)(2,1)}, u32[]{:S(2)}, u32[]{:S(2)}) collective-permute-start(bf16[128,2048]{1,0:T(8,128)(2,1)} %get-tuple-element.146), channel_id=1, source_target_pairs={{0,16},{4,20},{8,24},{12,28},{16,0},{20,4},{24,8},{28,12},{1,17},{... | collective-permute-start | bytes 1572872 | tf_op jit(solution)/shard_map/ppermute | solution.py:54
  895.0 86.7 %collective-permute-start.95 = (bf16[128,2048]{1,0:T(8,128)(2,1)}, bf16[128,2048]{1,0:T(8,128)(2,1)}, u32[]{:S(2)}, u32[]{:S(2)}) collective-permute-start(bf16[128,2048]{1,0:T(8,128)(2,1)} %get-tuple-element.147), channel_id=1, source_target_pairs={{0,16},{4,20},{8,24},{12,28},{16,0},{20,4},{24,8},{28,12},{1,17},{... | collective-permute-start | bytes 1572872 | tf_op jit(solution)/shard_map/ppermute | solution.py:54
  1155.2 249.9 %collective-permute-start.133 = (bf16[4,256,2048]{2,1,0:T(8,128)(2,1)}, bf16[4,256,2048]{2,1,0:T(8,128)(2,1)}, u32[]{:S(2)}, u32[]{:S(2)}) collective-permute-start(bf16[4,256,2048]{2,1,0:T(8,128)(2,1)} %fusion.5), channel_id=1, source_target_pairs={{0,4},{4,0},{8,12},{12,8},{16,20},{20,16},{24,28},{28,24},{1,5},{5... | collective-permute-start | bytes 12582920 | tf_op jit(solution)/shard_map/ppermute | solution.py:54
  1211.2 83.6 %collective-permute-start.142 = (bf16[512,4,512]{2,0,1:T(8,128)(2,1)}, bf16[512,4,512]{2,0,1:T(8,128)(2,1)}, u32[]{:S(2)}, u32[]{:S(2)}) collective-permute-start(bf16[512,4,512]{2,0,1:T(8,128)(2,1)} %bitcast.526), channel_id=1, source_target_pairs={{0,4},{4,0},{8,12},{12,8},{16,20},{20,16},{24,28},{28,24},{1,5},{5... | collective-permute-start | bytes 6291464 | tf_op jit(solution)/shard_map/ppermute | solution.py:54
  (242 other events, 7963.4 us)

commit v2 on v1

v2 whole, which is shorter than its diff:
```python
import jax
import jax.numpy as jnp
from jax import lax
from jax.sharding import PartitionSpec as P

HEADS = 16
EPS = 1e-05
THETA = 10000.0
ROUND_TOKENS = 2048
AXES = ("expert", "wshard")
LOW = jnp.bfloat16
F32 = jnp.float32


def rms_scale(values):
    return lax.rsqrt(jnp.mean(values * values, axis=-1, keepdims=True) + EPS)


def rotate(values, cosine, sine):
    half = values.shape[-1] // 2
    first = values[..., :half]
    second = values[..., half:]
    return jnp.concatenate(
        [first * cosine - second * sine, second * cosine + first * sine], axis=-1
    )


def norm_back(values, scale, gain, grads, inner):
    weighted = gain * grads
    return scale * weighted - values * scale * scale * scale * inner


def dot(a, b, dims):
    return lax.dot_general(a, b, (dims, ((), ())), preferred_element_type=F32)


def mm(a, b):
    return dot(a, b, ((1,), (0,)))


def mm_t(a, b):
    return dot(a, b, ((1,), (1,)))


def t_mm(a, b):
    return dot(a, b, ((0,), (0,)))


def build(n_e, n_w):
    bits = [1 << b for b in range(n_e.bit_length() - 1)]
    plane = bits[1:]
    nd = len(plane)

    def swap(x, d):
        return lax.ppermute(x, "expert", [(i, i ^ d) for i in range(n_e)])

    def shift(x, s):
        return lax.ppermute(x, "wshard", [(j, (j + s) % n_w) for j in range(n_w)])

    def joint(x, pairs):
        return lax.ppermute(x, AXES, pairs)

    def line_gather(x):
        return [x] + [shift(x, n_w - r) for r in range(1, n_w)]

    def line_scatter(blocks):
        total = blocks[0].astype(F32)
        for r in range(1, n_w):
            total = total + shift(blocks[r], r).astype(F32)
        return total

    def line_exchange(x, shard):
        out = jnp.zeros_like(x)
        for s in range(n_w):
            got = lax.dynamic_index_in_dim(x, (shard + s) % n_w, 0, keepdims=False)
            got = shift(got, s) if s else got
            out = lax.dynamic_update_index_in_dim(out, got, (shard - s + n_w) % n_w, 0)
        return out

    def line_sum(x, shard):
        x = jnp.roll(x.reshape(2, n_w, -1), shard, axis=1)
        return jnp.roll(lax.psum(x, "wshard"), -shard, axis=1)

    def plane_gather(parts):
        held = [([0], x) for x in parts]
        groups = [held]
        for step in range(nd):
            got = []
            for p, (masks, x) in enumerate(held):
                d = plane[(step + p) % nd]
                got.append(([m | d for m in masks], swap(x, d)))
            groups.append(got)
            held = [
                (a[0] + b[0], jnp.concatenate([a[1], b[1]], 0)) if step + 1 < nd else None
                for a, b in zip(held, got)
            ]
        return groups

    def plane_scatter(groups):
        out = []
        for p in range(nd):
            mine = [groups[step][p] for step in range(nd + 1)]
            for step in reversed(range(nd)):
                got = swap(mine[step + 1], plane[(step + p) % nd])
                at = 0
                for low in range(step + 1):
                    n = mine[low].shape[0]
                    mine[low] = (mine[low].astype(F32) + got[at : at + n].astype(F32)).astype(LOW)
                    at += n
            out.append(mine[0])
        return out

    def hyper_scatter(x, me, dims, kind):
        x = x.reshape((2,) * len(bits) + x.shape[1:])
        left = list(reversed(bits))
        for d in dims:
            at = left.index(d)
            bit = (me // d) % 2
            send = lax.dynamic_index_in_dim(x, 1 - bit, at, keepdims=False).astype(kind)
            keep = lax.dynamic_index_in_dim(x, bit, at, keepdims=False)
            x = (keep.astype(F32) + swap(send, d).astype(F32)).astype(kind)
            left.pop(at)
        return x

    def local(
        hidden_in,
        doc_ids,
        routes,
        attn_gain,
        q_gain,
        k_gain,
        ffn_gain,
        w_qkv,
        w_out,
        w_router,
        w_gate_up,
        w_down,
        cotangent,
    ):
        micro = hidden_in.shape[0]
        rows = hidden_in.shape[2]
        width = hidden_in.shape[3]
        heads = HEADS
        head = width // heads
        my_heads = heads // n_w
        cols = width // n_w
        experts = w_router.shape[1]
        local_experts = w_gate_up.shape[0]
        units = w_down.shape[1]
        own = micro * rows
        seq = n_w * rows
        me = lax.axis_index("expert")
        shard = lax.axis_index("wshard")
        scale = head ** (-0.5)

        tokens = hidden_in.reshape(own, width).astype(F32)
        scale_one = rms_scale(tokens)
        normed = (tokens * scale_one * attn_gain).astype(LOW)
        normed_all = jnp.concatenate(line_gather(normed), 0)

        piece = width // n_w // n_e
        mine = lax.dynamic_slice_in_dim(w_qkv, me * piece, piece, 0)
        mine = mine.reshape(piece, 3, n_w, cols).transpose(2, 0, 1, 3).reshape(n_w, piece, 3 * cols)
        bank = line_exchange(mine, shard)
        w_heads = jnp.zeros((n_e, n_w, piece, 3 * cols), LOW)
        half = piece // 2
        for p in range(2):
            masks, held = [0], bank[None, :, p * half : (p + 1) * half]
            for d in plane[p:] + plane[:p] + [1]:
                masks = masks + [m | d for m in masks]
                held = jnp.concatenate([held, swap(held, d)], 0)
            for at, m in enumerate(masks):
                w_heads = lax.dynamic_update_slice(
                    w_heads, held[at : at + 1], (jnp.bitwise_xor(me, m), 0, p * half, 0)
                )
        w_heads = w_heads.transpose(1, 0, 2, 3).reshape(width, 3 * cols)

        used = jnp.any(
            routes.reshape(own, -1, 1) == jnp.arange(experts, dtype=jnp.int32), axis=1
        ).astype(LOW)
        small = jnp.concatenate([w_router.reshape(-1, 128), used.reshape(-1, 128)], 0)
        cut = w_router.size // 128
        small = jnp.stack(line_gather(small))
        router = jnp.roll(small[:, :cut], shard, axis=0).reshape(width, experts)
        used = small[:, cut:].reshape(n_w, own, experts)

        hidden = units * local_experts // n_w
        up = w_gate_up.reshape(local_experts, -1, 2, n_w // local_experts, hidden)
        up = up.transpose(0, 3, 1, 2, 4).reshape(n_w, -1, 2 * hidden)
        dn = w_down.reshape(n_w, hidden, cols)
        up, dn, normed_all = lax.optimization_barrier((up, dn, normed_all))
        up = line_exchange(up, shard).reshape(width, 2 * hidden)
        dn = line_exchange(dn, shard).transpose(1, 0, 2).reshape(hidden, width)
        w_up = [up, swap(up, 1)]
        w_dn = [dn, swap(dn, 1)]
        my_expert = local_experts * me + shard * local_experts // n_w
        sib_expert = local_experts * jnp.bitwise_xor(me, 1) + shard * local_experts // n_w

        projected = mm(normed_all, w_heads)
        raw = projected.reshape(n_w, micro, rows, 3, my_heads, head)
        squares = jnp.sum(projected.reshape(-1, 3, cols)[:, :2] ** 2, axis=-1).T
        scales = lax.rsqrt(line_sum(squares, shard) / width + EPS)
        scales = scales.reshape(2, n_w, micro, rows, 1, 1)
        gain_q = lax.dynamic_slice_in_dim(q_gain, shard * cols, cols).reshape(my_heads, head)
        gain_k = lax.dynamic_slice_in_dim(k_gain, shard * cols, cols).reshape(my_heads, head)
        block_at = (shard + jnp.arange(n_w, dtype=jnp.int32)) % n_w
        positions = (
            block_at[:, None] * rows + jnp.arange(rows, dtype=jnp.int32)[None, :]
        )
        freq = THETA ** (-(jnp.arange(head // 2, dtype=F32) * 2.0 / head))
        angle = positions.astype(F32)[:, None, :, None, None] * freq
        cosine, sine = jnp.cos(angle), jnp.sin(angle)
        q_raw, k_raw, v_raw = raw[..., 0, :, :], raw[..., 1, :, :], raw[..., 2, :, :]
        queries = rotate(q_raw * scales[0] * gain_q, cosine, sine).astype(LOW)
        keys = rotate(k_raw * scales[1] * gain_k, cosine, sine).astype(LOW)
        values = v_raw.astype(LOW)

        def by_head(x):
            return x.transpose(1, 3, 0, 2, 4).reshape(micro * my_heads, seq, head)

        def by_token(x):
            x = x.reshape(micro, my_heads, n_w, rows, head)
            return x.transpose(2, 0, 3, 1, 4)

        q_h, k_h, v_h = by_head(queries), by_head(keys), by_head(values)
        flat_pos = positions.reshape(seq)
        docs = jnp.take(doc_ids[:, 0], flat_pos, axis=1)
        allowed = (flat_pos[None, :] <= flat_pos[:, None])[None] & (
            docs[:, :, None] == docs[:, None, :]
        )
        allowed = jnp.repeat(allowed, my_heads, axis=0)
        scores = jnp.einsum("bqd,bkd->bqk", q_h, k_h, preferred_element_type=F32) * scale
        scores = jnp.where(allowed, scores, -1e30)
        peak = jnp.max(scores, axis=-1, keepdims=True)
        expo = jnp.exp(scores - peak)
        probs = expo / jnp.sum(expo, axis=-1, keepdims=True)
        probs_low = probs.astype(LOW)
        attended = jnp.einsum("bqk,bkd->bqd", probs_low, v_h, preferred_element_type=F32)
        attended = by_token(attended.astype(LOW)).reshape(n_w * own, cols)
        branch = mm(attended, w_out).astype(LOW).reshape(n_w, own, width)
        resid = tokens + line_scatter([branch[r] for r in range(n_w)])

        scale_two = rms_scale(resid)
        ffn_in = (resid * scale_two * ffn_gain).astype(LOW)
        upstream = cotangent.reshape(own, width)
        per = n_w // nd
        expert_at = jnp.arange(experts, dtype=jnp.int32)[None, :]
        hots = [(expert_at == e).astype(F32) for e in (my_expert, sib_expert)]

        def to_parts(blocks):
            return [jnp.concatenate(blocks[p * per : (p + 1) * per], 0) for p in range(nd)]

        def to_owner(groups):
            blocks = []
            for part in plane_scatter(groups):
                blocks += jnp.split(part, per, 0)
            return line_scatter(blocks)

        def run_experts(ffn_rows, dy_rows, used_rows, grads):
            grad_up, grad_dn, grad_router = grads
            used = plane_gather(to_parts(used_rows))
            dy_groups = plane_gather(to_parts(line_gather(dy_rows)))
            x_groups = plane_gather(to_parts(line_gather(ffn_rows)))
            mix_parts, back_parts = [], []
            for x_group, dy_group, used_group in zip(x_groups, dy_groups, used):
                x = jnp.concatenate([b for _, b in x_group], 0)
                dy = jnp.concatenate([b for _, b in dy_group], 0)
                mask = jnp.concatenate([b for _, b in used_group], 0).astype(F32)
                gate_all = jax.nn.softmax(mm(x, router), axis=-1)
                mix, back, dlogits = 0.0, 0.0, 0.0
                for h in range(2):
                    gate = jnp.sum(gate_all * mask * hots[h], axis=-1, keepdims=True)
                    gate_up = mm(x, w_up[h])
                    g, u = gate_up[:, :hidden], gate_up[:, hidden:]
                    sigma = jax.nn.sigmoid(g)
                    silu = g * sigma
                    act = (silu * u).astype(LOW).astype(F32)
                    lifted = mm_t(dy, w_dn[h])
                    dgate = jnp.sum(act * lifted, axis=-1, keepdims=True)
                    act_gated = (act * gate).astype(LOW)
                    dact = lifted * gate
                    dgu = jnp.concatenate(
                        [dact * u * (sigma * (1.0 + g * (1.0 - sigma))), dact * silu], axis=-1
                    ).astype(LOW)
                    dlogits = dlogits + dgate * gate * (hots[h] - gate_all)
                    mix = mix + mm(act_gated, w_dn[h])
                    back = back + mm_t(dgu, w_up[h])
                    grad_up[h] = grad_up[h] + t_mm(x, dgu)
                    grad_dn[h] = grad_dn[h] + t_mm(act_gated, dy)
                dlogits = dlogits.astype(LOW)
                back = (back + mm_t(dlogits, router)).astype(LOW)
                grad_router = grad_router + t_mm(x, dlogits)
                mix_parts.append(jnp.split(mix.astype(LOW), nd, 0))
                back_parts.append(jnp.split(back, nd, 0))
            return to_owner(back_parts), to_owner(mix_parts), (grad_up, grad_dn, grad_router)

        rounds = max(1, n_e * n_w * own // 2 // ROUND_TOKENS)
        step = own // rounds
        grads = ([0.0, 0.0], [0.0, 0.0], 0.0)
        dffn, mixture = [], []
        for n in range(rounds):
            at = n * step
            ffn_rows, dy_rows = ffn_in[at : at + step], upstream[at : at + step]
            if n:
                ffn_rows, dy_rows, grads, dffn, mixture = lax.optimization_barrier(
                    (ffn_rows, dy_rows, grads, dffn, mixture)
                )
            used_rows = [used[r, at : at + step] for r in range(n_w)]
            back, mix, grads = run_experts(ffn_rows, dy_rows, used_rows, grads)
            dffn.append(back)
            mixture.append(mix)
        dffn, mixture = jnp.concatenate(dffn, 0), jnp.concatenate(mixture, 0)
        grad_up, grad_dn, grad_router = grads
        hidden_out = (resid + mixture).astype(LOW)

        up_sum = (grad_up[0] + swap(grad_up[1].astype(LOW), 1).astype(F32)).astype(LOW)
        dn_sum = (grad_dn[0] + swap(grad_dn[1].astype(LOW), 1).astype(F32)).astype(LOW)
        up_sum = line_exchange(up_sum.reshape(n_w, cols, 2 * hidden), shard)
        dn_sum = dn_sum.reshape(hidden, n_w, cols).transpose(1, 0, 2)
        dn_sum = line_exchange(dn_sum, shard)
        up_sum = up_sum.reshape(local_experts, n_w // local_experts, cols, 2, hidden)
        out_gate_up = up_sum.transpose(0, 2, 3, 1, 4).reshape(w_gate_up.shape).astype(F32)
        out_down = dn_sum.reshape(w_down.shape).astype(F32)

        upstream = upstream.astype(F32)
        weighted = ffn_gain * dffn
        inner = jnp.mean(resid * weighted, axis=-1, keepdims=True)
        dresid = upstream + norm_back(resid, scale_two, ffn_gain, dffn, inner)
        grad_ffn_gain = jnp.sum(dffn * resid * scale_two, axis=0)
        dbranch = jnp.concatenate(line_gather(dresid.astype(LOW)), 0)
        grad_out = t_mm(attended, dbranch)
        dattended = mm_t(dbranch, w_out).astype(LOW)
        datt_h = by_head(dattended.reshape(n_w, micro, rows, my_heads, head))
        dprobs = jnp.einsum("bqd,bkd->bqk", datt_h, v_h, preferred_element_type=F32)
        probs = jnp.where(allowed, probs, 0.0)
        dscores = probs * (dprobs - jnp.sum(probs * dprobs, axis=-1, keepdims=True))
        dscores = dscores.astype(LOW)
        dq = jnp.einsum("bqk,bkd->bqd", dscores, k_h, preferred_element_type=F32) * scale
        dk = jnp.einsum("bqk,bqd->bkd", dscores, q_h, preferred_element_type=F32) * scale
        dv = jnp.einsum("bqk,bqd->bkd", probs_low, datt_h, preferred_element_type=F32)
        dq = rotate(by_token(dq), cosine, -sine)
        dk = rotate(by_token(dk), cosine, -sine)
        dv = by_token(dv)
        inners = jnp.stack(
            [
                jnp.sum(q_raw * gain_q * dq, axis=(-2, -1)),
                jnp.sum(k_raw * gain_k * dk, axis=(-2, -1)),
            ]
        )
        inners = line_sum(inners, shard) / width
        inners = inners.reshape(2, n_w, micro, rows, 1, 1)
        dq_raw = norm_back(q_raw, scales[0], gain_q, dq, inners[0])
        dk_raw = norm_back(k_raw, scales[1], gain_k, dk, inners[1])
        grad_q = jnp.sum(dq * q_raw * scales[0], axis=(0, 1, 2)).reshape(cols)
        grad_k = jnp.sum(dk * k_raw * scales[1], axis=(0, 1, 2)).reshape(cols)
        dproj = jnp.stack([dq_raw, dk_raw, dv], axis=3).astype(LOW)
        dproj = dproj.reshape(n_w * own, 3 * cols)
        dnormed = mm_t(dproj, w_heads).astype(LOW).reshape(n_w, own, width)
        dnormed = line_scatter([dnormed[r] for r in range(n_w)])
        inner = jnp.mean(tokens * (attn_gain * dnormed), axis=-1, keepdims=True)
        dx = norm_back(tokens, scale_one, attn_gain, dnormed, inner)
        grad_in = (dresid + dx).astype(LOW)
        grad_attn_gain = jnp.sum(dnormed * tokens * scale_one, axis=0)
        grad_qkv = t_mm(normed_all, dproj)

        small = width // (n_e * n_w)
        core_first = [1] + plane
        qkv = hyper_scatter(grad_qkv.reshape(n_e, n_w * small, 3 * cols), me, core_first, LOW)
        qkv = line_exchange(qkv.reshape(n_w, small, 3 * cols), shard)
        qkv = qkv.reshape(n_w, small, 3, cols).transpose(1, 2, 0, 3)
        out_qkv = qkv.reshape(small, 3 * width).astype(F32)
        to_rows = [
            (i * n_w + w, w * n_e + i) for i in range(n_e) for w in range(n_w)
        ]
        out_rows = hyper_scatter(grad_out.reshape(n_e, small, width), me, core_first, LOW)
        out_rows = joint(out_rows, to_rows).astype(F32)
        gains = jnp.stack([grad_q, grad_k]).reshape(2, n_e, small).transpose(1, 0, 2)
        gains = joint(hyper_scatter(gains, me, core_first, F32), to_rows)
        pack = jnp.concatenate([grad_router.T, grad_attn_gain[None], grad_ffn_gain[None]], 0)
        pack = pack.reshape(experts + 2, n_e, n_w * small).transpose(1, 0, 2)
        pack = hyper_scatter(pack, me, core_first, F32)
        pack = pack.reshape(experts + 2, n_w, small)
        total = 0.0
        for s in range(n_w):
            got = lax.dynamic_index_in_dim(pack, (shard + s) % n_w, 1, keepdims=False)
            total = total + (shift(got, s) if s else got)
        return (
            hidden_out.reshape(micro, 1, rows, width),
            grad_in.reshape(micro, 1, rows, width),
            total[experts],
            gains[0],
            gains[1],
            total[experts + 1],
            out_qkv,
            out_rows,
            total[:experts].T,
            out_gate_up,
            out_down,
        )

    return local


def solution(mesh):
    in_specs = (
        P(None, "expert", "wshard", None),
        P(None, "expert", None),
        P(None, "expert", "wshard", None),
        P(),
        P(),
        P(),
        P(),
        P("wshard", None),
        P("wshard", None),
        P("wshard", None),
        P("expert", "wshard", None),
        P("expert", None, "wshard"),
        P(None, "expert", "wshard", None),
    )
    out_specs = (
        P(None, "expert", "wshard", None),
        P(None, "expert", "wshard", None),
        P(("expert", "wshard")),
        P(("expert", "wshard")),
        P(("expert", "wshard")),
        P(("expert", "wshard")),
        P(("expert", "wshard"), None),
        P(("expert", "wshard"), None),
        P(("expert", "wshard"), None),
        P("expert", "wshard", None),
        P("expert", None, "wshard"),
    )
    local = build(mesh.shape["expert"], mesh.shape["wshard"])
    return jax.shard_map(local, mesh=mesh, in_specs=in_specs, out_specs=out_specs, check_vma=False)
```

time: 1620 us -> 1170 us (0.72)
  starting transfers between devices: 357 us -> 117 us
  local copies, waits for them, and re-layouts: 376 us -> 237 us
  blocking collectives: 119 us -> 53.2 us
  matrix products: 207 us -> 228 us
    dynamic_update_slice x36 -> x37, local copies, waits for them, and re-layouts: 207 us -> 31.9 us  [the longest x21 25.1 us: line_exchange(): out = lax.dynamic_update_index_in_dim(out, got, (shard - s + n_w) % n_w, 0)]
    ppermute x34 -> x2, starting transfers between devices: 104 us -> 1.34 us  [joint(): return lax.ppermute(x, AXES, pairs)]
    all_gather x2 -> x0, blocking collectives: 86.8 us -> none  [the longest x1 66.1 us: local(): lax.all_gather(routes.reshape(own, -1), AXES, axis=0, tiled=False)]
    ppermute x34 -> x2, waiting for transfers between devices: 78.6 us -> 0.01 us  [joint(): return lax.ppermute(x, AXES, pairs)]
    ppermute x84 -> x42, starting transfers between devices: 128 us -> 54.8 us  [swap(): return lax.ppermute(x, 'expert', [(i, i ^ d) for i in range(n_e)])]
    ppermute x33 -> x48, waiting for transfers between devices: 203 us -> 270 us  [shift(): return lax.ppermute(x, 'wshard', [(j, (j + s) % n_w) for j in range(n_w)])]
    ppermute x33 -> x48, starting transfers between devices: 125 us -> 61.1 us  [shift(): return lax.ppermute(x, 'wshard', [(j, (j + s) % n_w) for j in range(n_w)])]
    concatenate x1 -> x18, other arithmetic: 0.22 us -> 25.6 us  [the longest x6 8.86 us: plane_gather(): jnp.concatenate([a[1], b[1]], 0)]
  transfers between devices with their start and end apart: 151 -> 92, of which waited for: 41 -> 32; matrix products, arithmetic and copies ran while one was open for 35% -> 43% of each run, Pallas kernels for 0% -> 0%
where the time goes in v2:
time: 1170 us; the launch traced here: 1150 us
  waiting for transfers between devices  418 us (36%)
  local copies, waits for them, and re-layouts  237 us (20%)
  matrix products  228 us (19%)
  starting transfers between devices  117 us (10%)
  other arithmetic  99.3 us (8%)
  blocking collectives  53.2 us (5%)
    ppermute x48, waiting for transfers between devices, shift(): return lax.ppermute(x, 'wshard', [(j, (j + s) % n_w) for j in range(n_w)])  270 us
    dot_general x51, matrix products, dot(): return lax.dot_general(a, b, (dims, ((), ())), preferred_element_type=F32)  216 us
    ppermute x42, waiting for transfers between devices, swap(): return lax.ppermute(x, 'expert', [(i, i ^ d) for i in range(n_e)])  148 us
    ppermute x48, starting transfers between devices, shift(): return lax.ppermute(x, 'wshard', [(j, (j + s) % n_w) for j in range(n_w)])  61.1 us
    ppermute x42, starting transfers between devices, swap(): return lax.ppermute(x, 'expert', [(i, i ^ d) for i in range(n_e)])  54.8 us
    psum x2, blocking collectives, line_sum(): return jnp.roll(lax.psum(x, 'wshard'), -shard, axis=1)  53.2 us
    unnamed x247, local copies, waits for them, and re-layouts  36.8 us
    dynamic_update_slice x21, local copies, waits for them, and re-layouts, line_exchange(): out = lax.dynamic_update_index_in_dim(out, got, (shard - s + n_w) % n_w, 0)  25.1 us
  transfers between devices with their start and end apart: 92, of which 32 were waited for; matrix products, arithmetic and copies ran while one was open for 43% of the time, Pallas kernels for 0%

profile of v2, /device:TPU:0, one launch (start us, length us, event | category | flops | bytes accessed | tf_op | source)
XLA Modules:
  0.0 1154.9 jit_solution(3184998316361908651)
XLA Ops:
  106.1 58.5 %collective-permute-done.45 = bf16[128,2048]{1,0:T(8,128)(2,1)} collective-permute-done((bf16[128,2048]{1,0:T(8,128)(2,1)}, bf16[128,2048]{1,0:T(8,128)(2,1)}, u32[]{:S(2)}, u32[]{:S(2)}) %collective-permute-start.45) | collective-permute-done | bytes 524320 | tf_op jit(solution)/shard_map/ppermute | solution.py:58
  206.4 23.7 %collective-permute-done.10 = bf16[2,4,32,1536]{3,2,0,1:T(8,128)(2,1)S(1)} collective-permute-done((bf16[2,4,32,1536]{3,2,0,1:T(8,128)(2,1)S(1)}, bf16[2,4,32,1536]{3,2,0,1:T(8,128)(2,1)S(1)}, u32[]{:S(2)}, u32[]{:S(2)}) %collective-permute-start.10) | collective-permute-done | bytes 786464 | tf_op jit(solution)/shard_map/ppermute | solution.py:55
  273.2 13.7 %psum.14 = f32[2,4,128]{2,1,0:T(4,128)S(1)} all-reduce(f32[2,4,128]{2,1,0:T(4,128)S(1)} %fusion.126), channel_id=1, replica_groups=mesh['expert'=8,'wshard'=4] {'wshard'}, use_global_device_ids=true, to_apply=%region_2.4 | all-reduce | flops 1024 | bytes 8192 | tf_op jit(solution)/shard_map/psum | solution.py:82
  315.5 32.2 %collective-permute-done.13 = bf16[128,2048]{1,0:T(8,128)(2,1)} collective-permute-done((bf16[128,2048]{1,0:T(8,128)(2,1)}, bf16[128,2048]{1,0:T(8,128)(2,1)}, u32[]{:S(2)}, u32[]{:S(2)}) %collective-permute-start.13) | collective-permute-done | bytes 524320 | tf_op jit(solution)/shard_map/ppermute | solution.py:58
  347.7 9.8 collective-permute-start.34
  367.0 18.4 %collective-permute-done.15 = bf16[128,2048]{1,0:T(8,128)(2,1)S(1)} collective-permute-done((bf16[128,2048]{1,0:T(8,128)(2,1)S(1)}, bf16[128,2048]{1,0:T(8,128)(2,1)S(1)}, u32[]{:S(2)}, u32[]{:S(2)}) %collective-permute-start.15) | collective-permute-done | bytes 524320 | tf_op jit(solution)/shard_map/ppermute | solution.py:58
  386.5 17.2 %collective-permute-done.16 = bf16[128,2048]{1,0:T(8,128)(2,1)S(1)} collective-permute-done((bf16[128,2048]{1,0:T(8,128)(2,1)S(1)}, bf16[128,2048]{1,0:T(8,128)(2,1)S(1)}, u32[]{:S(2)}, u32[]{:S(2)}) %collective-permute-start.16) | collective-permute-done | bytes 524320 | tf_op jit(solution)/shard_map/ppermute | solution.py:58
  415.0 17.1 %collective-permute-done.31 = bf16[256,2048]{1,0:T(8,128)(2,1)S(1)} collective-permute-done((bf16[256,2048]{1,0:T(8,128)(2,1)S(1)}, bf16[256,2048]{1,0:T(8,128)(2,1)S(1)}, u32[]{:S(2)}, u32[]{:S(2)}) %collective-permute-start.31) | collective-permute-done | bytes 1048608 | tf_op jit(solution)/shard_map/ppermute | solution.py:55
  531.0 7.5 add_convert_fusion.7
  540.3 6.8 fusion.172
  556.8 7.0 multiply_convert_fusion.4
  570.2 6.8 fusion.19
  577.0 14.1 %add_convert_fusion.2 = bf16[1024,2048]{1,0:T(8,128)(2,1)} fusion(f32[1024,2048]{1,0:T(8,128)} %fusion.151, f32[1024,2048]{1,0:T(8,128)} %fusion.19, bf16[2048,1024]{1,0:T(8,128)(2,1)} %bitcast.49, bf16[1024,512]{0,1:T(8,128)(2,1)} %get-tuple-element.126, bf16[1024,512]{0,1:T(8,128)(2,1)} %get-tuple-element.125), kind=kOutput, calls=%fused_computation.4 | convolution fusion | flops 4305453056 | bytes 27262976 | tf_op jit(solution)/shard_map/dot_general | solution.py:34
  615.3 11.3 add_convert_fusion.1
  626.6 8.0 fusion.20
  637.0 8.0 collective-permute-done.51
  659.8 9.6 constant_dynamic-slice_fusion.5
  676.4 13.5 %collective-permute-done.37 = bf16[512,2048]{1,0:T(8,128)(2,1)} collective-permute-done((bf16[512,2048]{1,0:T(8,128)(2,1)}, bf16[512,2048]{1,0:T(8,128)(2,1)}, u32[]{:S(2)}, u32[]{:S(2)}) %collective-permute-start.37) | collective-permute-done | bytes 2097184 | tf_op jit(solution)/shard_map/ppermute | solution.py:55
  708.9 12.9 %collective-permute-done.90 = bf16[512,512]{0,1:T(8,128)(2,1)} collective-permute-done((bf16[512,512]{0,1:T(8,128)(2,1)}, bf16[512,512]{0,1:T(8,128)(2,1)}, u32[]{:S(2)}, u32[]{:S(2)}) %collective-permute-start.90) | collective-permute-done | bytes 524320 | tf_op jit(solution)/shard_map/ppermute | solution.py:58
  732.9 13.5 %collective-permute-done.41 = bf16[256,2048]{1,0:T(8,128)(2,1)S(1)} collective-permute-done((bf16[256,2048]{1,0:T(8,128)(2,1)}, bf16[256,2048]{1,0:T(8,128)(2,1)S(1)}, u32[]{:S(2)}, u32[]{:S(2)}) %collective-permute-start.41) | collective-permute-done | bytes 1048608 | tf_op jit(solution)/shard_map/ppermute | solution.py:55
  755.3 43.9 %collective-permute-done.56 = bf16[128,2048]{1,0:T(8,128)(2,1)S(1)} collective-permute-done((bf16[128,2048]{1,0:T(8,128)(2,1)S(1)}, bf16[128,2048]{1,0:T(8,128)(2,1)S(1)}, u32[]{:S(2)}, u32[]{:S(2)}) %collective-permute-start.56) | collective-permute-done | bytes 524320 | tf_op jit(solution)/shard_map/ppermute | solution.py:58
  807.7 18.4 %collective-permute-done.42 = bf16[128,2048]{1,0:T(8,128)(2,1)} collective-permute-done((bf16[128,2048]{1,0:T(8,128)(2,1)}, bf16[128,2048]{1,0:T(8,128)(2,1)}, u32[]{:S(2)}, u32[]{:S(2)}) %collective-permute-start.42) | collective-permute-done | bytes 524320 | tf_op jit(solution)/shard_map/ppermute | solution.py:58
  836.0 11.6 %add_convert_fusion = bf16[2048,1024]{1,0:T(8,128)(2,1)S(1)} fusion(bf16[2048,1024]{1,0:T(8,128)(2,1)} %collective-permute-done.84, f32[2048,1024]{1,0:T(8,128)} %fusion.20, f32[2048,1024]{1,0:T(8,128)} %fusion.79, f32[2048,1024]{1,0:T(8,128)} %fusion.76), kind=kLoop, calls=%fused_computation.2 | loop fusion | flops 10485760 | bytes 33554432 | tf_op jit(solution)/shard_map/convert_element_type | solution.py:316
  852.2 17.0 %collective-permute-done.59 = bf16[128,2048]{1,0:T(8,128)(2,1)S(1)} collective-permute-done((bf16[128,2048]{1,0:T(8,128)(2,1)}, bf16[128,2048]{1,0:T(8,128)(2,1)S(1)}, u32[]{:S(2)}, u32[]{:S(2)}) %collective-permute-start.59) | collective-permute-done | bytes 524320 | tf_op jit(solution)/shard_map/ppermute | solution.py:58
  890.1 39.5 %psum.15 = f32[2,4,128]{2,1,0:T(4,128)S(1)} all-reduce(f32[2,4,128]{2,1,0:T(4,128)S(1)} %fusion.118), channel_id=1, replica_groups=mesh['expert'=8,'wshard'=4] {'wshard'}, use_global_device_ids=true, to_apply=%region_29.31 | all-reduce | flops 1024 | bytes 8192 | tf_op jit(solution)/shard_map/psum | solution.py:82
  971.1 25.7 %collective-permute-done.62 = bf16[128,2048]{1,0:T(8,128)(2,1)} collective-permute-done((bf16[128,2048]{1,0:T(8,128)(2,1)}, bf16[128,2048]{1,0:T(8,128)(2,1)}, u32[]{:S(2)}, u32[]{:S(2)}) %collective-permute-start.62) | collective-permute-done | bytes 524320 | tf_op jit(solution)/shard_map/ppermute | solution.py:58
  1034.5 42.2 %collective-permute-done.81 = bf16[2,64,2048]{2,1,0:T(8,128)(2,1)S(1)} collective-permute-done((bf16[2,64,2048]{2,1,0:T(8,128)(2,1)S(1)}, bf16[2,64,2048]{2,1,0:T(8,128)(2,1)S(1)}, u32[]{:S(2)}, u32[]{:S(2)}) %collective-permute-start.81) | collective-permute-done | bytes 524320 | tf_op jit(solution)/shard_map/ppermute | solution.py:55
  1080.6 21.6 %collective-permute-done.82 = bf16[64,2048]{1,0:T(8,128)(2,1)S(1)} collective-permute-done((bf16[64,2048]{1,0:T(8,128)(2,1)S(1)}, bf16[64,2048]{1,0:T(8,128)(2,1)S(1)}, u32[]{:S(2)}, u32[]{:S(2)}) %collective-permute-start.82) | collective-permute-done | bytes 262176 | tf_op jit(solution)/shard_map/ppermute | solution.py:55
  1109.1 6.9 copy.520
  1116.0 7.7 copy.521
  1123.8 8.7 copy.533
  1137.4 7.1 collective-permute-done.78
  (718 shorter events, 592.1 us)
Async XLA Ops:
  4.2 73.1 %collective-permute-start.2 = (bf16[128,2048]{1,0:T(8,128)(2,1)}, bf16[128,2048]{1,0:T(8,128)(2,1)}, u32[]{:S(2)}, u32[]{:S(2)}) collective-permute-start(bf16[128,2048]{1,0:T(8,128)(2,1)} %fusion.51), channel_id=1, source_target_pairs={{0,1},{1,2},{2,3},{3,0},{4,5},{5,6},{6,7},{7,4},{8,9},{9,10},{10,1... | collective-permute-start | bytes 1572872 | tf_op jit(solution)/shard_map/ppermute | solution.py:58
  7.2 70.6 %collective-permute-start.1 = (bf16[128,2048]{1,0:T(8,128)(2,1)}, bf16[128,2048]{1,0:T(8,128)(2,1)}, u32[]{:S(2)}, u32[]{:S(2)}) collective-permute-start(bf16[128,2048]{1,0:T(8,128)(2,1)} %fusion.51), channel_id=1, source_target_pairs={{0,2},{1,3},{2,0},{3,1},{4,6},{5,7},{6,4},{7,5},{8,10},{9,11},{10,... | collective-permute-start | bytes 1572872 | tf_op jit(solution)/shard_map/ppermute | solution.py:58
  77.2 87.3 %collective-permute-start.45 = (bf16[128,2048]{1,0:T(8,128)(2,1)}, bf16[128,2048]{1,0:T(8,128)(2,1)}, u32[]{:S(2)}, u32[]{:S(2)}) collective-permute-start(bf16[128,2048]{1,0:T(8,128)(2,1)} %bitcast.65), channel_id=1, source_target_pairs={{0,2},{1,3},{2,0},{3,1},{4,6},{5,7},{6,4},{7,5},{8,10},{9,11},{10,... | collective-permute-start | bytes 1572872 | tf_op jit(solution)/shard_map/ppermute | solution.py:58
  77.8 99.0 %collective-permute-start.6 = (bf16[1,4,32,1536]{3,2,1,0:T(8,128)(2,1)}, bf16[1,4,32,1536]{3,2,1,0:T(8,128)(2,1)}, u32[]{:S(2)}, u32[]{:S(2)}) collective-permute-start(bf16[1,4,32,1536]{3,2,1,0:T(8,128)(2,1)} %get-tuple-element.203), channel_id=1, source_target_pairs={{0,8},{4,12},{8,0},{12,4},{16,24},{20,28},{24,16},{28,20},{1,9},{5... | collective-permute-start | bytes 1179656 | tf_op jit(solution)/shard_map/ppermute | solution.py:55
  79.3 99.8 %collective-permute-start.9 = (bf16[1,4,32,1536]{3,2,0,1:T(8,128)(2,1)}, bf16[1,4,32,1536]{3,2,0,1:T(8,128)(2,1)}, u32[]{:S(2)}, u32[]{:S(2)}) collective-permute-start(bf16[1,4,32,1536]{3,2,0,1:T(8,128)(2,1)} %get-tuple-element.202), channel_id=1, source_target_pairs={{0,16},{4,20},{8,24},{12,28},{16,0},{20,4},{24,8},{28,12},{1,17},{... | collective-permute-start | bytes 1179656 | tf_op jit(solution)/shard_map/ppermute | solution.py:55
  100.0 142.1 %collective-permute-start.18 = (bf16[512,1024]{1,0:T(8,128)(2,1)}, bf16[512,1024]{1,0:T(8,128)(2,1)}, u32[]{:S(2)}, u32[]{:S(2)}) collective-permute-start(bf16[512,1024]{1,0:T(8,128)(2,1)} %bitcast.493), channel_id=1, source_target_pairs={{0,1},{1,2},{2,3},{3,0},{4,5},{5,6},{6,7},{7,4},{8,9},{9,10},{10,1... | collective-permute-start | bytes 3145736 | tf_op jit(solution)/shard_map/ppermute | solution.py:58
  106.1 78.7 %collective-permute-start.24 = (bf16[512,512]{1,0:T(8,128)(2,1)}, bf16[512,512]{1,0:T(8,128)(2,1)}, u32[]{:S(2)}, u32[]{:S(2)}) collective-permute-start(bf16[512,512]{1,0:T(8,128)(2,1)} %get-tuple-element.180), channel_id=1, source_target_pairs={{0,1},{1,2},{2,3},{3,0},{4,5},{5,6},{6,7},{7,4},{8,9},{9,10},{10,1... | collective-permute-start | bytes 1572872 | tf_op jit(solution)/shard_map/ppermute | solution.py:58
  184.7 59.9 %collective-permute-start.19 = (bf16[512,1024]{1,0:T(8,128)(2,1)}, bf16[512,1024]{1,0:T(8,128)(2,1)}, u32[]{:S(2)}, u32[]{:S(2)}) collective-permute-start(bf16[512,1024]{1,0:T(8,128)(2,1)} %bitcast.45), channel_id=1, source_target_pairs={{0,2},{1,3},{2,0},{3,1},{4,6},{5,7},{6,4},{7,5},{8,10},{9,11},{10,... | collective-permute-start | bytes 3145736 | tf_op jit(solution)/shard_map/ppermute | solution.py:58
  231.4 72.3 %collective-permute-start.20 = (bf16[512,1024]{1,0:T(8,128)(2,1)}, bf16[512,1024]{1,0:T(8,128)(2,1)}, u32[]{:S(2)}, u32[]{:S(2)}) collective-permute-start(bf16[512,1024]{1,0:T(8,128)(2,1)} %bitcast.47), channel_id=1, source_target_pairs={{0,3},{1,0},{2,1},{3,2},{4,7},{5,4},{6,5},{7,6},{8,11},{9,8},{10,9... | collective-permute-start | bytes 3145736 | tf_op jit(solution)/shard_map/ppermute | solution.py:58
  242.0 118.7 %collective-permute-start.48 = (bf16[512,2048]{1,0:T(8,128)(2,1)}, bf16[512,2048]{1,0:T(8,128)(2,1)}, u32[]{:S(2)}, u32[]{:S(2)}) collective-permute-start(bf16[512,2048]{1,0:T(8,128)(2,1)} %pad_maximum_fusion.7), channel_id=1, source_target_pairs={{0,16},{4,20},{8,24},{12,28},{16,0},{20,4},{24,8},{28,12},{1,17},{... | collective-permute-start | bytes 6291464 | tf_op jit(solution)/shard_map/ppermute | solution.py:55
  244.6 120.4 %collective-permute-start.50 = (bf16[512,2048]{1,0:T(8,128)(2,1)}, bf16[512,2048]{1,0:T(8,128)(2,1)}, u32[]{:S(2)}, u32[]{:S(2)}) collective-permute-start(bf16[512,2048]{1,0:T(8,128)(2,1)} %pad_maximum_fusion.8), channel_id=1, source_target_pairs={{0,8},{4,12},{8,0},{12,4},{16,24},{20,28},{24,16},{28,20},{1,9},{5... | collective-permute-start | bytes 6291464 | tf_op jit(solution)/shard_map/ppermute | solution.py:55
  303.7 53.9 %collective-permute-start.12 = (bf16[128,2048]{1,0:T(8,128)(2,1)}, bf16[128,2048]{1,0:T(8,128)(2,1)}, u32[]{:S(2)}, u32[]{:S(2)}) collective-permute-start(bf16[128,2048]{1,0:T(8,128)(2,1)} %get-tuple-element.182), channel_id=1, source_target_pairs={{0,1},{1,2},{2,3},{3,0},{4,5},{5,6},{6,7},{7,4},{8,9},{9,10},{10,1... | collective-permute-start | bytes 1572872 | tf_op jit(solution)/shard_map/ppermute | solution.py:58
  315.0 236.9 %collective-permute-start.36 = (bf16[512,16]{0,1:T(8,128)(2,1)S(1)}, bf16[512,16]{0,1:T(8,128)(2,1)S(1)}, u32[]{:S(2)}, u32[]{:S(2)}) collective-permute-start(bf16[512,16]{0,1:T(8,128)(2,1)S(1)} %copy-done.86), channel_id=1, source_target_pairs={{0,8},{4,12},{8,0},{12,4},{16,24},{20,28},{24,16},{28,20},{1,9},{5... | collective-permute-start | bytes 49160 | tf_op jit(solution)/shard_map/ppermute | solution.py:55
  347.7 204.1 %collective-permute-start.34 = (bf16[512,16]{0,1:T(8,128)(2,1)S(1)}, bf16[512,16]{0,1:T(8,128)(2,1)S(1)}, u32[]{:S(2)}, u32[]{:S(2)}) collective-permute-start(bf16[512,16]{0,1:T(8,128)(2,1)S(1)} %copy-done.87), channel_id=1, source_target_pairs={{0,16},{4,20},{8,24},{12,28},{16,0},{20,4},{24,8},{28,12},{1,17},{... | collective-permute-start | bytes 49160 | tf_op jit(solution)/shard_map/ppermute | solution.py:55
  385.3 88.0 %collective-permute-start.28 = (bf16[512,2048]{0,1:T(8,128)(2,1)}, bf16[512,2048]{0,1:T(8,128)(2,1)S(1)}, u32[]{:S(2)}, u32[]{:S(2)}) collective-permute-start(bf16[512,2048]{0,1:T(8,128)(2,1)} %bitcast.61), channel_id=1, source_target_pairs={{0,4},{4,0},{8,12},{12,8},{16,20},{20,16},{24,28},{28,24},{1,5},{5... | collective-permute-start | bytes 6291464 | tf_op jit(solution)/shard_map/ppermute | solution.py:55
  414.5 55.9 %collective-permute-start.27 = (bf16[2048,1024]{1,0:T(8,128)(2,1)}, bf16[2048,1024]{1,0:T(8,128)(2,1)S(1)}, u32[]{:S(2)}, u32[]{:S(2)}) collective-permute-start(bf16[2048,1024]{1,0:T(8,128)(2,1)} %bitcast.49), channel_id=1, source_target_pairs={{0,4},{4,0},{8,12},{12,8},{16,20},{20,16},{24,28},{28,24},{1,5},{5... | collective-permute-start | bytes 12582920 | tf_op jit(solution)/shard_map/ppermute | solution.py:55
  432.1 106.4 %collective-permute-start.30 = (bf16[512,2048]{1,0:T(8,128)(2,1)S(1)}, bf16[512,2048]{1,0:T(8,128)(2,1)S(1)}, u32[]{:S(2)}, u32[]{:S(2)}) collective-permute-start(bf16[512,2048]{1,0:T(8,128)(2,1)S(1)} %pad_maximum_fusion.3), channel_id=1, source_target_pairs={{0,16},{4,20},{8,24},{12,28},{16,0},{20,4},{24,8},{28,12},{1,17},{... | collective-permute-start | bytes 6291464 | tf_op jit(solution)/shard_map/ppermute | solution.py:55
  470.5 68.3 %collective-permute-start.32 = (bf16[512,2048]{1,0:T(8,128)(2,1)S(1)}, bf16[512,2048]{1,0:T(8,128)(2,1)S(1)}, u32[]{:S(2)}, u32[]{:S(2)}) collective-permute-start(bf16[512,2048]{1,0:T(8,128)(2,1)S(1)} %pad_maximum_fusion.4), channel_id=1, source_target_pairs={{0,8},{4,12},{8,0},{12,4},{16,24},{20,28},{24,16},{28,20},{1,9},{5... | collective-permute-start | bytes 6291464 | tf_op jit(solution)/shard_map/ppermute | solution.py:55
  596.0 48.9 %collective-permute-start.51 = (bf16[512,2048]{1,0:T(8,128)(2,1)}, bf16[512,2048]{1,0:T(8,128)(2,1)}, u32[]{:S(2)}, u32[]{:S(2)}) collective-permute-start(bf16[512,2048]{1,0:T(8,128)(2,1)} %get-tuple-element.137), channel_id=1, source_target_pairs={{0,16},{4,20},{8,24},{12,28},{16,0},{20,4},{24,8},{28,12},{1,17},{... | collective-permute-start | bytes 6291464 | tf_op jit(solution)/shard_map/ppermute | solution.py:55
  607.0 82.8 %collective-permute-start.37 = (bf16[512,2048]{1,0:T(8,128)(2,1)}, bf16[512,2048]{1,0:T(8,128)(2,1)}, u32[]{:S(2)}, u32[]{:S(2)}) collective-permute-start(bf16[512,2048]{1,0:T(8,128)(2,1)} %get-tuple-element.139), channel_id=1, source_target_pairs={{0,16},{4,20},{8,24},{12,28},{16,0},{20,4},{24,8},{28,12},{1,17},{... | collective-permute-start | bytes 6291464 | tf_op jit(solution)/shard_map/ppermute | solution.py:55
  608.8 81.4 %collective-permute-start.40 = (bf16[512,2048]{1,0:T(8,128)(2,1)}, bf16[512,2048]{1,0:T(8,128)(2,1)}, u32[]{:S(2)}, u32[]{:S(2)}) collective-permute-start(bf16[512,2048]{1,0:T(8,128)(2,1)} %get-tuple-element.140), channel_id=1, source_target_pairs={{0,8},{4,12},{8,0},{12,4},{16,24},{20,28},{24,16},{28,20},{1,9},{5... | collective-permute-start | bytes 6291464 | tf_op jit(solution)/shard_map/ppermute | solution.py:55
  644.9 191.0 %collective-permute-start.84 = (bf16[2048,1024]{1,0:T(8,128)(2,1)}, bf16[2048,1024]{1,0:T(8,128)(2,1)}, u32[]{:S(2)}, u32[]{:S(2)}) collective-permute-start(bf16[2048,1024]{1,0:T(8,128)(2,1)} %add_convert_fusion.1), channel_id=1, source_target_pairs={{0,4},{4,0},{8,12},{12,8},{16,20},{20,16},{24,28},{28,24},{1,5},{5... | collective-permute-start | bytes 12582920 | tf_op jit(solution)/shard_map/ppermute | solution.py:55
  648.9 75.9 %collective-permute-start.52 = (bf16[256,2048]{1,0:T(8,128)(2,1)}, bf16[256,2048]{1,0:T(8,128)(2,1)}, u32[]{:S(2)}, u32[]{:S(2)}) collective-permute-start(bf16[256,2048]{1,0:T(8,128)(2,1)} %get-tuple-element.172), channel_id=1, source_target_pairs={{0,8},{4,12},{8,0},{12,4},{16,24},{20,28},{24,16},{28,20},{1,9},{5... | collective-permute-start | bytes 3145736 | tf_op jit(solution)/shard_map/ppermute | solution.py:55
  650.4 74.4 %collective-permute-start.55 = (bf16[256,2048]{1,0:T(8,128)(2,1)}, bf16[256,2048]{1,0:T(8,128)(2,1)}, u32[]{:S(2)}, u32[]{:S(2)}) collective-permute-start(bf16[256,2048]{1,0:T(8,128)(2,1)} %get-tuple-element.173), channel_id=1, source_target_pairs={{0,16},{4,20},{8,24},{12,28},{16,0},{20,4},{24,8},{28,12},{1,17},{... | collective-permute-start | bytes 3145736 | tf_op jit(solution)/shard_map/ppermute | solution.py:55
  732.0 67.2 %collective-permute-start.56 = (bf16[128,2048]{1,0:T(8,128)(2,1)S(1)}, bf16[128,2048]{1,0:T(8,128)(2,1)S(1)}, u32[]{:S(2)}, u32[]{:S(2)}) collective-permute-start(bf16[128,2048]{1,0:T(8,128)(2,1)S(1)} %get-tuple-element.194), channel_id=1, source_target_pairs={{0,2},{1,3},{2,0},{3,1},{4,6},{5,7},{6,4},{7,5},{8,10},{9,11},{10,... | collective-permute-start | bytes 1572872 | tf_op jit(solution)/shard_map/ppermute | solution.py:58
  746.5 59.0 %collective-permute-start.53 = (bf16[128,2048]{1,0:T(8,128)(2,1)}, bf16[128,2048]{1,0:T(8,128)(2,1)}, u32[]{:S(2)}, u32[]{:S(2)}) collective-permute-start(bf16[128,2048]{1,0:T(8,128)(2,1)} %split.94), channel_id=1, source_target_pairs={{0,1},{1,2},{2,3},{3,0},{4,5},{5,6},{6,7},{7,4},{8,9},{9,10},{10,1... | collective-permute-start | bytes 1572872 | tf_op jit(solution)/shard_map/ppermute | solution.py:58
  751.5 56.2 %collective-permute-start.43 = (bf16[128,2048]{1,0:T(8,128)(2,1)}, bf16[128,2048]{1,0:T(8,128)(2,1)}, u32[]{:S(2)}, u32[]{:S(2)}) collective-permute-start(bf16[128,2048]{1,0:T(8,128)(2,1)} %get-tuple-element.197), channel_id=1, source_target_pairs={{0,3},{1,0},{2,1},{3,2},{4,7},{5,4},{6,5},{7,6},{8,11},{9,8},{10,9... | collective-permute-start | bytes 1572872 | tf_op jit(solution)/shard_map/ppermute | solution.py:58
  755.3 70.7 %collective-permute-start.42 = (bf16[128,2048]{1,0:T(8,128)(2,1)}, bf16[128,2048]{1,0:T(8,128)(2,1)}, u32[]{:S(2)}, u32[]{:S(2)}) collective-permute-start(bf16[128,2048]{1,0:T(8,128)(2,1)} %get-tuple-element.196), channel_id=1, source_target_pairs={{0,2},{1,3},{2,0},{3,1},{4,6},{5,7},{6,4},{7,5},{8,10},{9,11},{10,... | collective-permute-start | bytes 1572872 | tf_op jit(solution)/shard_map/ppermute | solution.py:58
  852.2 180.1 %collective-permute-start.85 = (bf16[512,1024]{1,0:T(8,128)(2,1)}, bf16[512,1024]{1,0:T(8,128)(2,1)}, u32[]{:S(2)}, u32[]{:S(2)}) collective-permute-start(bf16[512,1024]{1,0:T(8,128)(2,1)} %get-tuple-element.135), channel_id=1, source_target_pairs={{0,1},{1,2},{2,3},{3,0},{4,5},{5,6},{6,7},{7,4},{8,9},{9,10},{10,1... | collective-permute-start | bytes 3145736 | tf_op jit(solution)/shard_map/ppermute | solution.py:58
  970.6 52.9 %collective-permute-start.74 = (bf16[2,2,256,1536]{3,2,1,0:T(8,128)(2,1)}, bf16[2,2,256,1536]{3,2,1,0:T(8,128)(2,1)}, u32[]{:S(2)}, u32[]{:S(2)}) collective-permute-start(bf16[2,2,256,1536]{3,2,1,0:T(8,128)(2,1)} %fusion.2), channel_id=1, source_target_pairs={{0,4},{4,0},{8,12},{12,8},{16,20},{20,16},{24,28},{28,24},{1,5},{5... | collective-permute-start | bytes 9437192 | tf_op jit(solution)/shard_map/ppermute | solution.py:55
  1019.7 59.8 %collective-permute-start.86 = (bf16[512,1024]{1,0:T(8,128)(2,1)S(1)}, bf16[512,1024]{1,0:T(8,128)(2,1)S(1)}, u32[]{:S(2)}, u32[]{:S(2)}) collective-permute-start(bf16[512,1024]{1,0:T(8,128)(2,1)S(1)} %copy-done.57), channel_id=1, source_target_pairs={{0,2},{1,3},{2,0},{3,1},{4,6},{5,7},{6,4},{7,5},{8,10},{9,11},{10,... | collective-permute-start | bytes 3145736 | tf_op jit(solution)/shard_map/ppermute | solution.py:58
  1020.5 87.6 %collective-permute-start.87 = (bf16[512,1024]{1,0:T(8,128)(2,1)S(1)}, bf16[512,1024]{1,0:T(8,128)(2,1)S(1)}, u32[]{:S(2)}, u32[]{:S(2)}) collective-permute-start(bf16[512,1024]{1,0:T(8,128)(2,1)S(1)} %copy-done.56), channel_id=1, source_target_pairs={{0,3},{1,0},{2,1},{3,2},{4,7},{5,4},{6,5},{7,6},{8,11},{9,8},{10,9... | collective-permute-start | bytes 3145736 | tf_op jit(solution)/shard_map/ppermute | solution.py:58
  (175 other events, 3473.0 us)

commit v3 on v2

v3 whole, which is shorter than its diff:
```python
import functools

import jax
import jax.numpy as jnp
from jax import lax
from jax.experimental import pallas as pl
from jax.experimental.pallas import tpu as pltpu
from jax.sharding import PartitionSpec as P

HEADS = 16
EPS = 1e-05
THETA = 10000.0
ROUND_TOKENS = 2048
AXES = ("expert", "wshard")
LOW = jnp.bfloat16
F32 = jnp.float32


def rms_scale(values):
    return lax.rsqrt(jnp.mean(values * values, axis=-1, keepdims=True) + EPS)


def norm_back(values, scale, gain, grads, inner):
    weighted = gain * grads
    return scale * weighted - values * scale * scale * scale * inner


def dot(a, b, dims):
    return lax.dot_general(a, b, (dims, ((), ())), preferred_element_type=F32)


def mm(a, b):
    return dot(a, b, ((1,), (0,)))


def mm_t(a, b):
    return dot(a, b, ((1,), (1,)))


def t_mm(a, b):
    return dot(a, b, ((0,), (0,)))


def tie(x, *after):
    return lax.optimization_barrier((x, after))[0]


LIGHT = pl.CostEstimate(flops=1, bytes_accessed=1, transcendentals=0)


def turned(x, cos_ref, sin_ref, sign):
    return x * cos_ref[...] + sign * pltpu.roll(x, x.shape[1] // 2, 1) * sin_ref[...]


def attention_parts(q_ref, k_ref, v_ref, scale_ref, gain_ref, cos_ref, sin_ref, mask_ref):
    seq, head = cos_ref.shape
    raw_q = q_ref[:, 0].reshape(seq, head)
    raw_k = k_ref[:, 0].reshape(seq, head)
    values = v_ref[:, 0].reshape(seq, head).astype(LOW)
    scales = scale_ref[:, 0].reshape(seq, 2)
    hat_q = raw_q * scales[:, 0:1] * gain_ref[0:1, :]
    hat_k = raw_k * scales[:, 1:2] * gain_ref[1:2, :]
    queries = turned(hat_q, cos_ref, sin_ref, 1.0).astype(LOW)
    keys = turned(hat_k, cos_ref, sin_ref, 1.0).astype(LOW)
    scores = mm_t(queries, keys) * head ** (-0.5)
    scores = jnp.where(mask_ref[0] > 0, scores, -1e30)
    expo = jnp.exp(scores - jnp.max(scores, axis=-1, keepdims=True))
    probs = expo / jnp.sum(expo, axis=-1, keepdims=True)
    return raw_q, raw_k, values, scales, queries, keys, probs


def attention_kernel(*refs):
    out_ref = refs[-1]
    _, _, values, _, _, _, probs = attention_parts(*refs[:-1])
    out = mm(probs.astype(LOW), values).astype(LOW)
    out_ref[...] = out.reshape(out_ref.shape)


def attention_back_kernel(*refs):
    grad_ref, (dq_ref, dk_ref, dv_ref, inner_ref, gains_ref) = refs[8], refs[9:]
    gain_ref, cos_ref, sin_ref = refs[4:7]
    raw_q, raw_k, values, scales, queries, keys, probs = attention_parts(*refs[:8])
    seq, head = cos_ref.shape
    grad = grad_ref[:, 0].reshape(seq, head)
    dprobs = mm_t(grad, values)
    dscores = probs * (dprobs - jnp.sum(probs * dprobs, axis=-1, keepdims=True))
    dscores = dscores.astype(LOW)
    dq = turned(mm(dscores, keys) * head ** (-0.5), cos_ref, sin_ref, -1.0)
    dk = turned(t_mm(dscores, queries) * head ** (-0.5), cos_ref, sin_ref, -1.0)
    dv = t_mm(probs.astype(LOW), grad)
    dq_ref[...] = dq.reshape(dq_ref.shape)
    dk_ref[...] = dk.reshape(dk_ref.shape)
    dv_ref[...] = dv.astype(LOW).reshape(dv_ref.shape)
    inner_q = jnp.sum(raw_q * gain_ref[0:1, :] * dq, axis=-1, keepdims=True)
    inner_k = jnp.sum(raw_k * gain_ref[1:2, :] * dk, axis=-1, keepdims=True)
    inner_ref[...] = jnp.concatenate([inner_q, inner_k], 1).reshape(inner_ref.shape)
    gains_ref[0, 0:1, :] = jnp.sum(dq * raw_q * scales[:, 0:1], axis=0, keepdims=True)
    gains_ref[0, 1:2, :] = jnp.sum(dk * raw_k * scales[:, 1:2], axis=0, keepdims=True)


def attention_call(projected, scales, gains, cosine, sine, mask, grad=None):
    n_w, micro, rows, cols = projected.shape
    seq, head = cosine.shape
    cols = cols // 3
    heads = cols // head

    def part(p):
        return pl.BlockSpec((n_w, 1, rows, head), lambda m, h: (0, m, 0, p * heads + h))

    fixed = pl.BlockSpec((seq, head), lambda m, h: (0, 0))
    specs = [part(0), part(1), part(2)]
    specs.append(pl.BlockSpec((n_w, 1, rows, 2), lambda m, h: (0, m, 0, 0)))
    specs.append(pl.BlockSpec((2, head), lambda m, h: (0, h)))
    specs += [fixed, fixed, pl.BlockSpec((1, seq, seq), lambda m, h: (m, 0, 0))]
    ins = [projected] * 3 + [scales, gains, cosine, sine, mask]

    def like(kind):
        return jax.ShapeDtypeStruct((n_w, micro, rows, cols), kind)

    if grad is None:
        kernel, outs, out_specs = attention_kernel, like(LOW), part(0)
    else:
        ins, specs = ins + [grad], specs + [part(0)]
        kernel = attention_back_kernel
        outs = [
            like(F32),
            like(F32),
            like(LOW),
            jax.ShapeDtypeStruct((heads, n_w, micro, rows, 2), F32),
            jax.ShapeDtypeStruct((micro, 2, cols), F32),
        ]
        out_specs = [part(0)] * 3 + [
            pl.BlockSpec((1, n_w, 1, rows, 2), lambda m, h: (h, 0, m, 0, 0)),
            pl.BlockSpec((1, 2, head), lambda m, h: (m, 0, h)),
        ]
    return pl.pallas_call(
        kernel,
        grid=(micro, heads),
        in_specs=specs,
        out_specs=out_specs,
        out_shape=outs,
        compiler_params=pltpu.CompilerParams(vmem_limit_bytes=32 * 1024 * 1024),
        cost_estimate=LIGHT,
        name="attention" if grad is None else "attention_back",
    )(*ins)


def pack_kernel(at_ref, up_ref, down_ref, out_ref):
    step = pl.program_id(0)

    @pl.when(step < 2)
    def _():
        out_ref[...] = up_ref[0]

    @pl.when(step == 2)
    def _():
        out_ref[...] = down_ref[0]


def pack_half(t, w_gate_up, w_down, halves):
    rows = w_gate_up.shape[1]
    hidden = w_down.shape[1] // halves
    cols = w_down.shape[2]

    def up_at(i, at):
        return (at[0] // halves, 0, jnp.minimum(i, 1) * halves + at[0] % halves)

    def down_at(i, at):
        return (at[0] // halves, at[0] % halves, 0)

    return pl.pallas_call(
        pack_kernel,
        grid_spec=pltpu.PrefetchScalarGridSpec(
            num_scalar_prefetch=1,
            grid=(3,),
            in_specs=[
                pl.BlockSpec((1, rows, hidden), up_at),
                pl.BlockSpec((1, hidden, cols), down_at),
            ],
            out_specs=pl.BlockSpec((rows, hidden), lambda i, at: (0, i)),
        ),
        out_shape=jax.ShapeDtypeStruct((rows, 3 * hidden), LOW),
        name="pack",
    )(t.reshape(1), w_gate_up, w_down)


def unpack_kernel(n_w, shard_ref, *refs):
    pieces, (up_ref, down_ref) = refs[:n_w], refs[n_w:]
    halves, hidden = down_ref.shape[1], pieces[0].shape[1] // 3
    units = halves * hidden
    for s in range(n_w):
        t = lax.rem(shard_ref[0] - s + n_w, n_w)
        j, h = lax.div(t, halves), lax.rem(t, halves)
        for part in range(2):
            at = pl.multiple_of(part * units + h * hidden, 128)
            piece = pieces[s][:, part * hidden : (part + 1) * hidden]
            up_ref[j, :, pl.ds(at, hidden)] = piece.astype(F32)
        down_ref[j, h] = pieces[s][:, 2 * hidden :].astype(F32)


def unpack(pieces, shard, experts):
    n_w = len(pieces)
    rows, hidden = pieces[0].shape[0], pieces[0].shape[1] // 3
    halves = n_w // experts
    cols = hidden
    tile = min(128, rows)
    up, down = pl.pallas_call(
        functools.partial(unpack_kernel, n_w),
        grid_spec=pltpu.PrefetchScalarGridSpec(
            num_scalar_prefetch=1,
            grid=(rows // tile,),
            in_specs=[pl.BlockSpec((tile, 3 * hidden), lambda i, at: (i, 0))] * n_w,
            out_specs=[
                pl.BlockSpec((experts, tile, 2 * halves * hidden), lambda i, at: (0, i, 0)),
                pl.BlockSpec((experts, halves, tile, cols), lambda i, at: (0, 0, i, 0)),
            ],
        ),
        out_shape=[
            jax.ShapeDtypeStruct((experts, rows, 2 * halves * hidden), F32),
            jax.ShapeDtypeStruct((experts, halves, hidden, cols), F32),
        ],
        compiler_params=pltpu.CompilerParams(vmem_limit_bytes=32 * 1024 * 1024),
        name="unpack",
    )(shard.reshape(1), *pieces)
    return up, down.reshape(experts, halves * hidden, cols)


def expert_kernel(experts, n_w, at_ref, place_ref, x_ref, dy_all_ref, used_ref, hot_ref, *refs):
    router_ref, back_router_ref, refs = refs[0], refs[1], refs[2:]
    packs, refs = (refs[:n_w], refs[n_w : 2 * n_w]), refs[2 * n_w :]
    mix_ref, back_ref, dy_ref, dlogits_ref = refs[:4]
    dgu_refs, gated_refs = refs[4:6], refs[6:8]
    dy_ref[...] = dy_all_ref[...].reshape(dy_ref.shape)
    hidden = packs[0][0].shape[1] // 3
    cols = packs[0][0].shape[0]
    spans = [pl.ds(pl.multiple_of(at_ref[s] * cols, 128), cols) for s in range(n_w)]
    lane = lax.broadcasted_iota(jnp.int32, (1, router_ref.shape[1]), 1)
    logits = jnp.where(lane < experts, mm(x_ref[...], router_ref[...]), -1e30)
    expo = jnp.exp(logits - jnp.max(logits, axis=-1, keepdims=True))
    gate_all = expo / jnp.sum(expo, axis=-1, keepdims=True)
    used = gate_all * used_ref[...].astype(F32)
    dlogits = jnp.zeros_like(gate_all)
    for h in range(2):
        hot = hot_ref[h : h + 1, :]
        gate = jnp.sum(used * hot, axis=-1, keepdims=True)
        g = u = lifted = 0.0
        for s in range(n_w):
            g = g + mm(x_ref[:, spans[s]], packs[h][s][:, :hidden])
            u = u + mm(x_ref[:, spans[s]], packs[h][s][:, hidden : 2 * hidden])
            lifted = lifted + mm_t(dy_ref[:, spans[s]], packs[h][s][:, 2 * hidden :])
        sigma = jax.nn.sigmoid(g)
        silu = g * sigma
        act = (silu * u).astype(LOW).astype(F32)
        dgate = jnp.sum(act * lifted, axis=-1, keepdims=True)
        gated_refs[h][...] = (act * gate).astype(LOW)
        dact = lifted * gate
        dgu_refs[h][:, :hidden] = (dact * u * (sigma * (1.0 + g * (1.0 - sigma)))).astype(LOW)
        dgu_refs[h][:, hidden:] = (dact * silu).astype(LOW)
        dlogits = dlogits + dgate * gate * (hot - gate_all)
    dlogits = dlogits.astype(LOW)
    dlogits_ref[...] = dlogits
    for s in range(n_w):
        back = mm_t(dgu_refs[0][...], packs[0][s][:, : 2 * hidden])
        back = back + mm_t(dgu_refs[1][...], packs[1][s][:, : 2 * hidden])
        back = back + mm(dlogits, back_router_ref[:, spans[s]])
        back_ref[:, spans[s]] = back.astype(LOW)
    for s in range(n_w):
        mix = mm(gated_refs[0][...], packs[0][s][:, 2 * hidden :])
        mix = mix + mm(gated_refs[1][...], packs[1][s][:, 2 * hidden :])
        mix_ref[:, spans[s]] = mix.astype(LOW)


def expert_pass(x, dy, rows, used, hots, router, packs, at, place, experts):
    n, width = x.shape
    n_w = len(packs[0])
    tile = 2 * rows
    cols, hidden = packs[0][0].shape[0], packs[0][0].shape[1] // 3
    lanes = used.shape[1]

    def tiled(cols):
        return pl.BlockSpec((tile, cols), lambda i, at, place: (i, 0))

    def placed(cols):
        return pl.BlockSpec((tile, cols), lambda i, at, place: (place[i], 0))

    def fixed(shape):
        return pl.BlockSpec(shape, lambda i, at, place: (0, 0), pipeline_mode=pl.Buffered(1))

    router = jnp.pad(router, ((0, 0), (0, lanes - experts)))
    outs = [width, width, width, lanes, 2 * hidden, 2 * hidden, hidden, hidden]
    return pl.pallas_call(
        functools.partial(expert_kernel, experts, n_w),
        grid_spec=pltpu.PrefetchScalarGridSpec(
            num_scalar_prefetch=2,
            grid=(n // tile,),
            in_specs=[
                tiled(width),
                pl.BlockSpec((2, rows, width), lambda i, at, place: (place[i], 0, 0)),
                placed(lanes),
            ]
            + [fixed((2, lanes)), fixed((width, lanes)), fixed((lanes, width))]
            + [fixed((cols, 3 * hidden))] * (2 * n_w),
            out_specs=[placed(width)] + [tiled(c) for c in outs[1:]],
        ),
        out_shape=[jax.ShapeDtypeStruct((n, c), LOW) for c in outs],
        compiler_params=pltpu.CompilerParams(vmem_limit_bytes=56 * 1024 * 1024),
        cost_estimate=LIGHT,
        name="expert_pass",
    )(at, place, x, dy, used, hots, router, router.T, *packs[0], *packs[1])


def grad_kernel(shard_ref, x_ref, dy_ref, dgu_ref, gated_ref, *refs):
    out_ref = refs[-1]
    hidden = gated_ref.shape[1]
    if len(refs) > 1:
        dlogits_ref, out_ref, router_ref = refs
        router_ref[...] = t_mm(x_ref[...], dlogits_ref[...])
    out_ref[0, :, : 2 * hidden] = t_mm(x_ref[...], dgu_ref[...]).astype(out_ref.dtype)
    out_ref[0, :, 2 * hidden :] = t_mm(gated_ref[...], dy_ref[...]).astype(out_ref.dtype)


def grad_pass(x, dy, dgu, gated, dlogits, shard, n_w, kind):
    n, width = x.shape
    hidden = gated.shape[1]
    cols = width // n_w

    def fixed(a):
        return pl.BlockSpec(a.shape, lambda i, at: (0, 0), pipeline_mode=pl.Buffered(1))

    column = pl.BlockSpec((n, cols), lambda i, at: (0, lax.rem(at[0] + i, n_w)))
    ins, specs = [x, dy, dgu, gated], [column, column, fixed(dgu), fixed(gated)]
    out_specs = [pl.BlockSpec((1, cols, 3 * hidden), lambda i, at: (i, 0, 0))]
    outs = [jax.ShapeDtypeStruct((n_w, cols, 3 * hidden), kind)]
    if dlogits is not None:
        lanes = dlogits.shape[1]
        ins, specs = ins + [dlogits], specs + [fixed(dlogits)]
        out_specs.append(pl.BlockSpec((cols, lanes), lambda i, at: (lax.rem(at[0] + i, n_w), 0)))
        outs.append(jax.ShapeDtypeStruct((width, lanes), F32))
    return tuple(
        pl.pallas_call(
            grad_kernel,
            grid_spec=pltpu.PrefetchScalarGridSpec(
                num_scalar_prefetch=1, grid=(n_w,), in_specs=specs, out_specs=out_specs
            ),
            out_shape=outs,
            compiler_params=pltpu.CompilerParams(vmem_limit_bytes=56 * 1024 * 1024),
            cost_estimate=LIGHT,
            name="grad_pass",
        )(shard.reshape(1), *ins)
    )


def build(n_e, n_w):
    bits = [1 << b for b in range(n_e.bit_length() - 1)]
    plane = bits[1:]
    nd = len(plane)

    def swap(x, d):
        return lax.ppermute(x, "expert", [(i, i ^ d) for i in range(n_e)])

    def shift(x, s):
        return lax.ppermute(x, "wshard", [(j, (j + s) % n_w) for j in range(n_w)])

    def joint(x, pairs):
        return lax.ppermute(x, AXES, pairs)

    def line_gather(x):
        return [x] + [shift(x, n_w - r) for r in range(1, n_w)]

    def line_scatter(blocks):
        total = blocks[0].astype(F32)
        for r in range(1, n_w):
            total = total + shift(blocks[r], r).astype(F32)
        return total

    def across(x, r):
        return lax.ppermute(x, "wshard", [(j, j ^ r) for j in range(n_w)])

    def pair_parts(x, shard):
        odd = shard % 2 == 1
        blocks = [x] + [across(x, r) for r in range(1, n_w)]
        parts = []
        for a, b in zip(blocks[::2], blocks[1::2]):
            parts.append(jnp.concatenate([jnp.where(odd, b, a), jnp.where(odd, a, b)], 0))
        return parts

    def pair_scatter(parts, shard):
        odd = shard % 2 == 1
        total = 0.0
        for p, part in enumerate(parts):
            a, b = jnp.split(part, 2, 0)
            for r, block in ((2 * p, jnp.where(odd, b, a)), (2 * p + 1, jnp.where(odd, a, b))):
                total = total + (across(block, r) if r else block).astype(F32)
        return total

    def line_exchange(send, shard, order=None):
        got = {0: send(shard)}
        last = None
        for s in order or range(1, n_w):
            x = send((shard + s) % n_w)
            if order and last is not None:
                x = tie(x, last)
            last = got[s] = shift(x, s)
        out = jnp.zeros((n_w,) + got[0].shape, got[0].dtype)
        for s in range(n_w):
            out = lax.dynamic_update_index_in_dim(out, got[s], (shard - s + n_w) % n_w, 0)
        return out

    def line_sum(x, shard):
        x = jnp.roll(x.reshape(2, n_w, -1), shard, axis=1)
        total = x
        for s in range(1, n_w):
            total = total + shift(x, s)
        return jnp.roll(total, -shard, axis=1)

    def way(p, step):
        return plane[(step + p * nd // 2) % nd]

    def plane_gather(parts):
        held = [([0], x) for x in parts]
        groups = [held]
        for step in range(nd):
            got = []
            for p, (masks, x) in enumerate(held):
                got.append(([m | way(p, step) for m in masks], swap(x, way(p, step))))
            groups.append(got)
            held = [
                (a[0] + b[0], jnp.concatenate([a[1], b[1]], 0)) if step + 1 < nd else None
                for a, b in zip(held, got)
            ]
        return groups

    def plane_scatter(groups, beside):
        mine = [[group[p] for group in groups] for p in range(2)]
        for step in reversed(range(nd)):
            got = [swap(mine[p][step + 1], way(p, step)) for p in range(2)]
            if beside is not None:
                got, beside = tie(got, beside), None
            for p in range(2):
                at = 0
                for low in range(step + 1):
                    n = mine[p][low].shape[0]
                    total = mine[p][low].astype(F32) + got[p][at : at + n].astype(F32)
                    mine[p][low] = total.astype(LOW)
                    at += n
            mine = lax.optimization_barrier([m[: step + 1] for m in mine])
        return [m[0] for m in mine]

    def hyper_scatter(x, me, kind, cut=1):
        def halve(x, left, d):
            at = left.index(d)
            bit = (me // d) % 2
            send = lax.dynamic_index_in_dim(x, 1 - bit, at, keepdims=False).astype(kind)
            keep = lax.dynamic_index_in_dim(x, bit, at, keepdims=False)
            return (keep.astype(F32) + swap(send, d).astype(F32)).astype(kind)

        x = x.reshape((2,) * len(bits) + x.shape[1:])
        x = halve(x, list(reversed(bits)), 1)
        parts = []
        for p, part in enumerate(jnp.split(x, cut, -1)):
            left = list(reversed(plane))
            for d in plane[p:] + plane[:p]:
                part = halve(part, left, d)
                left.remove(d)
            parts.append(part)
        return jnp.concatenate(parts, -1)

    def local(
        hidden_in,
        doc_ids,
        routes,
        attn_gain,
        q_gain,
        k_gain,
        ffn_gain,
        w_qkv,
        w_out,
        w_router,
        w_gate_up,
        w_down,
        cotangent,
    ):
        micro = hidden_in.shape[0]
        rows = hidden_in.shape[2]
        width = hidden_in.shape[3]
        heads = HEADS
        head = width // heads
        my_heads = heads // n_w
        cols = width // n_w
        experts = w_router.shape[1]
        local_experts = w_gate_up.shape[0]
        units = w_down.shape[1]
        own = micro * rows
        seq = n_w * rows
        me = lax.axis_index("expert")
        shard = lax.axis_index("wshard")
        scale = head ** (-0.5)

        piece = width // n_w // n_e
        mine = lax.dynamic_slice_in_dim(w_qkv, me * piece, piece, 0)
        mine = mine.reshape(piece, 3, n_w, cols).transpose(2, 0, 1, 3).reshape(n_w, piece, 3 * cols)
        bank = line_exchange(
            lambda t: lax.dynamic_index_in_dim(mine, t, 0, keepdims=False), shard
        )
        upstream = cotangent.reshape(own, width)
        tokens = hidden_in.reshape(own, width).astype(F32)
        scale_one = rms_scale(tokens)
        normed = (tokens * scale_one * attn_gain).astype(LOW)
        used = jnp.any(
            routes.reshape(own, -1, 1) == jnp.arange(experts, dtype=jnp.int32), axis=1
        ).astype(LOW)
        blocks = line_gather(normed)
        blocks, bank = lax.optimization_barrier((blocks, bank))
        normed_all = jnp.concatenate(blocks, 0)

        half = piece // 2
        w_heads = []
        for p in range(2):
            held = bank[:, p * half : (p + 1) * half]
            dims = plane[p:] + plane[:p] + [1]
            for d in dims:
                got, upper = swap(held, d), (me // d) % 2 == 1
                held = jnp.stack([jnp.where(upper, got, held), jnp.where(upper, held, got)])
            at = {d: len(dims) - 1 - k for k, d in enumerate(dims)}
            k = len(dims)
            w_heads.append(held.transpose(k, *[at[d] for d in reversed(bits)], k + 1, k + 2))
        w_heads = jnp.stack(w_heads, 1 + len(bits)).reshape(width, 3 * cols)

        rounds = max(1, n_e * n_w * own // 2 // ROUND_TOKENS)
        step = own // rounds
        hidden = units * local_experts // n_w
        arrived = (shard - jnp.arange(n_w, dtype=jnp.int32) + n_w) % n_w

        def pack_for(t):
            return pack_half(t, w_gate_up, w_down, n_w // local_experts)

        pairs = [
            [(2 * c + k) * n_w + w for c in range(n_e // 2) for w in range(n_w)] for k in range(2)
        ]
        router_rows = w_router.size // width
        used_rows = step * experts // width

        def to_pairs(at):
            rows = [upstream[at : at + step], used[at : at + step].reshape(-1, width)]
            rows.append(w_router.reshape(-1, width))
            rows = jnp.concatenate(rows, 0)
            rows = jnp.pad(rows, ((0, -rows.shape[0] % 16), (0, 0)))
            return lax.all_gather(tie(rows, blocks), AXES, axis_index_groups=pairs)

        dy_all = to_pairs(0)
        pieces = [tie(pack_for((shard + k) % n_w), blocks) for k in range(n_w)]
        pieces = [pieces[k] if k in (0, 2) else shift(pieces[k], k) for k in range(n_w)]

        projected = mm(normed_all, w_heads)
        squares = jnp.sum(projected.reshape(-1, 3, cols)[:, :2] ** 2, axis=-1).T
        scales = lax.rsqrt(line_sum(squares, shard) / width + EPS)
        scales = scales.reshape(2, -1).T
        projected = projected.reshape(n_w, micro, rows, 3 * cols)
        gains = [lax.dynamic_slice_in_dim(g, shard * cols, cols) for g in (q_gain, k_gain)]
        gains = jnp.stack(gains)
        block_at = (shard + jnp.arange(n_w, dtype=jnp.int32)) % n_w
        positions = block_at[:, None] * rows + jnp.arange(rows, dtype=jnp.int32)[None, :]
        positions = positions.reshape(seq)
        freq = THETA ** (-(jnp.arange(head // 2, dtype=F32) * 2.0 / head))
        angle = positions.astype(F32)[:, None] * freq
        cosine, sine = jnp.cos(angle), jnp.sin(angle)
        cosine = jnp.concatenate([cosine, cosine], 1)
        sine = jnp.concatenate([-sine, sine], 1)
        docs = jnp.take(doc_ids[:, 0], positions, axis=1)
        mask = (positions[None, :] <= positions[:, None])[None] & (
            docs[:, :, None] == docs[:, None, :]
        )
        mask = mask.astype(F32)
        attention = functools.partial(
            attention_call,
            projected,
            scales.reshape(n_w, micro, rows, 2),
            gains,
            cosine,
            sine,
            mask,
        )
        attended = attention().reshape(n_w * own, cols)
        branch = mm(attended, w_out).astype(LOW)
        pieces = [p if k in (0, 2) else tie(p, branch) for k, p in enumerate(pieces)]
        branch = branch.reshape(n_w, own, width)
        resid = tokens + line_scatter([branch[r] for r in range(n_w)])

        scale_two = rms_scale(resid)
        ffn_in = (resid * scale_two * ffn_gain).astype(LOW)
        lanes = -(-experts // 128) * 128
        expert_at = jnp.arange(lanes, dtype=jnp.int32)
        my_expert = local_experts * me + shard * local_experts // n_w
        sib_expert = local_experts * jnp.bitwise_xor(me, 1) + shard * local_experts // n_w
        hots = jnp.stack([(expert_at == e).astype(F32) for e in (my_expert, sib_expert)])

        def whole(groups):
            return jnp.concatenate([b for group in groups for _, b in group], 0)

        dffn, mixture = [], []
        grads = None
        for n in range(rounds):
            at = n * step
            ffn_rows = ffn_in[at : at + step]
            if n:
                ffn_rows, grads, dffn, mixture = lax.optimization_barrier(
                    (ffn_rows, grads, dffn, mixture)
                )
                dy_all = to_pairs(at)
            parts = pair_parts(ffn_rows, shard)
            groups = plane_gather(parts)
            x = whole(groups)
            place = [
                jnp.bitwise_xor(me // 2, m // 2) * (n_w // 2) + jnp.bitwise_xor(shard // 2, p)
                for group in groups
                for p in range(2)
                for m in group[p][0]
            ]
            mask = dy_all[:, step : step + used_rows].reshape(-1, experts)
            mask = jnp.pad(mask, ((0, 0), (0, lanes - experts)))
            router = dy_all[:n_w, step + used_rows : step + used_rows + router_rows]
            router = router.reshape(width, experts)
            if n == 0:
                pieces[2] = tie(shift(tie(pieces[2], parts), 2), x)
                siblings = [swap(tie(piece, parts), 1) for piece in pieces]
                packs = [pieces, siblings]
            mix, back, dy, dlogits, dgu0, dgu1, gated0, gated1 = expert_pass(
                x, dy_all, step, mask, hots, router, packs, arrived, jnp.stack(place), experts
            )
            cuts = []
            for group in groups:
                for p in range(2):
                    cuts.append((cuts[-1] if cuts else 0) + group[p][1].shape[0])
            back = jnp.split(back, cuts[:-1], 0)
            back = [back[2 * g : 2 * g + 2] for g in range(nd + 1)]
            kind = LOW if rounds == 1 else F32
            grad_sib, grad_router = grad_pass(x, dy, dgu1, gated1, dlogits, shard, n_w, kind)
            (grad_own,) = grad_pass(x, dy, dgu0, gated0, None, shard, n_w, kind)
            if grads is not None:
                grad_sib, grad_router, grad_own = jax.tree.map(
                    jnp.add, grads, (grad_sib, grad_router, grad_own)
                )
            grads = (grad_sib, grad_router, grad_own)
            beside = grads
            if n == rounds - 1:
                grad_sib = swap(grad_sib.astype(LOW), 1)
                sums = [
                    (grad_own[s].astype(F32) + grad_sib[s].astype(F32)).astype(LOW)
                    for s in range(n_w)
                ]
                beside = sums
            back = plane_scatter(back, beside)
            if n == rounds - 1:
                sums[1], sums[3] = shift(sums[1], 1), shift(sums[3], 3)
                back = tie(back, sums[1])
            dffn.append(pair_scatter(back, shard))
            if n == rounds - 1:
                dffn = tie(dffn, sums[3])
            same = [[2 * c + k for c in range(n_e // 2)] for k in range(2)]
            mixture.append(
                lax.psum_scatter(tie(mix, back), "expert", axis_index_groups=same, tiled=True)
            )
        dffn = jnp.concatenate(dffn, 0)
        grad_router = grad_router[:, :experts]

        upstream = upstream.astype(F32)
        weighted = ffn_gain * dffn
        inner = jnp.mean(resid * weighted, axis=-1, keepdims=True)
        dresid = upstream + norm_back(resid, scale_two, ffn_gain, dffn, inner)
        grad_ffn_gain = jnp.sum(dffn * resid * scale_two, axis=0)
        dbranch = jnp.concatenate(line_gather(dresid.astype(LOW)), 0)
        sums[2] = shift(tie(sums[2], dbranch), 2)
        mixture = [
            lax.psum_scatter(tie(m, dbranch), "wshard", tiled=True).astype(F32) for m in mixture
        ]
        grad_out = t_mm(attended, dbranch)
        dattended = mm_t(dbranch, w_out).astype(LOW)
        dq, dk, dv, inners, grad_gains = attention(dattended.reshape(n_w, micro, rows, cols))
        inners = line_sum(jnp.sum(inners, 0).reshape(-1, 2).T, shard) / width
        inners = inners.reshape(2, -1).T
        flat = projected.reshape(-1, 3 * cols)
        dproj = jnp.concatenate(
            [
                norm_back(
                    flat[:, p * cols : (p + 1) * cols],
                    scales[:, p : p + 1],
                    gains[p],
                    d.reshape(-1, cols),
                    inners[:, p : p + 1],
                ).astype(LOW)
                for p, d in enumerate((dq, dk))
            ]
            + [dv.reshape(-1, cols)],
            1,
        )
        dnormed = tie(mm_t(dproj, w_heads).astype(LOW), sums[2])
        dnormed = dnormed.reshape(n_w, own, width)
        dnormed = line_scatter([dnormed[r] for r in range(n_w)])
        inner = jnp.mean(tokens * (attn_gain * dnormed), axis=-1, keepdims=True)
        dx = norm_back(tokens, scale_one, attn_gain, dnormed, inner)
        grad_in = (dresid + dx).astype(LOW)
        mixture = jnp.concatenate(mixture, 0)
        hidden_out = (resid + mixture).astype(LOW)
        out_gate_up, out_down = unpack(sums, shard, local_experts)
        grad_qkv = t_mm(normed_all, dproj)
        grad_attn_gain = jnp.sum(grad_qkv * w_heads.astype(F32), axis=1) / attn_gain

        small = width // (n_e * n_w)
        qkv = hyper_scatter(grad_qkv.reshape(n_e, n_w * small, 3 * cols), me, LOW, nd)
        qkv_rows = qkv.reshape(n_w, small, 3 * cols)
        qkv = line_exchange(
            lambda t: lax.dynamic_index_in_dim(qkv_rows, t, 0, keepdims=False), shard
        )
        qkv = qkv.reshape(n_w, small, 3, cols).transpose(1, 2, 0, 3)
        out_qkv = qkv.reshape(small, 3 * width).astype(F32)
        to_rows = [
            (i * n_w + w, w * n_e + i) for i in range(n_e) for w in range(n_w)
        ]
        out_rows = hyper_scatter(grad_out.reshape(n_e, small, width), me, LOW)
        out_rows = joint(out_rows, to_rows).astype(F32)
        def all_scatter(x):
            x = x.reshape(-1, n_e, n_w * small).transpose(1, 0, 2)
            x = hyper_scatter(x, me, F32).reshape(-1, n_w, small)
            total = lax.dynamic_index_in_dim(x, shard, 1, keepdims=False)
            for s in range(1, n_w):
                send = lax.dynamic_index_in_dim(x, (shard + s) % n_w, 1, keepdims=False)
                total = total + shift(send, s)
            return total

        gains = jnp.zeros((2, width), F32)
        gains = lax.dynamic_update_slice(gains, jnp.sum(grad_gains, 0), (0, shard * cols))
        pack = [gains, grad_attn_gain[None], grad_ffn_gain[None], grad_router.T]
        pack = all_scatter(jnp.concatenate(pack, 0))
        return (
            hidden_out.reshape(micro, 1, rows, width),
            grad_in.reshape(micro, 1, rows, width),
            pack[2],
            pack[0],
            pack[1],
            pack[3],
            out_qkv,
            out_rows,
            pack[4:].T,
            out_gate_up,
            out_down,
        )

    return local


def solution(mesh):
    in_specs = (
        P(None, "expert", "wshard", None),
        P(None, "expert", None),
        P(None, "expert", "wshard", None),
        P(),
        P(),
        P(),
        P(),
        P("wshard", None),
        P("wshard", None),
        P("wshard", None),
        P("expert", "wshard", None),
        P("expert", None, "wshard"),
        P(None, "expert", "wshard", None),
    )
    out_specs = (
        P(None, "expert", "wshard", None),
        P(None, "expert", "wshard", None),
        P(("expert", "wshard")),
        P(("expert", "wshard")),
        P(("expert", "wshard")),
        P(("expert", "wshard")),
        P(("expert", "wshard"), None),
        P(("expert", "wshard"), None),
        P(("expert", "wshard"), None),
        P("expert", "wshard", None),
        P("expert", None, "wshard"),
    )
    local = build(mesh.shape["expert"], mesh.shape["wshard"])
    return jax.shard_map(local, mesh=mesh, in_specs=in_specs, out_specs=out_specs, check_vma=False)
```

time: 1170 us -> 1070 us (0.915)
  matrix products: 228 us -> 30.5 us
  Pallas kernels: 0 us -> 147 us
  local copies, waits for them, and re-layouts: 237 us -> 102 us
  starting transfers between devices: 117 us -> 207 us
  waiting for transfers between devices: 418 us -> 483 us
  blocking collectives: 53.2 us -> 0 us
  other arithmetic: 99.3 us -> 73.6 us
  between operations: 2.99 us -> 15.8 us
    dot_general x51 -> x6, matrix products: 216 us -> 30.5 us  [dot(): return lax.dot_general(a, b, (dims, ((), ())), preferred_element_type=F32)]
    pallas_call x0 -> x10, Pallas kernels: none -> 147 us  [the longest x1 69.7 us: expert_pass(): pl.pallas_call(functools.partial(expert_kernel, experts, n_w), grid_spec=...]
    ppermute x0 -> x6, waiting for transfers between devices: none -> 102 us  [across(): return lax.ppermute(x, 'wshard', [(j, j ^ r) for j in range(n_w)])]
    ppermute x42 -> x30, waiting for transfers between devices: 148 us -> 86.9 us  [swap(): return lax.ppermute(x, 'expert', [(i, i ^ d) for i in range(n_e)])]
    psum x2 -> x0, blocking collectives: 53.2 us -> none  [line_sum(): return jnp.roll(lax.psum(x, 'wshard'), -shard, axis=1)]
    ppermute x48 -> x33, starting transfers between devices: 61.1 us -> 114 us  [shift(): return lax.ppermute(x, 'wshard', [(j, (j + s) % n_w) for j in range(n_w)])]
    ppermute x0 -> x6, starting transfers between devices: none -> 32.2 us  [across(): return lax.ppermute(x, 'wshard', [(j, j ^ r) for j in range(n_w)])]
    dynamic_update_slice x37 -> x7, local copies, waits for them, and re-layouts: 31.9 us -> 0.11 us  [the longest x6 0.1 us: line_exchange(): lax.dynamic_update_index_in_dim(out, got[s], (shard - s + n_w) % n_w, 0)]
  transfers between devices with their start and end apart: 92 -> 73, of which waited for: 32 -> 32; matrix products, arithmetic and copies ran while one was open for 43% -> 17% of each run, Pallas kernels for 0% -> 5%
where the time goes in v3:
time: 1070 us; the launch traced here: 1060 us
  waiting for transfers between devices  483 us (45%)
  starting transfers between devices  207 us (19%)
  Pallas kernels  147 us (14%)
  local copies, waits for them, and re-layouts  102 us (10%)
  other arithmetic  73.6 us (7%)
  matrix products  30.5 us (3%)
  between operations  15.8 us (1%)
    ppermute x33, waiting for transfers between devices, shift(): return lax.ppermute(x, 'wshard', [(j, (j + s) % n_w) for j in range(n_w)])  294 us
    ppermute x33, starting transfers between devices, shift(): return lax.ppermute(x, 'wshard', [(j, (j + s) % n_w) for j in range(n_w)])  114 us
    ppermute x6, waiting for transfers between devices, across(): return lax.ppermute(x, 'wshard', [(j, j ^ r) for j in range(n_w)])  102 us
    ppermute x30, waiting for transfers between devices, swap(): return lax.ppermute(x, 'expert', [(i, i ^ d) for i in range(n_e)])  86.9 us
    pallas_call x1, Pallas kernels, expert_pass(): pl.pallas_call(functools.partial(expert_kernel, experts, n_w), grid_spec=...  69.7 us
    ppermute x30, starting transfers between devices, swap(): return lax.ppermute(x, 'expert', [(i, i ^ d) for i in range(n_e)])  60.2 us
    pallas_call x2, Pallas kernels, grad_pass(): pl.pallas_call(grad_kernel, grid_spec=pltpu.PrefetchScalarGridSpec(num_sc...  40.9 us
    ppermute x6, starting transfers between devices, across(): return lax.ppermute(x, 'wshard', [(j, j ^ r) for j in range(n_w)])  32.2 us
  transfers between devices with their start and end apart: 73, of which 32 were waited for; matrix products, arithmetic and copies ran while one was open for 17% of the time, Pallas kernels for 5%

profile of v3, /device:TPU:0, one launch (start us, length us, event | category | flops | bytes accessed | tf_op | source)
XLA Modules:
  0.0 1059.8 jit_solution(11711938541845406463)
XLA Ops:
  32.8 23.2 %collective-permute-done.3 = bf16[64,1536]{1,0:T(8,128)(2,1)S(1)} collective-permute-done((bf16[64,1536]{1,0:T(8,128)(2,1)}, bf16[64,1536]{1,0:T(8,128)(2,1)S(1)}, u32[]{:S(2)}, u32[]{:S(2)}) %collective-permute-start.3) | collective-permute-done | bytes 196640 | tf_op jit(solution)/shard_map/ppermute | solution.py:362
  57.5 16.0 %collective-permute-done.4 = bf16[64,1536]{1,0:T(8,128)(2,1)S(1)} collective-permute-done((bf16[64,1536]{1,0:T(8,128)(2,1)}, bf16[64,1536]{1,0:T(8,128)(2,1)S(1)}, u32[]{:S(2)}, u32[]{:S(2)}) %collective-permute-start.4) | collective-permute-done | bytes 196640 | tf_op jit(solution)/shard_map/ppermute | solution.py:362
  73.4 5.7 collective-permute-done.5
  98.0 14.4 %collective-permute-done.7 = bf16[2,4,32,1536]{3,2,1,0:T(8,128)(2,1)} collective-permute-done((bf16[2,4,32,1536]{3,2,1,0:T(8,128)(2,1)}, bf16[2,4,32,1536]{3,2,1,0:T(8,128)(2,1)}, u32[]{:S(2)}, u32[]{:S(2)}) %collective-permute-start.7) | collective-permute-done | bytes 786464 | tf_op jit(solution)/shard_map/ppermute | solution.py:359
  159.1 6.4 attention.1
  170.8 24.0 %collective-permute-done.15 = bf16[128,2048]{1,0:T(8,128)(2,1)S(1)} collective-permute-done((bf16[128,2048]{1,0:T(8,128)(2,1)S(1)}, bf16[128,2048]{1,0:T(8,128)(2,1)S(1)}, u32[]{:S(2)}, u32[]{:S(2)}) %collective-permute-start.15) | collective-permute-done | bytes 524320 | tf_op jit(solution)/shard_map/ppermute | solution.py:362
  194.8 36.2 %collective-permute-done.16 = bf16[128,2048]{1,0:T(8,128)(2,1)S(1)} collective-permute-done((bf16[128,2048]{1,0:T(8,128)(2,1)S(1)}, bf16[128,2048]{1,0:T(8,128)(2,1)S(1)}, u32[]{:S(2)}, u32[]{:S(2)}) %collective-permute-start.16) | collective-permute-done | bytes 524320 | tf_op jit(solution)/shard_map/ppermute | solution.py:362
  237.6 27.1 %collective-permute-start.18 = (bf16[128,2048]{1,0:T(8,128)(2,1)}, bf16[128,2048]{1,0:T(8,128)(2,1)}, u32[]{:S(2)}, u32[]{:S(2)}) collective-permute-start(bf16[128,2048]{1,0:T(8,128)(2,1)} %multiply_convert_fusion), channel_id=1, source_target_pairs={{0,1},{1,0},{2,3},{3,2},{4,5},{5,4},{6,7},{7,6},{8,9},{9,8},{10,11... | collective-permute-start | bytes 1572872 | tf_op jit(solution)/shard_map/ppermute | solution.py:377
  266.2 20.1 %collective-permute-done.18 = bf16[128,2048]{1,0:T(8,128)(2,1)} collective-permute-done((bf16[128,2048]{1,0:T(8,128)(2,1)}, bf16[128,2048]{1,0:T(8,128)(2,1)}, u32[]{:S(2)}, u32[]{:S(2)}) %collective-permute-start.18) | collective-permute-done | bytes 524320 | tf_op jit(solution)/shard_map/ppermute | solution.py:377
  292.0 19.2 %collective-permute-done.20 = bf16[128,2048]{1,0:T(8,128)(2,1)S(1)} collective-permute-done((bf16[128,2048]{1,0:T(8,128)(2,1)}, bf16[128,2048]{1,0:T(8,128)(2,1)S(1)}, u32[]{:S(2)}, u32[]{:S(2)}) %collective-permute-start.20) | collective-permute-done | bytes 524320 | tf_op jit(solution)/shard_map/ppermute | solution.py:377
  327.3 13.4 %collective-permute-done.22 = bf16[256,2048]{1,0:T(8,128)(2,1)} collective-permute-done((bf16[256,2048]{1,0:T(8,128)(2,1)}, bf16[256,2048]{1,0:T(8,128)(2,1)}, u32[]{:S(2)}, u32[]{:S(2)}) %collective-permute-start.22) | collective-permute-done | bytes 1048608 | tf_op jit(solution)/shard_map/ppermute | solution.py:359
  351.0 41.4 %collective-permute-done.27.refs_5_ = bf16[512,1536]{1,0:T(8,128)(2,1)} collective-permute-done((bf16[512,1536]{1,0:T(8,128)(2,1)}, bf16[512,1536]{1,0:T(8,128)(2,1)}, u32[]{:S(2)}, u32[]{:S(2)}) %collective-permute-start.27) | collective-permute-done | bytes 1572896 | tf_op jit(solution)/shard_map/ppermute | solution.py:362
  404.1 51.4 %collective-permute-done.26.refs_4_ = bf16[512,1536]{1,0:T(8,128)(2,1)} collective-permute-done((bf16[512,1536]{1,0:T(8,128)(2,1)}, bf16[512,1536]{1,0:T(8,128)(2,1)}, u32[]{:S(2)}, u32[]{:S(2)}) %collective-permute-start.26) | collective-permute-done | bytes 1572896 | tf_op jit(solution)/shard_map/ppermute | solution.py:362
  473.3 69.7 %expert_pass.1 = (bf16[2048,2048]{1,0:T(8,128)(2,1)}, bf16[2048,2048]{1,0:T(8,128)(2,1)}, bf16[2048,2048]{1,0:T(8,128)(2,1)}, bf16[2048,128]{1,0:T(8,128)(2,1)},...) custom-call(s32[4]{0:T(128)} %and_select_fusion.at_ref, ...), custom_call_target="tpu_custom_call" | custom-call | flops 1 | bytes 1 | tf_op jit(solution)/shard_map/expert_pass/pallas_call | solution.py:291
  543.0 21.8 %grad_pass.3 = (bf16[4,512,1536]{2,1,0:T(8,128)(2,1)}, f32[2048,128]{1,0:T(8,128)}) custom-call(s32[1]{0:T(128)} %bitcast.52.shard_ref, bf16[2048,2048]{1,0:T(8,128)(2,1)} %constant_dynamic-update-slice_fusion.4.x_ref, bf16[2048,2048]{1,0:T(8,128)(2,1)} %get-tuple-element.82.dy_ref, bf16[2048,1024]{1,0:T(8,128)(2,1)} %get-tuple-element.85.dgu_ref, ...), custom_call_target="tpu_custom_call" | custom-call | flops 1 | bytes 1 | tf_op jit(solution)/shard_map/grad_pass/pallas_call | solution.py:340
  573.0 19.1 %grad_pass.2 = bf16[4,512,1536]{2,1,0:T(8,128)(2,1)} custom-call(s32[1]{0:T(128)} %bitcast.52.shard_ref, bf16[2048,2048]{1,0:T(8,128)(2,1)} %constant_dynamic-update-slice_fusion.4.x_ref, bf16[2048,2048]{1,0:T(8,128)(2,1)} %get-tuple-element.82.dy_ref, bf16[2048,1024]{1,0:T(8,128)(2,1)} %get-tuple-element.83.dgu_ref, ...), custom_call_target="tpu_custom_call" | custom-call | flops 1 | bytes 1 | tf_op jit(solution)/shard_map/grad_pass/pallas_call | solution.py:340
  592.1 7.4 fusion.9
  599.5 18.4 %collective-permute-done.32 = bf16[512,2048]{1,0:T(8,128)(2,1)S(1)} collective-permute-done((bf16[512,2048]{1,0:T(8,128)(2,1)}, bf16[512,2048]{1,0:T(8,128)(2,1)S(1)}, u32[]{:S(2)}, u32[]{:S(2)}) %collective-permute-start.32) | collective-permute-done | bytes 2097184 | tf_op jit(solution)/shard_map/ppermute | solution.py:359
  627.3 18.8 %collective-permute-done.36 = bf16[256,2048]{1,0:T(8,128)(2,1)S(1)} collective-permute-done((bf16[256,2048]{1,0:T(8,128)(2,1)S(1)}, bf16[256,2048]{1,0:T(8,128)(2,1)S(1)}, u32[]{:S(2)}, u32[]{:S(2)}) %collective-permute-start.36) | collective-permute-done | bytes 1048608 | tf_op jit(solution)/shard_map/ppermute | solution.py:359
  648.9 14.1 %collective-permute-done.37.refs_1_ = bf16[512,1536]{1,0:T(8,128)(2,1)S(1)} collective-permute-done((bf16[512,1536]{1,0:T(8,128)(2,1)S(1)}, bf16[512,1536]{1,0:T(8,128)(2,1)S(1)}, u32[]{:S(2)}, u32[]{:S(2)}) %collective-permute-start.37) | collective-permute-done | bytes 1572896 | tf_op jit(solution)/shard_map/ppermute | solution.py:362
  670.9 63.0 %collective-permute-done.39 = bf16[128,2048]{1,0:T(8,128)(2,1)S(1)} collective-permute-done((bf16[128,2048]{1,0:T(8,128)(2,1)S(1)}, bf16[128,2048]{1,0:T(8,128)(2,1)S(1)}, u32[]{:S(2)}, u32[]{:S(2)}) %collective-permute-start.39) | collective-permute-done | bytes 524320 | tf_op jit(solution)/shard_map/ppermute | solution.py:377
  738.3 21.6 %collective-permute-start.43 = (bf16[128,2048]{1,0:T(8,128)(2,1)}, bf16[128,2048]{1,0:T(8,128)(2,1)}, u32[]{:S(2)}, u32[]{:S(2)}) collective-permute-start(bf16[128,2048]{1,0:T(8,128)(2,1)} %fusion.65), channel_id=1, source_target_pairs={{0,2},{1,3},{2,0},{3,1},{4,6},{5,7},{6,4},{7,5},{8,10},{9,11},{10,... | collective-permute-start | bytes 1572872 | tf_op jit(solution)/shard_map/ppermute | solution.py:362
  770.3 35.6 %collective-permute-done.43 = bf16[128,2048]{1,0:T(8,128)(2,1)} collective-permute-done((bf16[128,2048]{1,0:T(8,128)(2,1)}, bf16[128,2048]{1,0:T(8,128)(2,1)}, u32[]{:S(2)}, u32[]{:S(2)}) %collective-permute-start.43) | collective-permute-done | bytes 524320 | tf_op jit(solution)/shard_map/ppermute | solution.py:362
  808.9 12.7 %attention_back.1 = (f32[4,2,64,512]{3,2,1,0:T(8,128)S(1)}, f32[4,2,64,512]{3,2,1,0:T(8,128)S(1)}, bf16[4,2,64,512]{3,2,1,0:T(8,128)(2,1)S(1)}, f32[4,4,2,64,2]{4,3,2,1,0:T(8,128)S(1)}, f32[2,2,512]{2,1,0:T(2,128)S(1)}) custom-call(f32[4,2,64,1536]{3,2,1,0:T(8,128)S(1)} %bitcast.293, f32[4,2,64,1536]{3,2,1,0:T(8,128)S(1)} %bitcast.294, ...), custom_call_target="tpu_custom_call" | custom-call | flops 1 | bytes 1 | tf_op jit(solution)/shard_map/attention_back/pallas_call | solution.py:136
  839.9 8.8 multiply_reduce_fusion
  859.2 7.4 convolution_convert_fusion
  866.8 30.0 %collective-permute-start.55 = (f32[20,64]{1,0:T(8,128)S(1)}, f32[20,64]{1,0:T(8,128)S(1)}, u32[]{:S(2)}, u32[]{:S(2)}) collective-permute-start(f32[20,64]{1,0:T(8,128)S(1)} %bitcast.333), channel_id=1, source_target_pairs={{0,1},{1,2},{2,3},{3,0},{4,5},{5,6},{6,7},{7,4},{8,9},{9,10},{10,1... | collective-permute-start | bytes 15368 | tf_op jit(solution)/shard_map/ppermute | solution.py:362
  904.1 11.2 %collective-permute-done.67 = bf16[2,64,2048]{2,1,0:T(8,128)(2,1)S(1)} collective-permute-done((bf16[2,64,2048]{2,1,0:T(8,128)(2,1)S(1)}, bf16[2,64,2048]{2,1,0:T(8,128)(2,1)S(1)}, u32[]{:S(2)}, u32[]{:S(2)}) %collective-permute-start.67) | collective-permute-done | bytes 524320 | tf_op jit(solution)/shard_map/ppermute | solution.py:359
  936.4 6.0 unpack.1
  948.0 36.4 %collective-permute-start.60 = (bf16[256,768]{1,0:T(8,128)(2,1)S(1)}, bf16[256,768]{1,0:T(8,128)(2,1)S(1)}, u32[]{:S(2)}, u32[]{:S(2)}) collective-permute-start(bf16[256,768]{1,0:T(8,128)(2,1)S(1)} %dynamic-slice_bitcast_fusion.4), channel_id=1, source_target_pairs={{0,16},{4,20},{8,24},{12,28},{16,0},{20,4},{24,8},{28,12},{1,17},{... | collective-permute-start | bytes 1179656 | tf_op jit(solution)/shard_map/ppermute | solution.py:359
  984.8 25.7 %collective-permute-done.50 = bf16[128,2048]{1,0:T(8,128)(2,1)S(1)} collective-permute-done((bf16[128,2048]{1,0:T(8,128)(2,1)S(1)}, bf16[128,2048]{1,0:T(8,128)(2,1)S(1)}, u32[]{:S(2)}, u32[]{:S(2)}) %collective-permute-start.50) | collective-permute-done | bytes 524320 | tf_op jit(solution)/shard_map/ppermute | solution.py:362
  1012.9 14.5 %collective-permute-start.63 = (bf16[64,1536]{1,0:T(8,128)(2,1)S(1)}, bf16[64,1536]{1,0:T(8,128)(2,1)S(1)}, u32[]{:S(2)}, u32[]{:S(2)}) collective-permute-start(bf16[64,1536]{1,0:T(8,128)(2,1)S(1)} %get-tuple-element.228), channel_id=1, source_target_pairs={{0,1},{1,2},{2,3},{3,0},{4,5},{5,6},{6,7},{7,4},{8,9},{9,10},{10,1... | collective-permute-start | bytes 589832 | tf_op jit(solution)/shard_map/ppermute | solution.py:362
  (496 shorter events, 303.4 us)
Async XLA Ops:
  7.2 450.0 %all-gather.3.cloned.1.call-start = ((), (), s32[]{:S(2)}) async-start(), calls=%async_computation.4 | async-start | bytes 10027008 | tf_op jit(solution)/shard_map/all_gather | solution.py:548
  10.7 68.5 %collective-permute-start = (bf16[128,2048]{1,0:T(8,128)(2,1)}, bf16[128,2048]{1,0:T(8,128)(2,1)}, u32[]{:S(2)}, u32[]{:S(2)}) collective-permute-start(bf16[128,2048]{1,0:T(8,128)(2,1)} %fusion.32), channel_id=1, source_target_pairs={{0,3},{1,0},{2,1},{3,2},{4,7},{5,4},{6,5},{7,6},{8,11},{9,8},{10,9... | collective-permute-start | bytes 1572872 | tf_op jit(solution)/shard_map/ppermute | solution.py:362
  15.8 63.4 %collective-permute-start.1 = (bf16[128,2048]{1,0:T(8,128)(2,1)}, bf16[128,2048]{1,0:T(8,128)(2,1)}, u32[]{:S(2)}, u32[]{:S(2)}) collective-permute-start(bf16[128,2048]{1,0:T(8,128)(2,1)} %fusion.32), channel_id=1, source_target_pairs={{0,2},{1,3},{2,0},{3,1},{4,6},{5,7},{6,4},{7,5},{8,10},{9,11},{10,... | collective-permute-start | bytes 1572872 | tf_op jit(solution)/shard_map/ppermute | solution.py:362
  15.8 63.4 %collective-permute-start.2 = (bf16[128,2048]{1,0:T(8,128)(2,1)}, bf16[128,2048]{1,0:T(8,128)(2,1)}, u32[]{:S(2)}, u32[]{:S(2)}) collective-permute-start(bf16[128,2048]{1,0:T(8,128)(2,1)} %fusion.32), channel_id=1, source_target_pairs={{0,1},{1,2},{2,3},{3,0},{4,5},{5,6},{6,7},{7,4},{8,9},{9,10},{10,1... | collective-permute-start | bytes 1572872 | tf_op jit(solution)/shard_map/ppermute | solution.py:362
  97.3 829.8 %reduce-scatter.3.cloned.1.call-start = ((), (), s32[]{:S(2)}) async-start(), calls=%async_computation.2 | async-start | bytes 10485760 | tf_op jit(solution)/shard_map/reduce_scatter | solution.py:661
  167.0 63.9 %collective-permute-start.16 = (bf16[128,2048]{1,0:T(8,128)(2,1)S(1)}, bf16[128,2048]{1,0:T(8,128)(2,1)S(1)}, u32[]{:S(2)}, u32[]{:S(2)}) collective-permute-start(bf16[128,2048]{1,0:T(8,128)(2,1)S(1)} %get-tuple-element.213), channel_id=1, source_target_pairs={{0,2},{1,3},{2,0},{3,1},{4,6},{5,7},{6,4},{7,5},{8,10},{9,11},{10,... | collective-permute-start | bytes 1572872 | tf_op jit(solution)/shard_map/ppermute | solution.py:362
  169.7 65.3 %collective-permute-start.17 = (bf16[128,2048]{1,0:T(8,128)(2,1)S(1)}, bf16[128,2048]{1,0:T(8,128)(2,1)S(1)}, u32[]{:S(2)}, u32[]{:S(2)}) collective-permute-start(bf16[128,2048]{1,0:T(8,128)(2,1)S(1)} %get-tuple-element.212), channel_id=1, source_target_pairs={{0,3},{1,0},{2,1},{3,2},{4,7},{5,4},{6,5},{7,6},{8,11},{9,8},{10,9... | collective-permute-start | bytes 1572872 | tf_op jit(solution)/shard_map/ppermute | solution.py:362
  237.6 48.8 %collective-permute-start.18 = (bf16[128,2048]{1,0:T(8,128)(2,1)}, bf16[128,2048]{1,0:T(8,128)(2,1)}, u32[]{:S(2)}, u32[]{:S(2)}) collective-permute-start(bf16[128,2048]{1,0:T(8,128)(2,1)} %multiply_convert_fusion), channel_id=1, source_target_pairs={{0,1},{1,0},{2,3},{3,2},{4,5},{5,4},{6,7},{7,6},{8,9},{9,8},{10,11... | collective-permute-start | bytes 1572872 | tf_op jit(solution)/shard_map/ppermute | solution.py:377
  265.1 46.1 %collective-permute-start.20 = (bf16[128,2048]{1,0:T(8,128)(2,1)}, bf16[128,2048]{1,0:T(8,128)(2,1)S(1)}, u32[]{:S(2)}, u32[]{:S(2)}) collective-permute-start(bf16[128,2048]{1,0:T(8,128)(2,1)} %multiply_convert_fusion), channel_id=1, source_target_pairs={{0,2},{1,3},{2,0},{3,1},{4,6},{5,7},{6,4},{7,5},{8,10},{9,11},{10,... | collective-permute-start | bytes 1572872 | tf_op jit(solution)/shard_map/ppermute | solution.py:377
  321.6 70.8 %collective-permute-start.27 = (bf16[512,1536]{1,0:T(8,128)(2,1)}, bf16[512,1536]{1,0:T(8,128)(2,1)}, u32[]{:S(2)}, u32[]{:S(2)}) collective-permute-start(bf16[512,1536]{1,0:T(8,128)(2,1)} %pack.7), channel_id=1, source_target_pairs={{0,3},{1,0},{2,1},{3,2},{4,7},{5,4},{6,5},{7,6},{8,11},{9,8},{10,9... | collective-permute-start | bytes 4718600 | tf_op jit(solution)/shard_map/ppermute | solution.py:362
  326.3 71.5 %collective-permute-start.23 = (bf16[512,2048]{1,0:T(8,128)(2,1)}, bf16[512,2048]{1,0:T(8,128)(2,1)}, u32[]{:S(2)}, u32[]{:S(2)}) collective-permute-start(bf16[512,2048]{1,0:T(8,128)(2,1)} %pad_maximum_fusion.1), channel_id=1, source_target_pairs={{0,16},{4,20},{8,24},{12,28},{16,0},{20,4},{24,8},{28,12},{1,17},{... | collective-permute-start | bytes 6291464 | tf_op jit(solution)/shard_map/ppermute | solution.py:359
  326.5 66.1 %collective-permute-start.25 = (bf16[512,1536]{1,0:T(8,128)(2,1)}, bf16[512,1536]{1,0:T(8,128)(2,1)}, u32[]{:S(2)}, u32[]{:S(2)}) collective-permute-start(bf16[512,1536]{1,0:T(8,128)(2,1)} %pack.5), channel_id=1, source_target_pairs={{0,1},{1,2},{2,3},{3,0},{4,5},{5,6},{6,7},{7,4},{8,9},{9,10},{10,1... | collective-permute-start | bytes 4718600 | tf_op jit(solution)/shard_map/ppermute | solution.py:362
  343.5 57.4 %collective-permute-start.24 = (bf16[512,2048]{1,0:T(8,128)(2,1)}, bf16[512,2048]{1,0:T(8,128)(2,1)}, u32[]{:S(2)}, u32[]{:S(2)}) collective-permute-start(bf16[512,2048]{1,0:T(8,128)(2,1)} %pad_maximum_fusion.2), channel_id=1, source_target_pairs={{0,8},{4,12},{8,0},{12,4},{16,24},{20,28},{24,16},{28,20},{1,9},{5... | collective-permute-start | bytes 6291464 | tf_op jit(solution)/shard_map/ppermute | solution.py:359
  348.1 107.4 %collective-permute-start.26 = (bf16[512,1536]{1,0:T(8,128)(2,1)}, bf16[512,1536]{1,0:T(8,128)(2,1)}, u32[]{:S(2)}, u32[]{:S(2)}) collective-permute-start(bf16[512,1536]{1,0:T(8,128)(2,1)} %pack.6), channel_id=1, source_target_pairs={{0,2},{1,3},{2,0},{3,1},{4,6},{5,7},{6,4},{7,5},{8,10},{9,11},{10,... | collective-permute-start | bytes 4718600 | tf_op jit(solution)/shard_map/ppermute | solution.py:362
  392.6 80.7 %collective-permute-start.31 = (bf16[512,1536]{1,0:T(8,128)(2,1)}, bf16[512,1536]{1,0:T(8,128)(2,1)}, u32[]{:S(2)}, u32[]{:S(2)}) collective-permute-start(bf16[512,1536]{1,0:T(8,128)(2,1)} %collective-permute-done.27.refs_5_), channel_id=1, source_target_pairs={{0,4},{4,0},{8,12},{12,8},{16,20},{20,16},{24,28},{28,24},{1,5},{5... | collective-permute-start | bytes 4718600 | tf_op jit(solution)/shard_map/ppermute | solution.py:359
  392.6 80.7 %collective-permute-start.29 = (bf16[512,1536]{1,0:T(8,128)(2,1)}, bf16[512,1536]{1,0:T(8,128)(2,1)}, u32[]{:S(2)}, u32[]{:S(2)}) collective-permute-start(bf16[512,1536]{1,0:T(8,128)(2,1)} %collective-permute-done.25.refs_3_), channel_id=1, source_target_pairs={{0,4},{4,0},{8,12},{12,8},{16,20},{20,16},{24,28},{28,24},{1,5},{5... | collective-permute-start | bytes 4718600 | tf_op jit(solution)/shard_map/ppermute | solution.py:359
  397.7 75.6 %collective-permute-start.28 = (bf16[512,1536]{1,0:T(8,128)(2,1)}, bf16[512,1536]{1,0:T(8,128)(2,1)}, u32[]{:S(2)}, u32[]{:S(2)}) collective-permute-start(bf16[512,1536]{1,0:T(8,128)(2,1)} %pack.4.refs_2_), channel_id=1, source_target_pairs={{0,4},{4,0},{8,12},{12,8},{16,20},{20,16},{24,28},{28,24},{1,5},{5... | collective-permute-start | bytes 4718600 | tf_op jit(solution)/shard_map/ppermute | solution.py:359
  570.1 47.8 %collective-permute-start.32 = (bf16[512,2048]{1,0:T(8,128)(2,1)}, bf16[512,2048]{1,0:T(8,128)(2,1)S(1)}, u32[]{:S(2)}, u32[]{:S(2)}) collective-permute-start(bf16[512,2048]{1,0:T(8,128)(2,1)} %get-tuple-element.201), channel_id=1, source_target_pairs={{0,16},{4,20},{8,24},{12,28},{16,0},{20,4},{24,8},{28,12},{1,17},{... | collective-permute-start | bytes 6291464 | tf_op jit(solution)/shard_map/ppermute | solution.py:359
  570.5 48.2 %collective-permute-start.33 = (bf16[512,2048]{1,0:T(8,128)(2,1)}, bf16[512,2048]{1,0:T(8,128)(2,1)S(1)}, u32[]{:S(2)}, u32[]{:S(2)}) collective-permute-start(bf16[512,2048]{1,0:T(8,128)(2,1)} %get-tuple-element.200), channel_id=1, source_target_pairs={{0,8},{4,12},{8,0},{12,4},{16,24},{20,28},{24,16},{28,20},{1,9},{5... | collective-permute-start | bytes 6291464 | tf_op jit(solution)/shard_map/ppermute | solution.py:359
  664.1 384.3 %reduce-scatter.5.cloned.1.call-start = ((), (), s32[]{:S(2)}) async-start(), calls=%async_computation.3 | async-start | bytes 2621440 | tf_op jit(solution)/shard_map/reduce_scatter | solution.py:674
  664.2 70.2 %collective-permute-start.41 = (bf16[512,1536]{1,0:T(8,128)(2,1)}, bf16[512,1536]{1,0:T(8,128)(2,1)S(1)}, u32[]{:S(2)}, u32[]{:S(2)}) collective-permute-start(bf16[512,1536]{1,0:T(8,128)(2,1)} %get-tuple-element.190), channel_id=1, source_target_pairs={{0,3},{1,0},{2,1},{3,2},{4,7},{5,4},{6,5},{7,6},{8,11},{9,8},{10,9... | collective-permute-start | bytes 4718600 | tf_op jit(solution)/shard_map/ppermute | solution.py:362
  667.2 66.7 %collective-permute-start.39 = (bf16[128,2048]{1,0:T(8,128)(2,1)S(1)}, bf16[128,2048]{1,0:T(8,128)(2,1)S(1)}, u32[]{:S(2)}, u32[]{:S(2)}) collective-permute-start(bf16[128,2048]{1,0:T(8,128)(2,1)S(1)} %get-tuple-element.224), channel_id=1, source_target_pairs={{0,2},{1,3},{2,0},{3,1},{4,6},{5,7},{6,4},{7,5},{8,10},{9,11},{10,... | collective-permute-start | bytes 1572872 | tf_op jit(solution)/shard_map/ppermute | solution.py:377
  667.4 66.5 %collective-permute-start.40 = (bf16[128,2048]{1,0:T(8,128)(2,1)S(1)}, bf16[128,2048]{1,0:T(8,128)(2,1)S(1)}, u32[]{:S(2)}, u32[]{:S(2)}) collective-permute-start(bf16[128,2048]{1,0:T(8,128)(2,1)S(1)} %get-tuple-element.225), channel_id=1, source_target_pairs={{0,3},{1,2},{2,1},{3,0},{4,7},{5,6},{6,5},{7,4},{8,11},{9,10},{10,... | collective-permute-start | bytes 1572872 | tf_op jit(solution)/shard_map/ppermute | solution.py:377
  670.1 63.8 %collective-permute-start.38 = (bf16[128,2048]{1,0:T(8,128)(2,1)S(1)}, bf16[128,2048]{1,0:T(8,128)(2,1)S(1)}, u32[]{:S(2)}, u32[]{:S(2)}) collective-permute-start(bf16[128,2048]{1,0:T(8,128)(2,1)S(1)} %broadcast_select_fusion.2), channel_id=1, source_target_pairs={{0,1},{1,0},{2,3},{3,2},{4,5},{5,4},{6,7},{7,6},{8,9},{9,8},{10,11... | collective-permute-start | bytes 1572872 | tf_op jit(solution)/shard_map/ppermute | solution.py:377
  738.3 67.6 %collective-permute-start.43 = (bf16[128,2048]{1,0:T(8,128)(2,1)}, bf16[128,2048]{1,0:T(8,128)(2,1)}, u32[]{:S(2)}, u32[]{:S(2)}) collective-permute-start(bf16[128,2048]{1,0:T(8,128)(2,1)} %fusion.65), channel_id=1, source_target_pairs={{0,2},{1,3},{2,0},{3,1},{4,6},{5,7},{6,4},{7,5},{8,10},{9,11},{10,... | collective-permute-start | bytes 1572872 | tf_op jit(solution)/shard_map/ppermute | solution.py:362
  830.7 86.3 %collective-permute-start.48 = (bf16[512,1536]{1,0:T(8,128)(2,1)}, bf16[512,1536]{1,0:T(8,128)(2,1)}, u32[]{:S(2)}, u32[]{:S(2)}) collective-permute-start(bf16[512,1536]{1,0:T(8,128)(2,1)} %get-tuple-element.106), channel_id=1, source_target_pairs={{0,2},{1,3},{2,0},{3,1},{4,6},{5,7},{6,4},{7,5},{8,10},{9,11},{10,... | collective-permute-start | bytes 4718600 | tf_op jit(solution)/shard_map/ppermute | solution.py:362
  858.5 58.5 %collective-permute-start.58 = (bf16[2,2,256,1536]{3,2,1,0:T(8,128)(2,1)}, bf16[2,2,256,1536]{3,2,1,0:T(8,128)(2,1)}, u32[]{:S(2)}, u32[]{:S(2)}) collective-permute-start(bf16[2,2,256,1536]{3,2,1,0:T(8,128)(2,1)} %fusion.1), channel_id=1, source_target_pairs={{0,4},{4,0},{8,12},{12,8},{16,20},{20,16},{24,28},{28,24},{1,5},{5... | collective-permute-start | bytes 9437192 | tf_op jit(solution)/shard_map/ppermute | solution.py:359
  928.5 55.9 %collective-permute-start.61 = (bf16[2,256,768]{2,1,0:T(8,128)(2,1)S(1)}, bf16[2,256,768]{2,1,0:T(8,128)(2,1)S(1)}, u32[]{:S(2)}, u32[]{:S(2)}) collective-permute-start(bf16[2,256,768]{2,1,0:T(8,128)(2,1)S(1)} %dynamic-slice_bitcast_fusion), channel_id=1, source_target_pairs={{0,16},{4,20},{8,24},{12,28},{16,0},{20,4},{24,8},{28,12},{1,17},{... | collective-permute-start | bytes 2359304 | tf_op jit(solution)/shard_map/ppermute | solution.py:359
  932.0 52.7 %collective-permute-start.49 = (bf16[128,2048]{1,0:T(8,128)(2,1)S(1)}, bf16[128,2048]{1,0:T(8,128)(2,1)S(1)}, u32[]{:S(2)}, u32[]{:S(2)}) collective-permute-start(bf16[128,2048]{1,0:T(8,128)(2,1)S(1)} %get-tuple-element.208), channel_id=1, source_target_pairs={{0,1},{1,2},{2,3},{3,0},{4,5},{5,6},{6,7},{7,4},{8,9},{9,10},{10,1... | collective-permute-start | bytes 1572872 | tf_op jit(solution)/shard_map/ppermute | solution.py:362
  934.0 76.4 %collective-permute-start.50 = (bf16[128,2048]{1,0:T(8,128)(2,1)S(1)}, bf16[128,2048]{1,0:T(8,128)(2,1)S(1)}, u32[]{:S(2)}, u32[]{:S(2)}) collective-permute-start(bf16[128,2048]{1,0:T(8,128)(2,1)S(1)} %get-tuple-element.210), channel_id=1, source_target_pairs={{0,2},{1,3},{2,0},{3,1},{4,6},{5,7},{6,4},{7,5},{8,10},{9,11},{10,... | collective-permute-start | bytes 1572872 | tf_op jit(solution)/shard_map/ppermute | solution.py:362
  942.4 68.1 %collective-permute-start.51 = (bf16[128,2048]{1,0:T(8,128)(2,1)S(1)}, bf16[128,2048]{1,0:T(8,128)(2,1)S(1)}, u32[]{:S(2)}, u32[]{:S(2)}) collective-permute-start(bf16[128,2048]{1,0:T(8,128)(2,1)S(1)} %get-tuple-element.209), channel_id=1, source_target_pairs={{0,3},{1,0},{2,1},{3,2},{4,7},{5,4},{6,5},{7,6},{8,11},{9,8},{10,9... | collective-permute-start | bytes 1572872 | tf_op jit(solution)/shard_map/ppermute | solution.py:362
  948.0 64.4 %collective-permute-start.60 = (bf16[256,768]{1,0:T(8,128)(2,1)S(1)}, bf16[256,768]{1,0:T(8,128)(2,1)S(1)}, u32[]{:S(2)}, u32[]{:S(2)}) collective-permute-start(bf16[256,768]{1,0:T(8,128)(2,1)S(1)} %dynamic-slice_bitcast_fusion.4), channel_id=1, source_target_pairs={{0,16},{4,20},{8,24},{12,28},{16,0},{20,4},{24,8},{28,12},{1,17},{... | collective-permute-start | bytes 1179656 | tf_op jit(solution)/shard_map/ppermute | solution.py:359
  (134 other events, 2103.8 us)
Sparse Core Ops, SparseCore 0:
  97.4 166.0 all-gather.2
  664.2 83.9 reduce-scatter.2
  927.3 81.1 reduce-scatter.4

commit v4 on v3

--- a/solution.py
+++ b/solution.py
@@ -41,8 +41,38 @@
     return dot(a, b, ((0,), (0,)))
 
 
+def both(*arrays):
+    return lax.optimization_barrier(arrays)
+
+
 def tie(x, *after):
     return lax.optimization_barrier((x, after))[0]
+
+
+def spread_kernel(n_w, shard_ref, *refs):
+    out_ref = refs[-1]
+    cols = refs[0].shape[1] // 3
+    for s in range(n_w):
+        t = lax.rem(shard_ref[0] - s + n_w, n_w)
+        for part in range(3):
+            at = pl.multiple_of((part * n_w + t) * cols, 128)
+            out_ref[:, pl.ds(at, cols)] = refs[s][:, part * cols : (part + 1) * cols].astype(F32)
+
+
+def spread(pieces, shard):
+    n_w = len(pieces)
+    rows, width = pieces[0].shape
+    return pl.pallas_call(
+        functools.partial(spread_kernel, n_w),
+        grid_spec=pltpu.PrefetchScalarGridSpec(
+            num_scalar_prefetch=1,
+            grid=(1,),
+            in_specs=[pl.BlockSpec((rows, width), lambda i, at: (0, 0))] * n_w,
+            out_specs=pl.BlockSpec((rows, n_w * width), lambda i, at: (0, 0)),
+        ),
+        out_shape=jax.ShapeDtypeStruct((rows, n_w * width), F32),
+        name="spread",
+    )(shard.reshape(1), *pieces)
 
 
 LIGHT = pl.CostEstimate(flops=1, bytes_accessed=1, transcendentals=0)
@@ -145,6 +175,83 @@
     )(*ins)
 
 
+def plane_rows(ref, order):
+    picks = range(1 << len(order))
+    return jnp.concatenate([ref[tuple((i // d) % 2 for d in order) + (0,)] for i in picks], 0)
+
+
+def out_kernel(n_w, orders, at_ref, x_ref, gain_ref, *refs):
+    pieces, weights, (resid_ref, ffn_ref) = refs[:n_w], refs[n_w : 3 * n_w], refs[3 * n_w :]
+    total = []
+    for p, order in enumerate(orders):
+        half = weights[0].shape[-1]
+        part = x_ref[:, p * half : (p + 1) * half].astype(F32)
+        for s in range(n_w):
+            part = part + mm(pieces[s][...], plane_rows(weights[p * n_w + s], order))
+        total.append(part)
+    total = jnp.concatenate(total, 1)
+    resid_ref[...] = total
+    ffn_ref[...] = (total * rms_scale(total) * gain_ref[...]).astype(LOW)
+
+
+def out_back_kernel(n_w, orders, at_ref, dffn_ref, resid_ref, dy_ref, gain_ref, *refs):
+    weights, (dresid_ref, low_ref, sum_ref) = refs[: 2 * n_w], refs[2 * n_w : 2 * n_w + 3]
+    outs = refs[2 * n_w + 3 :]
+    dffn, resid = dffn_ref[...], resid_ref[...]
+    scale = rms_scale(resid)
+    weighted = gain_ref[...] * dffn
+    inner = jnp.mean(resid * weighted, axis=-1, keepdims=True)
+    dresid = dy_ref[...].astype(F32) + norm_back(resid, scale, gain_ref[...], dffn, inner)
+    dresid_ref[...] = dresid
+    low_ref[...] = dresid.astype(LOW)
+    sum_ref[...] = jnp.sum(dffn * resid * scale, axis=0, keepdims=True)
+    for s in range(n_w):
+        total = 0.0
+        for p, order in enumerate(orders):
+            half = weights[0].shape[-1]
+            weight = plane_rows(weights[p * n_w + s], order)
+            total = total + mm_t(low_ref[:, p * half : (p + 1) * half], weight)
+        outs[s][...] = total.astype(LOW)
+
+
+def out_grad_kernel(n_w, orders, at_ref, low_ref, *refs):
+    pieces, out_ref = refs[:n_w], refs[n_w]
+    cols = pieces[0].shape[1]
+    for s in range(n_w):
+        rows = pl.ds(pl.multiple_of(at_ref[s] * cols, 128), cols)
+        out_ref[rows, :] = t_mm(pieces[s][...], low_ref[...]).astype(LOW)
+
+
+def out_call(kernel, name, at, ins, weights, orders, outs):
+    n_w = at.shape[0]
+
+    def fixed(shape):
+        return pl.BlockSpec(shape, lambda i, at: (0,) * len(shape))
+
+    specs = [fixed(a.shape) for a in ins]
+    for weight in weights:
+        lead = weight.ndim - 3
+        shape = weight.shape[:lead] + (1,) + weight.shape[-2:]
+        for s in range(n_w):
+            specs.append(
+                pl.BlockSpec(shape, lambda i, at, s=s, lead=lead: (0,) * lead + (at[s], 0, 0))
+            )
+        ins = ins + [weight] * n_w
+    return pl.pallas_call(
+        functools.partial(kernel, n_w, orders),
+        grid_spec=pltpu.PrefetchScalarGridSpec(
+            num_scalar_prefetch=1,
+            grid=(1,),
+            in_specs=specs,
+            out_specs=[fixed(o.shape) for o in outs],
+        ),
+        out_shape=outs,
+        compiler_params=pltpu.CompilerParams(vmem_limit_bytes=56 * 1024 * 1024),
+        cost_estimate=LIGHT,
+        name=name,
+    )(at, *ins)
+
+
 def pack_kernel(at_ref, up_ref, down_ref, out_ref):
     step = pl.program_id(0)
 
@@ -228,8 +335,8 @@
 def expert_kernel(experts, n_w, at_ref, place_ref, x_ref, dy_all_ref, used_ref, hot_ref, *refs):
     router_ref, back_router_ref, refs = refs[0], refs[1], refs[2:]
     packs, refs = (refs[:n_w], refs[n_w : 2 * n_w]), refs[2 * n_w :]
-    mix_ref, back_ref, dy_ref, dlogits_ref = refs[:4]
-    dgu_refs, gated_refs = refs[4:6], refs[6:8]
+    mix_ref, back_ref, dy_ref, dlogits_ref = refs[-8:-4]
+    dgu_refs, gated_refs = refs[-4:-2], refs[-2:]
     dy_ref[...] = dy_all_ref[...].reshape(dy_ref.shape)
     hidden = packs[0][0].shape[1] // 3
     cols = packs[0][0].shape[0]
@@ -270,7 +377,7 @@
         mix_ref[:, spans[s]] = mix.astype(LOW)
 
 
-def expert_pass(x, dy, rows, used, hots, router, packs, at, place, experts):
+def expert_pass(x, dy, rows, used, hots, router, packs, at, place, mix, experts):
     n, width = x.shape
     n_w = len(packs[0])
     tile = 2 * rows
@@ -286,8 +393,11 @@
     def fixed(shape):
         return pl.BlockSpec(shape, lambda i, at, place: (0, 0), pipeline_mode=pl.Buffered(1))
 
-    router = jnp.pad(router, ((0, 0), (0, lanes - experts)))
     outs = [width, width, width, lanes, 2 * hidden, 2 * hidden, hidden, hidden]
+    shapes = [jax.ShapeDtypeStruct((n, c), LOW) for c in outs]
+    shapes[0] = jax.ShapeDtypeStruct((used.shape[0], width), LOW)
+    ins = [x, dy, used, hots, *router, *packs[0], *packs[1]]
+    held = [mix] if mix.shape[0] else []
     return pl.pallas_call(
         functools.partial(expert_kernel, experts, n_w),
         grid_spec=pltpu.PrefetchScalarGridSpec(
@@ -299,54 +409,71 @@
                 placed(lanes),
             ]
             + [fixed((2, lanes)), fixed((width, lanes)), fixed((lanes, width))]
-            + [fixed((cols, 3 * hidden))] * (2 * n_w),
+            + [fixed((cols, 3 * hidden))] * (2 * n_w)
+            + [pl.BlockSpec(memory_space=pl.ANY)] * len(held),
             out_specs=[placed(width)] + [tiled(c) for c in outs[1:]],
         ),
-        out_shape=[jax.ShapeDtypeStruct((n, c), LOW) for c in outs],
+        out_shape=shapes,
+        input_output_aliases={len(ins) + 2: 0} if held else {},
         compiler_params=pltpu.CompilerParams(vmem_limit_bytes=56 * 1024 * 1024),
         cost_estimate=LIGHT,
         name="expert_pass",
-    )(at, place, x, dy, used, hots, router, router.T, *packs[0], *packs[1])
-
-
-def grad_kernel(shard_ref, x_ref, dy_ref, dgu_ref, gated_ref, *refs):
-    out_ref = refs[-1]
-    hidden = gated_ref.shape[1]
-    if len(refs) > 1:
-        dlogits_ref, out_ref, router_ref = refs
-        router_ref[...] = t_mm(x_ref[...], dlogits_ref[...])
-    out_ref[0, :, : 2 * hidden] = t_mm(x_ref[...], dgu_ref[...]).astype(out_ref.dtype)
-    out_ref[0, :, 2 * hidden :] = t_mm(gated_ref[...], dy_ref[...]).astype(out_ref.dtype)
-
-
-def grad_pass(x, dy, dgu, gated, dlogits, shard, n_w, kind):
-    n, width = x.shape
-    hidden = gated.shape[1]
+    )(at, place, *ins, *held)
+
+
+def grad_kernel(count, shard_ref, *refs):
+    hidden = refs[3].shape[1]
+    with_router = len(refs) > 4 * count + 1
+    each = 5 if with_router else 4
+    out_ref = refs[each * count]
+    up = down = router = 0.0
+    for k in range(count):
+        x_ref, dy_ref, dgu_ref, gated_ref = refs[each * k : each * k + 4]
+        up = up + t_mm(x_ref[...], dgu_ref[...])
+        down = down + t_mm(gated_ref[...], dy_ref[...])
+        if with_router:
+            router = router + t_mm(x_ref[...], refs[each * k + 4][...])
+    out_ref[0, :, : 2 * hidden] = up.astype(out_ref.dtype)
+    out_ref[0, :, 2 * hidden :] = down.astype(out_ref.dtype)
+    if with_router:
+        refs[-1][...] = router
+
+
+def grad_pass(parts, shard, n_w, kind):
+    width = parts[0][0].shape[1]
+    hidden = parts[0][3].shape[1]
     cols = width // n_w
-
-    def fixed(a):
-        return pl.BlockSpec(a.shape, lambda i, at: (0, 0), pipeline_mode=pl.Buffered(1))
-
-    column = pl.BlockSpec((n, cols), lambda i, at: (0, lax.rem(at[0] + i, n_w)))
-    ins, specs = [x, dy, dgu, gated], [column, column, fixed(dgu), fixed(gated)]
+    tokens = sum(part[0].shape[0] for part in parts)
+    specs = []
+    for part in parts:
+        n = part[0].shape[0]
+        column = pl.BlockSpec((n, cols), lambda i, at: (0, lax.rem(at[0] + i, n_w)))
+        specs += [column, column]
+        for a in part[2:]:
+            specs.append(
+                pl.BlockSpec(a.shape, lambda i, at: (0, 0), pipeline_mode=pl.Buffered(1))
+            )
     out_specs = [pl.BlockSpec((1, cols, 3 * hidden), lambda i, at: (i, 0, 0))]
     outs = [jax.ShapeDtypeStruct((n_w, cols, 3 * hidden), kind)]
-    if dlogits is not None:
-        lanes = dlogits.shape[1]
-        ins, specs = ins + [dlogits], specs + [fixed(dlogits)]
+    if len(parts[0]) > 4:
+        lanes = parts[0][4].shape[1]
         out_specs.append(pl.BlockSpec((cols, lanes), lambda i, at: (lax.rem(at[0] + i, n_w), 0)))
         outs.append(jax.ShapeDtypeStruct((width, lanes), F32))
     return tuple(
         pl.pallas_call(
-            grad_kernel,
+            functools.partial(grad_kernel, len(parts)),
             grid_spec=pltpu.PrefetchScalarGridSpec(
                 num_scalar_prefetch=1, grid=(n_w,), in_specs=specs, out_specs=out_specs
             ),
             out_shape=outs,
             compiler_params=pltpu.CompilerParams(vmem_limit_bytes=56 * 1024 * 1024),
-            cost_estimate=LIGHT,
+            cost_estimate=pl.CostEstimate(
+                flops=6 * tokens * width * hidden,
+                bytes_accessed=4 * tokens * width + 20 * width * hidden,
+                transcendentals=0,
+            ),
             name="grad_pass",
-        )(shard.reshape(1), *ins)
+        )(shard.reshape(1), *[a for part in parts for a in part])
     )
 
 
@@ -360,9 +487,6 @@
 
     def shift(x, s):
         return lax.ppermute(x, "wshard", [(j, (j + s) % n_w) for j in range(n_w)])
-
-    def joint(x, pairs):
-        return lax.ppermute(x, AXES, pairs)
 
     def line_gather(x):
         return [x] + [shift(x, n_w - r) for r in range(1, n_w)]
@@ -372,6 +496,10 @@
         for r in range(1, n_w):
             total = total + shift(blocks[r], r).astype(F32)
         return total
+
+    def joined(x, d, me):
+        got, upper = swap(x, d), (me // d) % 2 == 1
+        return jnp.stack([jnp.where(upper, got, x), jnp.where(upper, x, got)])
 
     def across(x, r):
         return lax.ppermute(x, "wshard", [(j, j ^ r) for j in range(n_w)])
@@ -416,11 +544,14 @@
     def way(p, step):
         return plane[(step + p * nd // 2) % nd]
 
-    def plane_gather(parts):
+    def plane_gather(parts, early):
         held = [([0], x) for x in parts]
         groups = [held]
         for step in range(nd):
             got = []
+            if step == nd - 1:
+                arrays, early = both([x for _, x in held], early)
+                held = [(masks, x) for (masks, _), x in zip(held, arrays)]
             for p, (masks, x) in enumerate(held):
                 got.append(([m | way(p, step) for m in masks], swap(x, way(p, step))))
             groups.append(got)
@@ -428,14 +559,14 @@
                 (a[0] + b[0], jnp.concatenate([a[1], b[1]], 0)) if step + 1 < nd else None
                 for a, b in zip(held, got)
             ]
-        return groups
-
-    def plane_scatter(groups, beside):
+        return groups, early
+
+    def plane_scatter(groups, held):
         mine = [[group[p] for group in groups] for p in range(2)]
         for step in reversed(range(nd)):
             got = [swap(mine[p][step + 1], way(p, step)) for p in range(2)]
-            if beside is not None:
-                got, beside = tie(got, beside), None
+            if step == nd - 1:
+                got, held = both(got, held())
             for p in range(2):
                 at = 0
                 for low in range(step + 1):
@@ -443,8 +574,8 @@
                     total = mine[p][low].astype(F32) + got[p][at : at + n].astype(F32)
                     mine[p][low] = total.astype(LOW)
                     at += n
-            mine = lax.optimization_barrier([m[: step + 1] for m in mine])
-        return [m[0] for m in mine]
+            (mine,) = both([m[: step + 1] for m in mine])
+        return [m[0] for m in mine], held
 
     def hyper_scatter(x, me, kind, cut=1):
         def halve(x, left, d):
@@ -510,46 +641,63 @@
             routes.reshape(own, -1, 1) == jnp.arange(experts, dtype=jnp.int32), axis=1
         ).astype(LOW)
         blocks = line_gather(normed)
-        blocks, bank = lax.optimization_barrier((blocks, bank))
+
+        rounds = max(1, n_e * n_w * own // 2 // ROUND_TOKENS)
+        step = own // rounds
+        hidden = units * local_experts // n_w
+        arrived = (shard - jnp.arange(n_w, dtype=jnp.int32) + n_w) % n_w
+        same = [[2 * c + k for c in range(n_e // 2)] for k in range(2)]
+        router_rows = w_router.size // width
+        used_rows = step * experts // width
+
+        def rows_for(at):
+            rows = [upstream[at : at + step], used[at : at + step].reshape(-1, width)]
+            rows = jnp.concatenate(rows + [w_router.reshape(-1, width)], 0)
+            return jnp.pad(rows, ((0, -rows.shape[0] % 16), (0, 0)))
+
+        def to_line(rows):
+            return lax.all_gather(rows, "wshard")
+
+        def to_pairs(rows):
+            rows = lax.all_gather(rows, "expert", axis_index_groups=same)
+            return rows.reshape((-1,) + rows.shape[2:])
+
+        pieces = [
+            pack_half((shard + k) % n_w, w_gate_up, w_down, n_w // local_experts)
+            for k in range(n_w)
+        ]
+        out_slice = lax.dynamic_slice_in_dim(w_out, me * piece, piece, 0)
+        blocks, bank, dy_rows, pieces, out_slice = both(blocks, bank, rows_for(0), pieces, out_slice)
+
+        full_out = line_gather(out_slice)
+        dy_rows = to_line(dy_rows)
+        first, second = jnp.split(pieces[2], 2, 0)
+        first = shift(first, 2)
         normed_all = jnp.concatenate(blocks, 0)
 
         half = piece // 2
-        w_heads = []
+        helds = []
         for p in range(2):
             held = bank[:, p * half : (p + 1) * half]
+            for d in plane[p:] + plane[:p]:
+                held = joined(held, d, me)
+            helds.append(held)
+        helds, full_out = both(helds, full_out)
+        w_heads = []
+        for p, held in enumerate(helds):
+            held = joined(held, 1, me)
             dims = plane[p:] + plane[:p] + [1]
-            for d in dims:
-                got, upper = swap(held, d), (me // d) % 2 == 1
-                held = jnp.stack([jnp.where(upper, got, held), jnp.where(upper, held, got)])
             at = {d: len(dims) - 1 - k for k, d in enumerate(dims)}
             k = len(dims)
             w_heads.append(held.transpose(k, *[at[d] for d in reversed(bits)], k + 1, k + 2))
         w_heads = jnp.stack(w_heads, 1 + len(bits)).reshape(width, 3 * cols)
-
-        rounds = max(1, n_e * n_w * own // 2 // ROUND_TOKENS)
-        step = own // rounds
-        hidden = units * local_experts // n_w
-        arrived = (shard - jnp.arange(n_w, dtype=jnp.int32) + n_w) % n_w
-
-        def pack_for(t):
-            return pack_half(t, w_gate_up, w_down, n_w // local_experts)
-
-        pairs = [
-            [(2 * c + k) * n_w + w for c in range(n_e // 2) for w in range(n_w)] for k in range(2)
-        ]
-        router_rows = w_router.size // width
-        used_rows = step * experts // width
-
-        def to_pairs(at):
-            rows = [upstream[at : at + step], used[at : at + step].reshape(-1, width)]
-            rows.append(w_router.reshape(-1, width))
-            rows = jnp.concatenate(rows, 0)
-            rows = jnp.pad(rows, ((0, -rows.shape[0] % 16), (0, 0)))
-            return lax.all_gather(tie(rows, blocks), AXES, axis_index_groups=pairs)
-
-        dy_all = to_pairs(0)
-        pieces = [tie(pack_for((shard + k) % n_w), blocks) for k in range(n_w)]
-        pieces = [pieces[k] if k in (0, 2) else shift(pieces[k], k) for k in range(n_w)]
+        full_out = jnp.split(jnp.roll(jnp.stack(full_out), shard, axis=0), 2, -1)
+        ways = [plane[p:] + plane[:p] + [1] for p in range(2)]
+        for step_at, (d0, d1) in enumerate(zip(*ways)):
+            full_out = [joined(full_out[0], d0, me), joined(full_out[1], d1, me)]
+            if step_at == 0:
+                w_heads, full_out, first = both(w_heads, full_out, first)
+        orders = [list(reversed(w)) for w in ways]
 
         projected = mm(normed_all, w_heads)
         squares = jnp.sum(projected.reshape(-1, 3, cols)[:, :2] ** 2, axis=-1).T
@@ -580,14 +728,20 @@
             sine,
             mask,
         )
-        attended = attention().reshape(n_w * own, cols)
-        branch = mm(attended, w_out).astype(LOW)
-        pieces = [p if k in (0, 2) else tie(p, branch) for k, p in enumerate(pieces)]
-        branch = branch.reshape(n_w, own, width)
-        resid = tokens + line_scatter([branch[r] for r in range(n_w)])
-
-        scale_two = rms_scale(resid)
-        ffn_in = (resid * scale_two * ffn_gain).astype(LOW)
+        attended = attention().reshape(n_w, own, cols)
+        attended, dy_rows, full_out = both(attended, dy_rows, full_out)
+        dy_all = to_pairs(dy_rows)
+        attended = [shift(attended[r], r) if r else attended[r] for r in range(n_w)]
+        resid, ffn_in = out_call(
+            out_kernel,
+            "out",
+            arrived,
+            [hidden_in.reshape(own, width), ffn_gain[None]] + attended,
+            full_out,
+            orders,
+            [jax.ShapeDtypeStruct((own, width), F32), jax.ShapeDtypeStruct((own, width), LOW)],
+        )
+
         lanes = -(-experts // 128) * 128
         expert_at = jnp.arange(lanes, dtype=jnp.int32)
         my_expert = local_experts * me + shard * local_experts // n_w
@@ -606,77 +760,109 @@
                 ffn_rows, grads, dffn, mixture = lax.optimization_barrier(
                     (ffn_rows, grads, dffn, mixture)
                 )
-                dy_all = to_pairs(at)
+                dy_all = to_pairs(to_line(tie(rows_for(at), ffn_rows)))
             parts = pair_parts(ffn_rows, shard)
-            groups = plane_gather(parts)
-            x = whole(groups)
-            place = [
-                jnp.bitwise_xor(me // 2, m // 2) * (n_w // 2) + jnp.bitwise_xor(shard // 2, p)
-                for group in groups
-                for p in range(2)
-                for m in group[p][0]
-            ]
+            if n == 0:
+                parts, pieces, second = both(parts, pieces, second)
+                pieces[1] = shift(pieces[1], 1)
             mask = dy_all[:, step : step + used_rows].reshape(-1, experts)
             mask = jnp.pad(mask, ((0, 0), (0, lanes - experts)))
             router = dy_all[:n_w, step + used_rows : step + used_rows + router_rows]
-            router = router.reshape(width, experts)
+            router = jnp.pad(router.reshape(width, experts), ((0, 0), (0, lanes - experts)))
+            groups, (mask, router, router_t, pieces) = plane_gather(
+                parts, (mask, router, router.T, pieces)
+            )
+            waves = [groups]
+            xs = [whole(wave) for wave in waves]
+            places = [
+                jnp.stack(
+                    [
+                        jnp.bitwise_xor(me // 2, m // 2) * (n_w // 2)
+                        + jnp.bitwise_xor(shard // 2, p)
+                        for group in wave
+                        for p in range(2)
+                        for m in group[p][0]
+                    ]
+                )
+                for wave in waves
+            ]
             if n == 0:
-                pieces[2] = tie(shift(tie(pieces[2], parts), 2), x)
-                siblings = [swap(tie(piece, parts), 1) for piece in pieces]
-                packs = [pieces, siblings]
-            mix, back, dy, dlogits, dgu0, dgu1, gated0, gated1 = expert_pass(
-                x, dy_all, step, mask, hots, router, packs, arrived, jnp.stack(place), experts
-            )
-            cuts = []
-            for group in groups:
-                for p in range(2):
-                    cuts.append((cuts[-1] if cuts else 0) + group[p][1].shape[0])
-            back = jnp.split(back, cuts[:-1], 0)
-            back = [back[2 * g : 2 * g + 2] for g in range(nd + 1)]
+                pieces[3] = shift(pieces[3], 3)
+                pieces[2] = jnp.concatenate([first, shift(second, 2)], 0)
+                packs = [pieces, [swap(piece, 1) for piece in pieces]]
+            mix = jnp.zeros((0, width), LOW)
+            back, passed = [], []
+            for wave, x, place in zip(waves, xs, places):
+                mix, part, *rest = expert_pass(
+                    x, dy_all, step, mask, hots, (router, router_t), packs, arrived, place, mix, experts
+                )
+                cuts = []
+                for group in wave:
+                    for p in range(2):
+                        cuts.append((cuts[-1] if cuts else 0) + group[p][1].shape[0])
+                part = jnp.split(part, cuts[:-1], 0)
+                back += [part[2 * g : 2 * g + 2] for g in range(len(wave))]
+                passed.append([x] + rest)
             kind = LOW if rounds == 1 else F32
-            grad_sib, grad_router = grad_pass(x, dy, dgu1, gated1, dlogits, shard, n_w, kind)
-            (grad_own,) = grad_pass(x, dy, dgu0, gated0, None, shard, n_w, kind)
-            if grads is not None:
-                grad_sib, grad_router, grad_own = jax.tree.map(
-                    jnp.add, grads, (grad_sib, grad_router, grad_own)
-                )
-            grads = (grad_sib, grad_router, grad_own)
-            beside = grads
+            def weight_grads():
+                ins = [[x, dy, dgu1, gated1, dlogits] for x, dy, dlogits, _, dgu1, _, gated1 in passed]
+                sib = grad_pass(ins, shard, n_w, kind)
+                ins = [[x, dy, dgu0, gated0] for x, dy, _, dgu0, _, gated0, _ in passed]
+                return sib + grad_pass(ins, shard, n_w, kind)
+
+            back, new = plane_scatter(back, weight_grads)
+            grads = new if grads is None else jax.tree.map(jnp.add, grads, new)
+            grad_sib, grad_router, grad_own = grads
             if n == rounds - 1:
                 grad_sib = swap(grad_sib.astype(LOW), 1)
                 sums = [
                     (grad_own[s].astype(F32) + grad_sib[s].astype(F32)).astype(LOW)
                     for s in range(n_w)
                 ]
-                beside = sums
-            back = plane_scatter(back, beside)
-            if n == rounds - 1:
-                sums[1], sums[3] = shift(sums[1], 1), shift(sums[3], 3)
-                back = tie(back, sums[1])
+                sums[1] = shift(sums[1], 1)
+                back, sums[1] = both(back, sums[1])
+            back, mix = both(back, mix)
             dffn.append(pair_scatter(back, shard))
-            if n == rounds - 1:
-                dffn = tie(dffn, sums[3])
-            same = [[2 * c + k for c in range(n_e // 2)] for k in range(2)]
             mixture.append(
-                lax.psum_scatter(tie(mix, back), "expert", axis_index_groups=same, tiled=True)
+                lax.psum_scatter(mix, "expert", axis_index_groups=same, tiled=True)
             )
         dffn = jnp.concatenate(dffn, 0)
         grad_router = grad_router[:, :experts]
 
-        upstream = upstream.astype(F32)
-        weighted = ffn_gain * dffn
-        inner = jnp.mean(resid * weighted, axis=-1, keepdims=True)
-        dresid = upstream + norm_back(resid, scale_two, ffn_gain, dffn, inner)
-        grad_ffn_gain = jnp.sum(dffn * resid * scale_two, axis=0)
-        dbranch = jnp.concatenate(line_gather(dresid.astype(LOW)), 0)
-        sums[2] = shift(tie(sums[2], dbranch), 2)
-        mixture = [
-            lax.psum_scatter(tie(m, dbranch), "wshard", tiled=True).astype(F32) for m in mixture
-        ]
-        grad_out = t_mm(attended, dbranch)
-        dattended = mm_t(dbranch, w_out).astype(LOW)
+        piece_type = jax.ShapeDtypeStruct((own, cols), LOW)
+        dresid, dbranch, grad_ffn_gain, *dattended = out_call(
+            out_back_kernel,
+            "out_back",
+            arrived,
+            [dffn, resid, upstream, ffn_gain[None]],
+            full_out,
+            orders,
+            [
+                jax.ShapeDtypeStruct((own, width), F32),
+                jax.ShapeDtypeStruct((own, width), LOW),
+                jax.ShapeDtypeStruct((1, width), F32),
+            ]
+            + [piece_type] * n_w,
+        )
+        dattended = [shift(x, n_w - r) if r else x for r, x in enumerate(dattended)]
+        dattended = jnp.concatenate(dattended, 0)
+        third, fourth = jnp.split(sums[3], 2, 0)
+        third = shift(third, 3)
         dq, dk, dv, inners, grad_gains = attention(dattended.reshape(n_w, micro, rows, cols))
+        dbranch, inners, mixture, third = both(dbranch, inners, mixture, third)
+        mixture = [lax.psum_scatter(m, "wshard", tiled=True).astype(F32) for m in mixture]
+        (grad_out,) = out_call(
+            out_grad_kernel,
+            "out_grad",
+            arrived,
+            [dbranch] + attended,
+            [],
+            orders,
+            [jax.ShapeDtypeStruct((width, width), LOW)],
+        )
         inners = line_sum(jnp.sum(inners, 0).reshape(-1, 2).T, shard) / width
+        inners, fourth = both(inners, fourth)
+        fourth = shift(fourth, 3)
         inners = inners.reshape(2, -1).T
         flat = projected.reshape(-1, 3 * cols)
         dproj = jnp.concatenate(
@@ -693,31 +879,36 @@
             + [dv.reshape(-1, cols)],
             1,
         )
-        dnormed = tie(mm_t(dproj, w_heads).astype(LOW), sums[2])
+        dnormed = mm_t(dproj, w_heads).astype(LOW)
+        dnormed, fourth = both(dnormed, fourth)
+        sums[3] = jnp.concatenate([third, fourth], 0)
         dnormed = dnormed.reshape(n_w, own, width)
         dnormed = line_scatter([dnormed[r] for r in range(n_w)])
+        dnormed, sums[2], grad_out, dproj = both(dnormed, sums[2], grad_out, dproj)
+        sums[2] = shift(sums[2], 2)
+        small = width // (n_e * n_w)
+        out_part = hyper_scatter(grad_out.reshape(n_e, n_w * small, width), me, LOW, nd)
+        out_part = out_part.reshape(n_w, small, width)
+        out_rows = 0.0
+        for k in range(n_w):
+            block = lax.dynamic_index_in_dim(out_part, (shard + k) % n_w, 0, keepdims=False)
+            out_rows = out_rows + (shift(block, k) if k else block).astype(F32)
         inner = jnp.mean(tokens * (attn_gain * dnormed), axis=-1, keepdims=True)
         dx = norm_back(tokens, scale_one, attn_gain, dnormed, inner)
         grad_in = (dresid + dx).astype(LOW)
         mixture = jnp.concatenate(mixture, 0)
         hidden_out = (resid + mixture).astype(LOW)
-        out_gate_up, out_down = unpack(sums, shard, local_experts)
         grad_qkv = t_mm(normed_all, dproj)
         grad_attn_gain = jnp.sum(grad_qkv * w_heads.astype(F32), axis=1) / attn_gain
 
-        small = width // (n_e * n_w)
         qkv = hyper_scatter(grad_qkv.reshape(n_e, n_w * small, 3 * cols), me, LOW, nd)
-        qkv_rows = qkv.reshape(n_w, small, 3 * cols)
-        qkv = line_exchange(
-            lambda t: lax.dynamic_index_in_dim(qkv_rows, t, 0, keepdims=False), shard
-        )
-        qkv = qkv.reshape(n_w, small, 3, cols).transpose(1, 2, 0, 3)
-        out_qkv = qkv.reshape(small, 3 * width).astype(F32)
-        to_rows = [
-            (i * n_w + w, w * n_e + i) for i in range(n_e) for w in range(n_w)
-        ]
-        out_rows = hyper_scatter(grad_out.reshape(n_e, small, width), me, LOW)
-        out_rows = joint(out_rows, to_rows).astype(F32)
+        qkv, sums[2] = both(qkv.reshape(n_w, small, 3 * cols), sums[2])
+        arrivals = []
+        for k in range(n_w):
+            rows_k = lax.dynamic_index_in_dim(qkv, (shard + k) % n_w, 0, keepdims=False)
+            arrivals.append(shift(rows_k, k) if k else rows_k)
+        out_qkv = spread(arrivals, shard)
+        out_gate_up, out_down = unpack(sums, shard, local_experts)
         def all_scatter(x):
             x = x.reshape(-1, n_e, n_w * small).transpose(1, 0, 2)
             x = hyper_scatter(x, me, F32).reshape(-1, n_w, small)
@@ -729,8 +920,9 @@
 
         gains = jnp.zeros((2, width), F32)
         gains = lax.dynamic_update_slice(gains, jnp.sum(grad_gains, 0), (0, shard * cols))
-        pack = [gains, grad_attn_gain[None], grad_ffn_gain[None], grad_router.T]
-        pack = all_scatter(jnp.concatenate(pack, 0))
+        pack = [gains, grad_attn_gain[None], grad_ffn_gain, grad_router.T]
+        pack, dnormed = both(jnp.concatenate(pack, 0), dnormed)
+        pack = all_scatter(pack)
         return (
             hidden_out.reshape(micro, 1, rows, width),
             grad_in.reshape(micro, 1, rows, width),

time: 1070 us -> 985 us (0.921)
  starting transfers between devices: 207 us -> 111 us
  Pallas kernels: 147 us -> 173 us
  matrix products: 30.5 us -> 14.3 us
    ppermute x30 -> x38, waiting for transfers between devices: 86.9 us -> 156 us  [swap(): return lax.ppermute(x, 'expert', [(i, i ^ d) for i in range(n_e)])]
    ppermute x33 -> x41, starting transfers between devices: 114 us -> 68.5 us  [shift(): return lax.ppermute(x, 'wshard', [(j, (j + s) % n_w) for j in range(n_w)])]
    ppermute x33 -> x41, waiting for transfers between devices: 294 us -> 252 us  [shift(): return lax.ppermute(x, 'wshard', [(j, (j + s) % n_w) for j in range(n_w)])]
    ppermute x30 -> x38, starting transfers between devices: 60.2 us -> 33.3 us  [swap(): return lax.ppermute(x, 'expert', [(i, i ^ d) for i in range(n_e)])]
    pallas_call x2 -> x6, Pallas kernels: 40.9 us -> 67.4 us  [the longest x2 40.8 us: grad_pass(): pl.pallas_call(functools.partial(grad_kernel, len(parts)), grid_spec=pltp...]
    ppermute x6, starting transfers between devices: 32.2 us -> 8.55 us  [across(): return lax.ppermute(x, 'wshard', [(j, j ^ r) for j in range(n_w)])]
    ppermute x6, waiting for transfers between devices: 102 us -> 83.4 us  [across(): return lax.ppermute(x, 'wshard', [(j, j ^ r) for j in range(n_w)])]
    dot_general x6 -> x3, matrix products: 30.5 us -> 14.3 us  [dot(): return lax.dot_general(a, b, (dims, ((), ())), preferred_element_type=F32)]
  transfers between devices with their start and end apart: 73 -> 89, of which waited for: 32 -> 45; matrix products, arithmetic and copies ran while one was open for 17% -> 14% of each run, Pallas kernels for 5% -> 11%
where the time goes in v4:
time: 985 us; the launch traced here: 976 us
  waiting for transfers between devices  492 us (50%)
  Pallas kernels  173 us (18%)
  starting transfers between devices  111 us (11%)
  local copies, waits for them, and re-layouts  99.2 us (10%)
  other arithmetic  71.6 us (7%)
  between operations  15.7 us (2%)
  matrix products  14.3 us (1%)
    ppermute x41, waiting for transfers between devices, shift(): return lax.ppermute(x, 'wshard', [(j, (j + s) % n_w) for j in range(n_w)])  252 us
    ppermute x38, waiting for transfers between devices, swap(): return lax.ppermute(x, 'expert', [(i, i ^ d) for i in range(n_e)])  156 us
    ppermute x6, waiting for transfers between devices, across(): return lax.ppermute(x, 'wshard', [(j, j ^ r) for j in range(n_w)])  83.4 us
    pallas_call x1, Pallas kernels, expert_pass(): pl.pallas_call(functools.partial(expert_kernel, experts, n_w), grid_spec=...  70 us
    ppermute x41, starting transfers between devices, shift(): return lax.ppermute(x, 'wshard', [(j, (j + s) % n_w) for j in range(n_w)])  68.5 us
    pallas_call x2, Pallas kernels, grad_pass(): pl.pallas_call(functools.partial(grad_kernel, len(parts)), grid_spec=pltp...  40.8 us
    unnamed x178, local copies, waits for them, and re-layouts  36.8 us
    ppermute x38, starting transfers between devices, swap(): return lax.ppermute(x, 'expert', [(i, i ^ d) for i in range(n_e)])  33.3 us
  transfers between devices with their start and end apart: 89, of which 45 were waited for; matrix products, arithmetic and copies ran while one was open for 14% of the time, Pallas kernels for 11%

profile of v4, /device:TPU:0, one launch (start us, length us, event | category | flops | bytes accessed | tf_op | source)
XLA Modules:
  0.0 976.1 jit_solution(4063527417957827088)
XLA Ops:
  41.7 14.4 %collective-permute-done.3 = bf16[64,1536]{1,0:T(8,128)(2,1)} collective-permute-done((bf16[64,1536]{1,0:T(8,128)(2,1)}, bf16[64,1536]{1,0:T(8,128)(2,1)}, u32[]{:S(2)}, u32[]{:S(2)}) %collective-permute-start.3) | collective-permute-done | bytes 196640 | tf_op jit(solution)/shard_map/ppermute | solution.py:489
  58.5 15.1 %collective-permute-done.4 = bf16[64,1536]{1,0:T(8,128)(2,1)} collective-permute-done((bf16[64,1536]{1,0:T(8,128)(2,1)}, bf16[64,1536]{1,0:T(8,128)(2,1)}, u32[]{:S(2)}, u32[]{:S(2)}) %collective-permute-start.4) | collective-permute-done | bytes 196640 | tf_op jit(solution)/shard_map/ppermute | solution.py:489
  98.8 7.4 collective-permute-done.7
  107.6 6.4 collective-permute-done.9
  124.4 7.0 collective-permute-done.15
  136.9 21.5 %collective-permute-done.17 = bf16[256,1536]{1,0:T(8,128)(2,1)S(1)} collective-permute-done((bf16[256,1536]{1,0:T(8,128)(2,1)S(1)}, bf16[256,1536]{1,0:T(8,128)(2,1)S(1)}, u32[]{:S(2)}, u32[]{:S(2)}) %collective-permute-start.17) | collective-permute-done | bytes 786464 | tf_op jit(solution)/shard_map/ppermute | solution.py:489
  164.4 19.1 %collective-permute-done.23 = bf16[2,4,64,1024]{3,2,1,0:T(8,128)(2,1)} collective-permute-done((bf16[2,4,64,1024]{3,2,1,0:T(8,128)(2,1)S(1)}, bf16[2,4,64,1024]{3,2,1,0:T(8,128)(2,1)}, u32[]{:S(2)}, u32[]{:S(2)}) %collective-permute-start.23) | collective-permute-done | bytes 1048608 | tf_op jit(solution)/shard_map/ppermute | solution.py:486
  209.5 6.4 attention.1
  238.1 6.8 out.1
  248.9 12.6 %collective-permute-done.28 = bf16[128,2048]{1,0:T(8,128)(2,1)} collective-permute-done((bf16[128,2048]{1,0:T(8,128)(2,1)}, bf16[128,2048]{1,0:T(8,128)(2,1)}, u32[]{:S(2)}, u32[]{:S(2)}) %collective-permute-start.28) | collective-permute-done | bytes 524320 | tf_op jit(solution)/shard_map/ppermute | solution.py:505
  262.9 9.8 %collective-permute-done.29 = bf16[128,2048]{1,0:T(8,128)(2,1)S(1)} collective-permute-done((bf16[128,2048]{1,0:T(8,128)(2,1)}, bf16[128,2048]{1,0:T(8,128)(2,1)S(1)}, u32[]{:S(2)}, u32[]{:S(2)}) %collective-permute-start.29) | collective-permute-done | bytes 524320 | tf_op jit(solution)/shard_map/ppermute | solution.py:505
  272.8 21.1 %collective-permute-done.30 = bf16[128,2048]{1,0:T(8,128)(2,1)S(1)} collective-permute-done((bf16[128,2048]{1,0:T(8,128)(2,1)}, bf16[128,2048]{1,0:T(8,128)(2,1)S(1)}, u32[]{:S(2)}, u32[]{:S(2)}) %collective-permute-start.30) | collective-permute-done | bytes 524320 | tf_op jit(solution)/shard_map/ppermute | solution.py:505
  296.1 44.4 %collective-permute-done.31 = bf16[256,2048]{1,0:T(8,128)(2,1)S(1)} collective-permute-done((bf16[256,2048]{1,0:T(8,128)(2,1)S(1)}, bf16[256,2048]{1,0:T(8,128)(2,1)S(1)}, u32[]{:S(2)}, u32[]{:S(2)}) %collective-permute-start.31) | collective-permute-done | bytes 1048608 | tf_op jit(solution)/shard_map/ppermute | solution.py:486
  364.9 62.3 %collective-permute-done.36 = bf16[256,1536]{1,0:T(8,128)(2,1)} collective-permute-done((bf16[256,1536]{1,0:T(8,128)(2,1)}, bf16[256,1536]{1,0:T(8,128)(2,1)}, u32[]{:S(2)}, u32[]{:S(2)}) %collective-permute-start.36) | collective-permute-done | bytes 786464 | tf_op jit(solution)/shard_map/ppermute | solution.py:489
  445.5 70.0 %expert_pass.1 = (bf16[2048,2048]{1,0:T(8,128)(2,1)}, bf16[2048,2048]{1,0:T(8,128)(2,1)}, bf16[2048,2048]{1,0:T(8,128)(2,1)}, bf16[2048,128]{1,0:T(8,128)(2,1)},...) custom-call(s32[4]{0:T(128)} %and_select_fusion.1.at_ref, ...), custom_call_target="tpu_custom_call" | custom-call | flops 1 | bytes 1 | tf_op jit(solution)/shard_map/expert_pass/pallas_call | solution.py:401
  522.3 19.2 %grad_pass.3 = bf16[4,512,1536]{2,1,0:T(8,128)(2,1)} custom-call(s32[1]{0:T(128)} %bitcast.75.shard_ref, bf16[2048,2048]{1,0:T(8,128)(2,1)} %constant_dynamic-update-slice_fusion.4.x_ref.refs_0_, bf16[2048,2048]{1,0:T(8,128)(2,1)} %get-tuple-element.151.refs_1_, bf16[2048,1024]{1,0:T(8,128)(2,1)} %get-tuple-element.157.refs_2_, ...), custom_call_target="tpu_custom_call" | custom-call | flops 12884901888 | bytes 37748736 | tf_op jit(solution)/shard_map/grad_pass/pallas_call | solution.py:463
  541.5 21.6 %grad_pass.2 = (bf16[4,512,1536]{2,1,0:T(8,128)(2,1)}, f32[2048,128]{1,0:T(8,128)}) custom-call(s32[1]{0:T(128)} %bitcast.75.shard_ref, bf16[2048,2048]{1,0:T(8,128)(2,1)} %constant_dynamic-update-slice_fusion.4.x_ref.refs_0_, bf16[2048,2048]{1,0:T(8,128)(2,1)} %get-tuple-element.151.refs_1_, bf16[2048,1024]{1,0:T(8,128)(2,1)} %get-tuple-element.152.refs_2_, ...), custom_call_target="tpu_custom_call" | custom-call | flops 12884901888 | bytes 37748736 | tf_op jit(solution)/shard_map/grad_pass/pallas_call | solution.py:463
  582.8 14.7 %collective-permute-done.44 = bf16[256,2048]{1,0:T(8,128)(2,1)S(1)} collective-permute-done((bf16[256,2048]{1,0:T(8,128)(2,1)S(1)}, bf16[256,2048]{1,0:T(8,128)(2,1)S(1)}, u32[]{:S(2)}, u32[]{:S(2)}) %collective-permute-start.44) | collective-permute-done | bytes 1048608 | tf_op jit(solution)/shard_map/ppermute | solution.py:486
  600.3 20.0 %collective-permute-done.47.refs_1_ = bf16[512,1536]{1,0:T(8,128)(2,1)S(1)} collective-permute-done((bf16[512,1536]{1,0:T(8,128)(2,1)S(1)}, bf16[512,1536]{1,0:T(8,128)(2,1)S(1)}, u32[]{:S(2)}, u32[]{:S(2)}) %collective-permute-start.47) | collective-permute-done | bytes 1572896 | tf_op jit(solution)/shard_map/ppermute | solution.py:489
  630.2 9.5 collective-permute-done.50
  639.7 30.3 %collective-permute-done.49 = bf16[128,2048]{1,0:T(8,128)(2,1)S(1)} collective-permute-done((bf16[128,2048]{1,0:T(8,128)(2,1)S(1)}, bf16[128,2048]{1,0:T(8,128)(2,1)S(1)}, u32[]{:S(2)}, u32[]{:S(2)}) %collective-permute-start.49) | collective-permute-done | bytes 524320 | tf_op jit(solution)/shard_map/ppermute | solution.py:505
  671.5 9.1 out_back.1
  680.6 14.7 %collective-permute-start.53 = (bf16[128,512]{1,0:T(8,128)(2,1)}, bf16[128,512]{1,0:T(8,128)(2,1)S(1)}, u32[]{:S(2)}, u32[]{:S(2)}) collective-permute-start(bf16[128,512]{1,0:T(8,128)(2,1)} %get-tuple-element.178), channel_id=1, source_target_pairs={{0,1},{1,2},{2,3},{3,0},{4,5},{5,6},{6,7},{7,4},{8,9},{9,10},{10,1... | collective-permute-start | bytes 393224 | tf_op jit(solution)/shard_map/ppermute | solution.py:489
  707.2 12.7 %attention_back.1 = (f32[4,2,64,512]{3,2,1,0:T(8,128)S(1)}, f32[4,2,64,512]{3,2,1,0:T(8,128)S(1)}, bf16[4,2,64,512]{3,2,1,0:T(8,128)(2,1)S(1)}, f32[4,4,2,64,2]{4,3,2,1,0:T(8,128)S(1)}, f32[2,2,512]{2,1,0:T(2,128)S(1)}) custom-call(f32[4,2,64,1536]{3,2,1,0:T(8,128)S(1)} %bitcast.326, f32[4,2,64,1536]{3,2,1,0:T(8,128)S(1)} %bitcast.327, ...), custom_call_target="tpu_custom_call" | custom-call | flops 1 | bytes 1 | tf_op jit(solution)/shard_map/attention_back/pallas_call | solution.py:166
  737.7 6.8 convolution_convert_fusion
  744.5 8.8 collective-permute-done.58
  757.5 8.2 out_grad.1
  769.5 29.4 %collective-permute-done.60 = bf16[128,2048]{1,0:T(8,128)(2,1)} collective-permute-done((bf16[128,2048]{1,0:T(8,128)(2,1)}, bf16[128,2048]{1,0:T(8,128)(2,1)}, u32[]{:S(2)}, u32[]{:S(2)}) %collective-permute-start.60) | collective-permute-done | bytes 524320 | tf_op jit(solution)/shard_map/ppermute | solution.py:489
  845.2 12.2 %collective-permute-done.71 = bf16[2,256,768]{2,1,0:T(8,128)(2,1)S(1)} collective-permute-done((bf16[2,256,768]{2,1,0:T(8,128)(2,1)S(1)}, bf16[2,256,768]{2,1,0:T(8,128)(2,1)S(1)}, u32[]{:S(2)}, u32[]{:S(2)}) %collective-permute-start.71) | collective-permute-done | bytes 786464 | tf_op jit(solution)/shard_map/ppermute | solution.py:486
  873.5 21.6 %collective-permute-done.70 = bf16[256,768]{1,0:T(8,128)(2,1)S(1)} collective-permute-done((bf16[256,768]{1,0:T(8,128)(2,1)S(1)}, bf16[256,768]{1,0:T(8,128)(2,1)S(1)}, u32[]{:S(2)}, u32[]{:S(2)}) %collective-permute-start.70) | collective-permute-done | bytes 393248 | tf_op jit(solution)/shard_map/ppermute | solution.py:486
  898.6 24.7 %collective-permute-done.73.refs_2_ = bf16[512,1536]{1,0:T(8,128)(2,1)S(1)} collective-permute-done((bf16[512,1536]{1,0:T(8,128)(2,1)S(1)}, bf16[512,1536]{1,0:T(8,128)(2,1)S(1)}, u32[]{:S(2)}, u32[]{:S(2)}) %collective-permute-start.73) | collective-permute-done | bytes 1572896 | tf_op jit(solution)/shard_map/ppermute | solution.py:489
  948.2 18.9 %collective-permute-done.83 = bf16[64,2048]{1,0:T(8,128)(2,1)} collective-permute-done((bf16[64,2048]{1,0:T(8,128)(2,1)}, bf16[64,2048]{1,0:T(8,128)(2,1)}, u32[]{:S(2)}, u32[]{:S(2)}) %collective-permute-start.83) | collective-permute-done | bytes 262176 | tf_op jit(solution)/shard_map/ppermute | solution.py:489
  (519 shorter events, 353.8 us)
Async XLA Ops:
  7.2 216.2 %all-gather.5.cloned.1.call-start = ((), (), s32[]{:S(2)}) async-start(), calls=%async_computation.4 | async-start | bytes 2949120 | tf_op jit(solution)/shard_map/all_gather | solution.py:659
  10.8 68.5 %collective-permute-start = (bf16[128,2048]{1,0:T(8,128)(2,1)}, bf16[128,2048]{1,0:T(8,128)(2,1)}, u32[]{:S(2)}, u32[]{:S(2)}) collective-permute-start(bf16[128,2048]{1,0:T(8,128)(2,1)} %fusion.16), channel_id=1, source_target_pairs={{0,3},{1,0},{2,1},{3,2},{4,7},{5,4},{6,5},{7,6},{8,11},{9,8},{10,9... | collective-permute-start | bytes 1572872 | tf_op jit(solution)/shard_map/ppermute | solution.py:489
  15.8 63.4 %collective-permute-start.1 = (bf16[128,2048]{1,0:T(8,128)(2,1)}, bf16[128,2048]{1,0:T(8,128)(2,1)}, u32[]{:S(2)}, u32[]{:S(2)}) collective-permute-start(bf16[128,2048]{1,0:T(8,128)(2,1)} %fusion.16), channel_id=1, source_target_pairs={{0,2},{1,3},{2,0},{3,1},{4,6},{5,7},{6,4},{7,5},{8,10},{9,11},{10,... | collective-permute-start | bytes 1572872 | tf_op jit(solution)/shard_map/ppermute | solution.py:489
  15.8 63.4 %collective-permute-start.2 = (bf16[128,2048]{1,0:T(8,128)(2,1)}, bf16[128,2048]{1,0:T(8,128)(2,1)}, u32[]{:S(2)}, u32[]{:S(2)}) collective-permute-start(bf16[128,2048]{1,0:T(8,128)(2,1)} %fusion.16), channel_id=1, source_target_pairs={{0,1},{1,2},{2,3},{3,0},{4,5},{5,6},{6,7},{7,4},{8,9},{9,10},{10,1... | collective-permute-start | bytes 1572872 | tf_op jit(solution)/shard_map/ppermute | solution.py:489
  25.0 31.2 %collective-permute-start.3 = (bf16[64,1536]{1,0:T(8,128)(2,1)}, bf16[64,1536]{1,0:T(8,128)(2,1)}, u32[]{:S(2)}, u32[]{:S(2)}) collective-permute-start(bf16[64,1536]{1,0:T(8,128)(2,1)} %get-tuple-element.342), channel_id=1, source_target_pairs={{0,1},{1,2},{2,3},{3,0},{4,5},{5,6},{6,7},{7,4},{8,9},{9,10},{10,1... | collective-permute-start | bytes 589832 | tf_op jit(solution)/shard_map/ppermute | solution.py:489
  27.4 46.1 %collective-permute-start.4 = (bf16[64,1536]{1,0:T(8,128)(2,1)}, bf16[64,1536]{1,0:T(8,128)(2,1)}, u32[]{:S(2)}, u32[]{:S(2)}) collective-permute-start(bf16[64,1536]{1,0:T(8,128)(2,1)} %get-tuple-element.341), channel_id=1, source_target_pairs={{0,2},{1,3},{2,0},{3,1},{4,6},{5,7},{6,4},{7,5},{8,10},{9,11},{10,... | collective-permute-start | bytes 589832 | tf_op jit(solution)/shard_map/ppermute | solution.py:489
  121.6 36.8 %collective-permute-start.17 = (bf16[256,1536]{1,0:T(8,128)(2,1)S(1)}, bf16[256,1536]{1,0:T(8,128)(2,1)S(1)}, u32[]{:S(2)}, u32[]{:S(2)}) collective-permute-start(bf16[256,1536]{1,0:T(8,128)(2,1)S(1)} %get-tuple-element.310), channel_id=1, source_target_pairs={{0,2},{1,3},{2,0},{3,1},{4,6},{5,7},{6,4},{7,5},{8,10},{9,11},{10,... | collective-permute-start | bytes 2359304 | tf_op jit(solution)/shard_map/ppermute | solution.py:489
  161.9 182.9 %all-gather.7.cloned.1.call-start = ((), (), s32[]{:S(2)}) async-start(), calls=%async_computation.5 | async-start | bytes 11796480 | tf_op jit(solution)/shard_map/all_gather | solution.py:662
  223.5 500.1 %reduce-scatter.3.cloned.1.call-start = ((), (), s32[]{:S(2)}) async-start(), calls=%async_computation.2 | async-start | bytes 10485760 | tf_op jit(solution)/shard_map/reduce_scatter | solution.py:827
  248.4 45.5 %collective-permute-start.30 = (bf16[128,2048]{1,0:T(8,128)(2,1)}, bf16[128,2048]{1,0:T(8,128)(2,1)S(1)}, u32[]{:S(2)}, u32[]{:S(2)}) collective-permute-start(bf16[128,2048]{1,0:T(8,128)(2,1)} %get-tuple-element.130), channel_id=1, source_target_pairs={{0,2},{1,3},{2,0},{3,1},{4,6},{5,7},{6,4},{7,5},{8,10},{9,11},{10,... | collective-permute-start | bytes 1572872 | tf_op jit(solution)/shard_map/ppermute | solution.py:505
  294.1 46.5 %collective-permute-start.31 = (bf16[256,2048]{1,0:T(8,128)(2,1)S(1)}, bf16[256,2048]{1,0:T(8,128)(2,1)S(1)}, u32[]{:S(2)}, u32[]{:S(2)}) collective-permute-start(bf16[256,2048]{1,0:T(8,128)(2,1)S(1)} %pad_maximum_fusion.13), channel_id=1, source_target_pairs={{0,8},{4,12},{8,0},{12,4},{16,24},{20,28},{24,16},{28,20},{1,9},{5... | collective-permute-start | bytes 3145736 | tf_op jit(solution)/shard_map/ppermute | solution.py:486
  295.5 46.7 %collective-permute-start.32 = (bf16[256,2048]{1,0:T(8,128)(2,1)S(1)}, bf16[256,2048]{1,0:T(8,128)(2,1)S(1)}, u32[]{:S(2)}, u32[]{:S(2)}) collective-permute-start(bf16[256,2048]{1,0:T(8,128)(2,1)S(1)} %pad_maximum_fusion.14), channel_id=1, source_target_pairs={{0,16},{4,20},{8,24},{12,28},{16,0},{20,4},{24,8},{28,12},{1,17},{... | collective-permute-start | bytes 3145736 | tf_op jit(solution)/shard_map/ppermute | solution.py:486
  296.1 62.0 %collective-permute-start.33 = (bf16[512,1536]{1,0:T(8,128)(2,1)}, bf16[512,1536]{1,0:T(8,128)(2,1)}, u32[]{:S(2)}, u32[]{:S(2)}) collective-permute-start(bf16[512,1536]{1,0:T(8,128)(2,1)} %pack.5), channel_id=1, source_target_pairs={{0,1},{1,2},{2,3},{3,0},{4,5},{5,6},{6,7},{7,4},{8,9},{9,10},{10,1... | collective-permute-start | bytes 4718600 | tf_op jit(solution)/shard_map/ppermute | solution.py:489
  358.2 71.6 %collective-permute-start.34 = (bf16[512,2048]{1,0:T(8,128)(2,1)}, bf16[512,2048]{1,0:T(8,128)(2,1)}, u32[]{:S(2)}, u32[]{:S(2)}) collective-permute-start(bf16[512,2048]{1,0:T(8,128)(2,1)} %pad_maximum_fusion.5), channel_id=1, source_target_pairs={{0,16},{4,20},{8,24},{12,28},{16,0},{20,4},{24,8},{28,12},{1,17},{... | collective-permute-start | bytes 6291464 | tf_op jit(solution)/shard_map/ppermute | solution.py:486
  359.6 70.2 %collective-permute-start.37 = (bf16[512,1536]{1,0:T(8,128)(2,1)}, bf16[512,1536]{1,0:T(8,128)(2,1)}, u32[]{:S(2)}, u32[]{:S(2)}) collective-permute-start(bf16[512,1536]{1,0:T(8,128)(2,1)} %pack.7), channel_id=1, source_target_pairs={{0,3},{1,0},{2,1},{3,2},{4,7},{5,4},{6,5},{7,6},{8,11},{9,8},{10,9... | collective-permute-start | bytes 4718600 | tf_op jit(solution)/shard_map/ppermute | solution.py:489
  361.9 65.4 %collective-permute-start.36 = (bf16[256,1536]{1,0:T(8,128)(2,1)}, bf16[256,1536]{1,0:T(8,128)(2,1)}, u32[]{:S(2)}, u32[]{:S(2)}) collective-permute-start(bf16[256,1536]{1,0:T(8,128)(2,1)} %get-tuple-element.148), channel_id=1, source_target_pairs={{0,2},{1,3},{2,0},{3,1},{4,6},{5,7},{6,4},{7,5},{8,10},{9,11},{10,... | collective-permute-start | bytes 2359304 | tf_op jit(solution)/shard_map/ppermute | solution.py:489
  361.9 80.5 %collective-permute-start.35 = (bf16[512,2048]{1,0:T(8,128)(2,1)}, bf16[512,2048]{1,0:T(8,128)(2,1)}, u32[]{:S(2)}, u32[]{:S(2)}) collective-permute-start(bf16[512,2048]{1,0:T(8,128)(2,1)} %pad_maximum_fusion.6), channel_id=1, source_target_pairs={{0,8},{4,12},{8,0},{12,4},{16,24},{20,28},{24,16},{28,20},{1,9},{5... | collective-permute-start | bytes 6291464 | tf_op jit(solution)/shard_map/ppermute | solution.py:486
  520.3 47.8 %collective-permute-start.42 = (bf16[512,2048]{1,0:T(8,128)(2,1)}, bf16[512,2048]{1,0:T(8,128)(2,1)S(1)}, u32[]{:S(2)}, u32[]{:S(2)}) collective-permute-start(bf16[512,2048]{1,0:T(8,128)(2,1)} %get-tuple-element.283), channel_id=1, source_target_pairs={{0,16},{4,20},{8,24},{12,28},{16,0},{20,4},{24,8},{28,12},{1,17},{... | collective-permute-start | bytes 6291464 | tf_op jit(solution)/shard_map/ppermute | solution.py:486
  520.7 47.5 %collective-permute-start.43 = (bf16[512,2048]{1,0:T(8,128)(2,1)}, bf16[512,2048]{1,0:T(8,128)(2,1)S(1)}, u32[]{:S(2)}, u32[]{:S(2)}) collective-permute-start(bf16[512,2048]{1,0:T(8,128)(2,1)} %get-tuple-element.282), channel_id=1, source_target_pairs={{0,8},{4,12},{8,0},{12,4},{16,24},{20,28},{24,16},{28,20},{1,9},{5... | collective-permute-start | bytes 6291464 | tf_op jit(solution)/shard_map/ppermute | solution.py:486
  581.5 38.8 %collective-permute-start.47 = (bf16[512,1536]{1,0:T(8,128)(2,1)S(1)}, bf16[512,1536]{1,0:T(8,128)(2,1)S(1)}, u32[]{:S(2)}, u32[]{:S(2)}) collective-permute-start(bf16[512,1536]{1,0:T(8,128)(2,1)S(1)} %get-tuple-element.275), channel_id=1, source_target_pairs={{0,1},{1,2},{2,3},{3,0},{4,5},{5,6},{6,7},{7,4},{8,9},{9,10},{10,1... | collective-permute-start | bytes 4718600 | tf_op jit(solution)/shard_map/ppermute | solution.py:489
  621.4 313.2 %reduce-scatter.5.cloned.1.call-start = ((), (), s32[]{:S(2)}) async-start(), calls=%async_computation.3 | async-start | bytes 2621440 | tf_op jit(solution)/shard_map/reduce_scatter | solution.py:853
  624.7 45.3 %collective-permute-start.49 = (bf16[128,2048]{1,0:T(8,128)(2,1)S(1)}, bf16[128,2048]{1,0:T(8,128)(2,1)S(1)}, u32[]{:S(2)}, u32[]{:S(2)}) collective-permute-start(bf16[128,2048]{1,0:T(8,128)(2,1)S(1)} %get-tuple-element.322), channel_id=1, source_target_pairs={{0,2},{1,3},{2,0},{3,1},{4,6},{5,7},{6,4},{7,5},{8,10},{9,11},{10,... | collective-permute-start | bytes 1572872 | tf_op jit(solution)/shard_map/ppermute | solution.py:505
  624.8 45.3 %collective-permute-start.48 = (bf16[128,2048]{1,0:T(8,128)(2,1)S(1)}, bf16[128,2048]{1,0:T(8,128)(2,1)S(1)}, u32[]{:S(2)}, u32[]{:S(2)}) collective-permute-start(bf16[128,2048]{1,0:T(8,128)(2,1)S(1)} %broadcast_select_fusion.2), channel_id=1, source_target_pairs={{0,1},{1,0},{2,3},{3,2},{4,5},{5,4},{6,7},{7,6},{8,9},{9,8},{10,11... | collective-permute-start | bytes 1572872 | tf_op jit(solution)/shard_map/ppermute | solution.py:505
  628.5 95.1 %collective-permute-start.54 = (bf16[256,1536]{1,0:T(8,128)(2,1)S(1)}, bf16[256,1536]{1,0:T(8,128)(2,1)}, u32[]{:S(2)}, u32[]{:S(2)}) collective-permute-start(bf16[256,1536]{1,0:T(8,128)(2,1)S(1)} %get-tuple-element.308), channel_id=1, source_target_pairs={{0,3},{1,0},{2,1},{3,2},{4,7},{5,4},{6,5},{7,6},{8,11},{9,8},{10,9... | collective-permute-start | bytes 2359304 | tf_op jit(solution)/shard_map/ppermute | solution.py:489
  756.8 42.1 %collective-permute-start.60 = (bf16[128,2048]{1,0:T(8,128)(2,1)}, bf16[128,2048]{1,0:T(8,128)(2,1)}, u32[]{:S(2)}, u32[]{:S(2)}) collective-permute-start(bf16[128,2048]{1,0:T(8,128)(2,1)} %get-tuple-element.300), channel_id=1, source_target_pairs={{0,2},{1,3},{2,0},{3,1},{4,6},{5,7},{6,4},{7,5},{8,10},{9,11},{10,... | collective-permute-start | bytes 1572872 | tf_op jit(solution)/shard_map/ppermute | solution.py:489
  756.8 42.1 %collective-permute-start.59 = (bf16[128,2048]{1,0:T(8,128)(2,1)}, bf16[128,2048]{1,0:T(8,128)(2,1)}, u32[]{:S(2)}, u32[]{:S(2)}) collective-permute-start(bf16[128,2048]{1,0:T(8,128)(2,1)} %get-tuple-element.298), channel_id=1, source_target_pairs={{0,1},{1,2},{2,3},{3,0},{4,5},{5,6},{6,7},{7,4},{8,9},{9,10},{10,1... | collective-permute-start | bytes 1572872 | tf_op jit(solution)/shard_map/ppermute | solution.py:489
  818.2 41.5 %collective-permute-start.77 = (bf16[2,2,256,2048]{3,2,1,0:T(8,128)(2,1)}, bf16[2,2,256,2048]{3,2,1,0:T(8,128)(2,1)}, u32[]{:S(2)}, u32[]{:S(2)}) collective-permute-start(bf16[2,2,256,2048]{3,2,1,0:T(8,128)(2,1)} %dynamic-slice_bitcast_fusion), channel_id=1, source_target_pairs={{0,4},{4,0},{8,12},{12,8},{16,20},{20,16},{24,28},{28,24},{1,5},{5... | collective-permute-start | bytes 12582920 | tf_op jit(solution)/shard_map/ppermute | solution.py:486
  842.6 80.8 %collective-permute-start.73 = (bf16[512,1536]{1,0:T(8,128)(2,1)S(1)}, bf16[512,1536]{1,0:T(8,128)(2,1)S(1)}, u32[]{:S(2)}, u32[]{:S(2)}) collective-permute-start(bf16[512,1536]{1,0:T(8,128)(2,1)S(1)} %copy-done.48), channel_id=1, source_target_pairs={{0,2},{1,3},{2,0},{3,1},{4,6},{5,7},{6,4},{7,5},{8,10},{9,11},{10,... | collective-permute-start | bytes 4718600 | tf_op jit(solution)/shard_map/ppermute | solution.py:489
  895.6 32.4 %collective-permute-start.81 = (bf16[256,1024]{1,0:T(8,128)(2,1)S(1)}, bf16[256,1024]{1,0:T(8,128)(2,1)S(1)}, u32[]{:S(2)}, u32[]{:S(2)}) collective-permute-start(bf16[256,1024]{1,0:T(8,128)(2,1)S(1)} %dynamic-slice_bitcast_fusion.5), channel_id=1, source_target_pairs={{0,8},{4,12},{8,0},{12,4},{16,24},{20,28},{24,16},{28,20},{1,9},{5... | collective-permute-start | bytes 1572872 | tf_op jit(solution)/shard_map/ppermute | solution.py:486
  897.0 31.3 %collective-permute-start.79 = (bf16[256,1024]{1,0:T(8,128)(2,1)S(1)}, bf16[256,1024]{1,0:T(8,128)(2,1)S(1)}, u32[]{:S(2)}, u32[]{:S(2)}) collective-permute-start(bf16[256,1024]{1,0:T(8,128)(2,1)S(1)} %dynamic-slice_bitcast_fusion.6), channel_id=1, source_target_pairs={{0,16},{4,20},{8,24},{12,28},{16,0},{20,4},{24,8},{28,12},{1,17},{... | collective-permute-start | bytes 1572872 | tf_op jit(solution)/shard_map/ppermute | solution.py:486
  930.0 37.1 %collective-permute-start.83 = (bf16[64,2048]{1,0:T(8,128)(2,1)}, bf16[64,2048]{1,0:T(8,128)(2,1)}, u32[]{:S(2)}, u32[]{:S(2)}) collective-permute-start(bf16[64,2048]{1,0:T(8,128)(2,1)} %get-tuple-element.321), channel_id=1, source_target_pairs={{0,2},{1,3},{2,0},{3,1},{4,6},{5,7},{6,4},{7,5},{8,10},{9,11},{10,... | collective-permute-start | bytes 786440 | tf_op jit(solution)/shard_map/ppermute | solution.py:489
  934.6 32.5 %collective-permute-start.82 = (bf16[64,2048]{1,0:T(8,128)(2,1)S(1)}, bf16[64,2048]{1,0:T(8,128)(2,1)}, u32[]{:S(2)}, u32[]{:S(2)}) collective-permute-start(bf16[64,2048]{1,0:T(8,128)(2,1)S(1)} %get-tuple-element.319), channel_id=1, source_target_pairs={{0,1},{1,2},{2,3},{3,0},{4,5},{5,6},{6,7},{7,4},{8,9},{9,10},{10,1... | collective-permute-start | bytes 786440 | tf_op jit(solution)/shard_map/ppermute | solution.py:489
  (133 other events, 1805.1 us)
Sparse Core Ops, SparseCore 0:
  162.1 48.5 all-gather.4
  223.6 116.6 all-gather.6
  621.6 84.8 reduce-scatter.2
  812.1 55.4 reduce-scatter.4

commit v5 on v4

--- a/solution.py
+++ b/solution.py
@@ -436,10 +436,10 @@
     out_ref[0, :, : 2 * hidden] = up.astype(out_ref.dtype)
     out_ref[0, :, 2 * hidden :] = down.astype(out_ref.dtype)
     if with_router:
-        refs[-1][...] = router
-
-
-def grad_pass(parts, shard, n_w, kind):
+        refs[-1][0] = router
+
+
+def grad_pass(parts, shard, n_w, kind, first, count):
     width = parts[0][0].shape[1]
     hidden = parts[0][3].shape[1]
     cols = width // n_w
@@ -447,28 +447,28 @@
     specs = []
     for part in parts:
         n = part[0].shape[0]
-        column = pl.BlockSpec((n, cols), lambda i, at: (0, lax.rem(at[0] + i, n_w)))
+        column = pl.BlockSpec((n, cols), lambda i, at: (0, lax.rem(at[0] + first + i, n_w)))
         specs += [column, column]
         for a in part[2:]:
             specs.append(
                 pl.BlockSpec(a.shape, lambda i, at: (0, 0), pipeline_mode=pl.Buffered(1))
             )
     out_specs = [pl.BlockSpec((1, cols, 3 * hidden), lambda i, at: (i, 0, 0))]
-    outs = [jax.ShapeDtypeStruct((n_w, cols, 3 * hidden), kind)]
+    outs = [jax.ShapeDtypeStruct((count, cols, 3 * hidden), kind)]
     if len(parts[0]) > 4:
         lanes = parts[0][4].shape[1]
-        out_specs.append(pl.BlockSpec((cols, lanes), lambda i, at: (lax.rem(at[0] + i, n_w), 0)))
-        outs.append(jax.ShapeDtypeStruct((width, lanes), F32))
+        out_specs.append(pl.BlockSpec((1, cols, lanes), lambda i, at: (i, 0, 0)))
+        outs.append(jax.ShapeDtypeStruct((count, cols, lanes), F32))
     return tuple(
         pl.pallas_call(
             functools.partial(grad_kernel, len(parts)),
             grid_spec=pltpu.PrefetchScalarGridSpec(
-                num_scalar_prefetch=1, grid=(n_w,), in_specs=specs, out_specs=out_specs
+                num_scalar_prefetch=1, grid=(count,), in_specs=specs, out_specs=out_specs
             ),
             out_shape=outs,
             compiler_params=pltpu.CompilerParams(vmem_limit_bytes=56 * 1024 * 1024),
             cost_estimate=pl.CostEstimate(
-                flops=6 * tokens * width * hidden,
+                flops=6 * tokens * cols * count * hidden,
                 bytes_accessed=4 * tokens * width + 20 * width * hidden,
                 transcendentals=0,
             ),
@@ -670,7 +670,6 @@
         blocks, bank, dy_rows, pieces, out_slice = both(blocks, bank, rows_for(0), pieces, out_slice)
 
         full_out = line_gather(out_slice)
-        dy_rows = to_line(dy_rows)
         first, second = jnp.split(pieces[2], 2, 0)
         first = shift(first, 2)
         normed_all = jnp.concatenate(blocks, 0)
@@ -696,10 +695,15 @@
         for step_at, (d0, d1) in enumerate(zip(*ways)):
             full_out = [joined(full_out[0], d0, me), joined(full_out[1], d1, me)]
             if step_at == 0:
-                w_heads, full_out, first = both(w_heads, full_out, first)
+                w_heads, full_out, first, dy_rows = both(w_heads, full_out, first, dy_rows)
+                dy_rows = to_line(dy_rows)
+                break
         orders = [list(reversed(w)) for w in ways]
 
         projected = mm(normed_all, w_heads)
+        projected, full_out = both(projected, full_out)
+        for d0, d1 in list(zip(*ways))[1:]:
+            full_out = [joined(full_out[0], d0, me), joined(full_out[1], d1, me)]
         squares = jnp.sum(projected.reshape(-1, 3, cols)[:, :2] ** 2, axis=-1).T
         scales = lax.rsqrt(line_sum(squares, shard) / width + EPS)
         scales = scales.reshape(2, -1).T
@@ -805,29 +809,49 @@
                 passed.append([x] + rest)
             kind = LOW if rounds == 1 else F32
             def weight_grads():
-                ins = [[x, dy, dgu1, gated1, dlogits] for x, dy, dlogits, _, dgu1, _, gated1 in passed]
-                sib = grad_pass(ins, shard, n_w, kind)
-                ins = [[x, dy, dgu0, gated0] for x, dy, _, dgu0, _, gated0, _ in passed]
-                return sib + grad_pass(ins, shard, n_w, kind)
-
-            back, new = plane_scatter(back, weight_grads)
+                sib = [[x, dy, dgu1, gated1, dl] for x, dy, dl, _, dgu1, _, gated1 in passed]
+                own_half = [[x, dy, dgu0, gated0] for x, dy, _, dgu0, _, gated0, _ in passed]
+                early = grad_pass(sib, shard, n_w, kind, 1, 1)
+                early += grad_pass(own_half, shard, n_w, kind, 1, 1)
+                sent = None
+                if rounds == 1:
+                    sent = early[2][0].astype(F32) + swap(early[0][0], 1).astype(F32)
+                    sent = shift(sent.astype(LOW), 1)
+                middle = grad_pass(sib, shard, n_w, kind, 3, n_w - 2)
+                middle += grad_pass(own_half, shard, n_w, kind, 3, n_w - 2)
+                if rounds == 1:
+                    middle = (swap(middle[0], 1),) + middle[1:]
+                late = grad_pass(sib, shard, n_w, kind, 2, 1)
+                late += grad_pass(own_half, shard, n_w, kind, 2, 1)
+                return [early, middle, late], sent
+
+            back, (new, sent) = plane_scatter(back, weight_grads)
             grads = new if grads is None else jax.tree.map(jnp.add, grads, new)
-            grad_sib, grad_router, grad_own = grads
             if n == rounds - 1:
-                grad_sib = swap(grad_sib.astype(LOW), 1)
-                sums = [
-                    (grad_own[s].astype(F32) + grad_sib[s].astype(F32)).astype(LOW)
-                    for s in range(n_w)
-                ]
-                sums[1] = shift(sums[1], 1)
-                back, sums[1] = both(back, sums[1])
+                (sib1, router1, own1), (sib3, router3, own3), (sib2, router2, own2) = grads
+                sib2 = swap(sib2.astype(LOW), 1)
+                if sent is None:
+                    sent = own1[0].astype(F32) + swap(sib1[0].astype(LOW), 1).astype(F32)
+                    sent = shift(sent.astype(LOW), 1)
+                    sib3 = swap(sib3.astype(LOW), 1)
+
+                def added(a, b):
+                    return (a.astype(F32) + b.astype(F32)).astype(LOW)
+
+                sums = [added(own3[1], sib3[1]), sent, added(own2[0], sib2[0])]
+                sums.append(added(own3[0], sib3[0]))
+                third, fourth = jnp.split(sums[3], 2, 0)
+                third = shift(third, 3)
+                back, third = both(back, third)
+                grad_router = jnp.concatenate([router3[1:], router1, router2, router3[:1]], 0)
+                grad_router = jnp.roll(grad_router[..., :experts], shard, axis=0)
+                grad_router = grad_router.reshape(width, experts)
             back, mix = both(back, mix)
             dffn.append(pair_scatter(back, shard))
             mixture.append(
                 lax.psum_scatter(mix, "expert", axis_index_groups=same, tiled=True)
             )
         dffn = jnp.concatenate(dffn, 0)
-        grad_router = grad_router[:, :experts]
 
         piece_type = jax.ShapeDtypeStruct((own, cols), LOW)
         dresid, dbranch, grad_ffn_gain, *dattended = out_call(
@@ -846,11 +870,8 @@
         )
         dattended = [shift(x, n_w - r) if r else x for r, x in enumerate(dattended)]
         dattended = jnp.concatenate(dattended, 0)
-        third, fourth = jnp.split(sums[3], 2, 0)
-        third = shift(third, 3)
         dq, dk, dv, inners, grad_gains = attention(dattended.reshape(n_w, micro, rows, cols))
-        dbranch, inners, mixture, third = both(dbranch, inners, mixture, third)
-        mixture = [lax.psum_scatter(m, "wshard", tiled=True).astype(F32) for m in mixture]
+        dbranch, inners = both(dbranch, inners)
         (grad_out,) = out_call(
             out_grad_kernel,
             "out_grad",
@@ -884,7 +905,10 @@
         sums[3] = jnp.concatenate([third, fourth], 0)
         dnormed = dnormed.reshape(n_w, own, width)
         dnormed = line_scatter([dnormed[r] for r in range(n_w)])
-        dnormed, sums[2], grad_out, dproj = both(dnormed, sums[2], grad_out, dproj)
+        dnormed, sums[2], grad_out, dproj, mixture = both(
+            dnormed, sums[2], grad_out, dproj, mixture
+        )
+        mixture = [lax.psum_scatter(m, "wshard", tiled=True).astype(F32) for m in mixture]
         sums[2] = shift(sums[2], 2)
         small = width // (n_e * n_w)
         out_part = hyper_scatter(grad_out.reshape(n_e, n_w * small, width), me, LOW, nd)

time: 985 us -> 977 us (level)
  Pallas kernels: 173 us -> 194 us
  waiting for transfers between devices: 492 us -> 473 us
  starting transfers between devices: 111 us -> 97 us
    ppermute x41, waiting for transfers between devices: 252 us -> 227 us  [shift(): return lax.ppermute(x, 'wshard', [(j, (j + s) % n_w) for j in range(n_w)])]
    pallas_call x2 -> x6, Pallas kernels: 40.8 us -> 62.4 us  [grad_pass(): pl.pallas_call(functools.partial(grad_kernel, len(parts)), grid_spec=pltp...]
    ppermute x41, starting transfers between devices: 68.5 us -> 57.4 us  [shift(): return lax.ppermute(x, 'wshard', [(j, (j + s) % n_w) for j in range(n_w)])]
    ppermute x38 -> x40, waiting for transfers between devices: 156 us -> 163 us  [swap(): return lax.ppermute(x, 'expert', [(i, i ^ d) for i in range(n_e)])]
    ppermute x38 -> x40, starting transfers between devices: 33.3 us -> 31 us  [swap(): return lax.ppermute(x, 'expert', [(i, i ^ d) for i in range(n_e)])]
    unnamed x178 -> x170, local copies, waits for them, and re-layouts: 36.8 us -> 35.5 us
  transfers between devices with their start and end apart: 89 -> 91, of which waited for: 45 -> 43; matrix products, arithmetic and copies ran while one was open for 14% -> 15% of each run, Pallas kernels for 11% -> 12%
where the time goes in v5:
time: 977 us; the launch traced here: 968 us
  waiting for transfers between devices  473 us (48%)
  Pallas kernels  194 us (20%)
  starting transfers between devices  97 us (10%)
  local copies, waits for them, and re-layouts  96.4 us (10%)
  other arithmetic  75.3 us (8%)
  matrix products  16.7 us (2%)
  between operations  15.6 us (2%)
    ppermute x41, waiting for transfers between devices, shift(): return lax.ppermute(x, 'wshard', [(j, (j + s) % n_w) for j in range(n_w)])  227 us
    ppermute x40, waiting for transfers between devices, swap(): return lax.ppermute(x, 'expert', [(i, i ^ d) for i in range(n_e)])  163 us
    ppermute x6, waiting for transfers between devices, across(): return lax.ppermute(x, 'wshard', [(j, j ^ r) for j in range(n_w)])  82.8 us
    pallas_call x1, Pallas kernels, expert_pass(): pl.pallas_call(functools.partial(expert_kernel, experts, n_w), grid_spec=...  69.6 us
    pallas_call x6, Pallas kernels, grad_pass(): pl.pallas_call(functools.partial(grad_kernel, len(parts)), grid_spec=pltp...  62.4 us
    ppermute x41, starting transfers between devices, shift(): return lax.ppermute(x, 'wshard', [(j, (j + s) % n_w) for j in range(n_w)])  57.4 us
    unnamed x170, local copies, waits for them, and re-layouts  35.5 us
    ppermute x40, starting transfers between devices, swap(): return lax.ppermute(x, 'expert', [(i, i ^ d) for i in range(n_e)])  31 us
  transfers between devices with their start and end apart: 91, of which 43 were waited for; matrix products, arithmetic and copies ran while one was open for 15% of the time, Pallas kernels for 12%

profile of v5, /device:TPU:0, one launch (start us, length us, event | category | flops | bytes accessed | tf_op | source)
XLA Modules:
  0.0 967.5 jit_solution(12871254050065844494)
XLA Ops:
  41.6 14.6 %collective-permute-done.3 = bf16[64,1536]{1,0:T(8,128)(2,1)} collective-permute-done((bf16[64,1536]{1,0:T(8,128)(2,1)}, bf16[64,1536]{1,0:T(8,128)(2,1)}, u32[]{:S(2)}, u32[]{:S(2)}) %collective-permute-start.3) | collective-permute-done | bytes 196640 | tf_op jit(solution)/shard_map/ppermute | solution.py:489
  58.5 15.1 %collective-permute-done.4 = bf16[64,1536]{1,0:T(8,128)(2,1)} collective-permute-done((bf16[64,1536]{1,0:T(8,128)(2,1)}, bf16[64,1536]{1,0:T(8,128)(2,1)}, u32[]{:S(2)}, u32[]{:S(2)}) %collective-permute-start.4) | collective-permute-done | bytes 196640 | tf_op jit(solution)/shard_map/ppermute | solution.py:489
  96.3 8.8 collective-permute-done.7
  106.9 13.0 %collective-permute-done.9 = bf16[2,4,32,1536]{3,2,0,1:T(8,128)(2,1)S(1)} collective-permute-done((bf16[2,4,32,1536]{3,2,0,1:T(8,128)(2,1)S(1)}, bf16[2,4,32,1536]{3,2,0,1:T(8,128)(2,1)S(1)}, u32[]{:S(2)}, u32[]{:S(2)}) %collective-permute-start.9) | collective-permute-done | bytes 786464 | tf_op jit(solution)/shard_map/ppermute | solution.py:486
  120.2 7.0 collective-permute-done.11
  132.2 9.8 %collective-permute-done.15 = bf16[4,64,1024]{2,1,0:T(8,128)(2,1)S(1)} collective-permute-done((bf16[4,64,1024]{2,1,0:T(8,128)(2,1)S(1)}, bf16[4,64,1024]{2,1,0:T(8,128)(2,1)S(1)}, u32[]{:S(2)}, u32[]{:S(2)}) %collective-permute-start.15) | collective-permute-done | bytes 524320 | tf_op jit(solution)/shard_map/ppermute | solution.py:486
  155.9 19.9 %collective-permute-done.23 = bf16[2,4,64,1024]{3,2,1,0:T(8,128)(2,1)} collective-permute-done((bf16[2,4,64,1024]{3,2,1,0:T(8,128)(2,1)}, bf16[2,4,64,1024]{3,2,1,0:T(8,128)(2,1)}, u32[]{:S(2)}, u32[]{:S(2)}) %collective-permute-start.23) | collective-permute-done | bytes 1048608 | tf_op jit(solution)/shard_map/ppermute | solution.py:486
  228.7 6.8 out.1
  239.4 19.7 %collective-permute-done.28 = bf16[128,2048]{1,0:T(8,128)(2,1)} collective-permute-done((bf16[128,2048]{1,0:T(8,128)(2,1)}, bf16[128,2048]{1,0:T(8,128)(2,1)}, u32[]{:S(2)}, u32[]{:S(2)}) %collective-permute-start.28) | collective-permute-done | bytes 524320 | tf_op jit(solution)/shard_map/ppermute | solution.py:505
  262.9 21.3 %collective-permute-done.30 = bf16[128,2048]{1,0:T(8,128)(2,1)S(1)} collective-permute-done((bf16[128,2048]{1,0:T(8,128)(2,1)}, bf16[128,2048]{1,0:T(8,128)(2,1)S(1)}, u32[]{:S(2)}, u32[]{:S(2)}) %collective-permute-start.30) | collective-permute-done | bytes 524320 | tf_op jit(solution)/shard_map/ppermute | solution.py:505
  285.6 45.8 %collective-permute-done.31 = bf16[256,2048]{1,0:T(8,128)(2,1)S(1)} collective-permute-done((bf16[256,2048]{1,0:T(8,128)(2,1)S(1)}, bf16[256,2048]{1,0:T(8,128)(2,1)S(1)}, u32[]{:S(2)}, u32[]{:S(2)}) %collective-permute-start.31) | collective-permute-done | bytes 1048608 | tf_op jit(solution)/shard_map/ppermute | solution.py:486
  355.4 62.2 %collective-permute-done.36 = bf16[256,1536]{1,0:T(8,128)(2,1)} collective-permute-done((bf16[256,1536]{1,0:T(8,128)(2,1)}, bf16[256,1536]{1,0:T(8,128)(2,1)}, u32[]{:S(2)}, u32[]{:S(2)}) %collective-permute-start.36) | collective-permute-done | bytes 786464 | tf_op jit(solution)/shard_map/ppermute | solution.py:489
  435.9 69.6 %expert_pass.1 = (bf16[2048,2048]{1,0:T(8,128)(2,1)}, bf16[2048,2048]{1,0:T(8,128)(2,1)}, bf16[2048,2048]{1,0:T(8,128)(2,1)}, bf16[2048,128]{1,0:T(8,128)(2,1)},...) custom-call(s32[4]{0:T(128)} %and_select_fusion.1.at_ref, ...), custom_call_target="tpu_custom_call" | custom-call | flops 1 | bytes 1 | tf_op jit(solution)/shard_map/expert_pass/pallas_call | solution.py:401
  505.5 9.4 grad_pass.6
  515.0 14.0 %grad_pass.8 = (bf16[2,512,1536]{2,1,0:T(8,128)(2,1)}, f32[2,512,128]{2,1,0:T(8,128)}) custom-call(s32[1]{0:T(128)} %bitcast.76.shard_ref, bf16[2048,2048]{1,0:T(8,128)(2,1)} %constant_dynamic-update-slice_fusion.4.x_ref.refs_0_, bf16[2048,2048]{1,0:T(8,128)(2,1)} %get-tuple-element.167.refs_1_, bf16[2048,1024]{1,0:T(8,128)(2,1)} %get-tuple-element.168.refs_2_, ...), custom_call_target="tpu_custom_call" | custom-call | flops 6442450944 | bytes 37748736 | tf_op jit(solution)/shard_map/grad_pass/pallas_call | solution.py:463
  536.1 8.7 grad_pass.7
  548.3 9.3 grad_pass.10
  557.6 8.6 grad_pass.11
  566.2 12.4 %grad_pass.9 = bf16[2,512,1536]{2,1,0:T(8,128)(2,1)} custom-call(s32[1]{0:T(128)} %bitcast.76.shard_ref, bf16[2048,2048]{1,0:T(8,128)(2,1)} %constant_dynamic-update-slice_fusion.4.x_ref.refs_0_, bf16[2048,2048]{1,0:T(8,128)(2,1)} %get-tuple-element.167.refs_1_, bf16[2048,1024]{1,0:T(8,128)(2,1)} %get-tuple-element.173.refs_2_, ...), custom_call_target="tpu_custom_call" | custom-call | flops 6442450944 | bytes 37748736 | tf_op jit(solution)/shard_map/grad_pass/pallas_call | solution.py:463
  597.0 17.1 %collective-permute-done.47 = bf16[256,2048]{1,0:T(8,128)(2,1)S(1)} collective-permute-done((bf16[256,2048]{1,0:T(8,128)(2,1)S(1)}, bf16[256,2048]{1,0:T(8,128)(2,1)S(1)}, u32[]{:S(2)}, u32[]{:S(2)}) %collective-permute-start.47) | collective-permute-done | bytes 1048608 | tf_op jit(solution)/shard_map/ppermute | solution.py:486
  623.1 12.2 %collective-permute-done.52 = bf16[128,2048]{1,0:T(8,128)(2,1)S(1)} collective-permute-done((bf16[128,2048]{1,0:T(8,128)(2,1)S(1)}, bf16[128,2048]{1,0:T(8,128)(2,1)S(1)}, u32[]{:S(2)}, u32[]{:S(2)}) %collective-permute-start.52) | collective-permute-done | bytes 524320 | tf_op jit(solution)/shard_map/ppermute | solution.py:505
  635.3 27.1 %collective-permute-done.51 = bf16[128,2048]{1,0:T(8,128)(2,1)S(1)} collective-permute-done((bf16[128,2048]{1,0:T(8,128)(2,1)S(1)}, bf16[128,2048]{1,0:T(8,128)(2,1)S(1)}, u32[]{:S(2)}, u32[]{:S(2)}) %collective-permute-start.51) | collective-permute-done | bytes 524320 | tf_op jit(solution)/shard_map/ppermute | solution.py:505
  663.7 9.0 out_back.1
  686.4 12.7 %attention_back.1 = (f32[4,2,64,512]{3,2,1,0:T(8,128)S(1)}, f32[4,2,64,512]{3,2,1,0:T(8,128)S(1)}, bf16[4,2,64,512]{3,2,1,0:T(8,128)(2,1)S(1)}, f32[4,4,2,64,2]{4,3,2,1,0:T(8,128)S(1)}, f32[2,2,512]{2,1,0:T(2,128)S(1)}) custom-call(f32[4,2,64,1536]{3,2,1,0:T(8,128)S(1)} %bitcast.335, f32[4,2,64,1536]{3,2,1,0:T(8,128)S(1)} %bitcast.336, ...), custom_call_target="tpu_custom_call" | custom-call | flops 1 | bytes 1 | tf_op jit(solution)/shard_map/attention_back/pallas_call | solution.py:166
  716.3 6.7 convolution_convert_fusion
  723.0 6.7 collective-permute-done.59
  736.6 7.8 out_grad.1
  747.2 30.3 %collective-permute-done.61 = bf16[128,2048]{1,0:T(8,128)(2,1)S(1)} collective-permute-done((bf16[128,2048]{1,0:T(8,128)(2,1)}, bf16[128,2048]{1,0:T(8,128)(2,1)S(1)}, u32[]{:S(2)}, u32[]{:S(2)}) %collective-permute-start.61) | collective-permute-done | bytes 524320 | tf_op jit(solution)/shard_map/ppermute | solution.py:489
  826.5 11.4 %collective-permute-done.73 = bf16[2,256,768]{2,1,0:T(8,128)(2,1)S(1)} collective-permute-done((bf16[2,256,768]{2,1,0:T(8,128)(2,1)S(1)}, bf16[2,256,768]{2,1,0:T(8,128)(2,1)S(1)}, u32[]{:S(2)}, u32[]{:S(2)}) %collective-permute-start.73) | collective-permute-done | bytes 786464 | tf_op jit(solution)/shard_map/ppermute | solution.py:486
  854.5 19.5 %collective-permute-done.72 = bf16[256,768]{1,0:T(8,128)(2,1)S(1)} collective-permute-done((bf16[256,768]{1,0:T(8,128)(2,1)S(1)}, bf16[256,768]{1,0:T(8,128)(2,1)S(1)}, u32[]{:S(2)}, u32[]{:S(2)}) %collective-permute-start.72) | collective-permute-done | bytes 393248 | tf_op jit(solution)/shard_map/ppermute | solution.py:486
  877.3 37.5 %collective-permute-done.75.refs_2_ = bf16[512,1536]{1,0:T(8,128)(2,1)S(1)} collective-permute-done((bf16[512,1536]{1,0:T(8,128)(2,1)S(1)}, bf16[512,1536]{1,0:T(8,128)(2,1)S(1)}, u32[]{:S(2)}, u32[]{:S(2)}) %collective-permute-start.75) | collective-permute-done | bytes 1572896 | tf_op jit(solution)/shard_map/ppermute | solution.py:489
  939.7 18.8 %collective-permute-done.85 = bf16[64,2048]{1,0:T(8,128)(2,1)} collective-permute-done((bf16[64,2048]{1,0:T(8,128)(2,1)}, bf16[64,2048]{1,0:T(8,128)(2,1)}, u32[]{:S(2)}, u32[]{:S(2)}) %collective-permute-start.85) | collective-permute-done | bytes 262176 | tf_op jit(solution)/shard_map/ppermute | solution.py:489
  (521 shorter events, 359.4 us)
Async XLA Ops:
  7.2 207.4 %all-gather.5.cloned.1.call-start = ((), (), s32[]{:S(2)}) async-start(), calls=%async_computation.4 | async-start | bytes 2949120 | tf_op jit(solution)/shard_map/all_gather | solution.py:659
  10.8 68.5 %collective-permute-start = (bf16[128,2048]{1,0:T(8,128)(2,1)}, bf16[128,2048]{1,0:T(8,128)(2,1)}, u32[]{:S(2)}, u32[]{:S(2)}) collective-permute-start(bf16[128,2048]{1,0:T(8,128)(2,1)} %fusion.16), channel_id=1, source_target_pairs={{0,3},{1,0},{2,1},{3,2},{4,7},{5,4},{6,5},{7,6},{8,11},{9,8},{10,9... | collective-permute-start | bytes 1572872 | tf_op jit(solution)/shard_map/ppermute | solution.py:489
  15.8 63.4 %collective-permute-start.1 = (bf16[128,2048]{1,0:T(8,128)(2,1)}, bf16[128,2048]{1,0:T(8,128)(2,1)}, u32[]{:S(2)}, u32[]{:S(2)}) collective-permute-start(bf16[128,2048]{1,0:T(8,128)(2,1)} %fusion.16), channel_id=1, source_target_pairs={{0,2},{1,3},{2,0},{3,1},{4,6},{5,7},{6,4},{7,5},{8,10},{9,11},{10,... | collective-permute-start | bytes 1572872 | tf_op jit(solution)/shard_map/ppermute | solution.py:489
  15.8 63.4 %collective-permute-start.2 = (bf16[128,2048]{1,0:T(8,128)(2,1)}, bf16[128,2048]{1,0:T(8,128)(2,1)}, u32[]{:S(2)}, u32[]{:S(2)}) collective-permute-start(bf16[128,2048]{1,0:T(8,128)(2,1)} %fusion.16), channel_id=1, source_target_pairs={{0,1},{1,2},{2,3},{3,0},{4,5},{5,6},{6,7},{7,4},{8,9},{9,10},{10,1... | collective-permute-start | bytes 1572872 | tf_op jit(solution)/shard_map/ppermute | solution.py:489
  27.4 46.1 %collective-permute-start.4 = (bf16[64,1536]{1,0:T(8,128)(2,1)}, bf16[64,1536]{1,0:T(8,128)(2,1)}, u32[]{:S(2)}, u32[]{:S(2)}) collective-permute-start(bf16[64,1536]{1,0:T(8,128)(2,1)} %get-tuple-element.374), channel_id=1, source_target_pairs={{0,2},{1,3},{2,0},{3,1},{4,6},{5,7},{6,4},{7,5},{8,10},{9,11},{10,... | collective-permute-start | bytes 589832 | tf_op jit(solution)/shard_map/ppermute | solution.py:489
  82.4 37.8 %collective-permute-start.10 = (bf16[64,2048]{1,0:T(8,128)(2,1)S(1)}, bf16[64,2048]{1,0:T(8,128)(2,1)S(1)}, u32[]{:S(2)}, u32[]{:S(2)}) collective-permute-start(bf16[64,2048]{1,0:T(8,128)(2,1)S(1)} %constant_dynamic-slice_fusion.20), channel_id=1, source_target_pairs={{0,3},{1,0},{2,1},{3,2},{4,7},{5,4},{6,5},{7,6},{8,11},{9,8},{10,9... | collective-permute-start | bytes 786440 | tf_op jit(solution)/shard_map/ppermute | solution.py:489
  85.7 41.5 %collective-permute-start.11 = (bf16[64,2048]{1,0:T(8,128)(2,1)S(1)}, bf16[64,2048]{1,0:T(8,128)(2,1)S(1)}, u32[]{:S(2)}, u32[]{:S(2)}) collective-permute-start(bf16[64,2048]{1,0:T(8,128)(2,1)S(1)} %constant_dynamic-slice_fusion.20), channel_id=1, source_target_pairs={{0,2},{1,3},{2,0},{3,1},{4,6},{5,7},{6,4},{7,5},{8,10},{9,11},{10,... | collective-permute-start | bytes 786440 | tf_op jit(solution)/shard_map/ppermute | solution.py:489
  86.3 40.9 %collective-permute-start.12 = (bf16[64,2048]{1,0:T(8,128)(2,1)S(1)}, bf16[64,2048]{1,0:T(8,128)(2,1)S(1)}, u32[]{:S(2)}, u32[]{:S(2)}) collective-permute-start(bf16[64,2048]{1,0:T(8,128)(2,1)S(1)} %constant_dynamic-slice_fusion.20), channel_id=1, source_target_pairs={{0,1},{1,2},{2,3},{3,0},{4,5},{5,6},{6,7},{7,4},{8,9},{9,10},{10,1... | collective-permute-start | bytes 786440 | tf_op jit(solution)/shard_map/ppermute | solution.py:489
  91.2 56.1 %collective-permute-start.17 = (bf16[256,1536]{1,0:T(8,128)(2,1)S(1)}, bf16[256,1536]{1,0:T(8,128)(2,1)S(1)}, u32[]{:S(2)}, u32[]{:S(2)}) collective-permute-start(bf16[256,1536]{1,0:T(8,128)(2,1)S(1)} %get-tuple-element.343), channel_id=1, source_target_pairs={{0,2},{1,3},{2,0},{3,1},{4,6},{5,7},{6,4},{7,5},{8,10},{9,11},{10,... | collective-permute-start | bytes 2359304 | tf_op jit(solution)/shard_map/ppermute | solution.py:489
  155.7 180.0 %all-gather.7.cloned.1.call-start = ((), (), s32[]{:S(2)}) async-start(), calls=%async_computation.5 | async-start | bytes 11796480 | tf_op jit(solution)/shard_map/all_gather | solution.py:662
  214.6 565.1 %reduce-scatter.3.cloned.1.call-start = ((), (), s32[]{:S(2)}) async-start(), calls=%async_computation.2 | async-start | bytes 10485760 | tf_op jit(solution)/shard_map/reduce_scatter | solution.py:852
  238.6 45.7 %collective-permute-start.30 = (bf16[128,2048]{1,0:T(8,128)(2,1)}, bf16[128,2048]{1,0:T(8,128)(2,1)S(1)}, u32[]{:S(2)}, u32[]{:S(2)}) collective-permute-start(bf16[128,2048]{1,0:T(8,128)(2,1)} %get-tuple-element.146), channel_id=1, source_target_pairs={{0,2},{1,3},{2,0},{3,1},{4,6},{5,7},{6,4},{7,5},{8,10},{9,11},{10,... | collective-permute-start | bytes 1572872 | tf_op jit(solution)/shard_map/ppermute | solution.py:505
  284.4 47.0 %collective-permute-start.31 = (bf16[256,2048]{1,0:T(8,128)(2,1)S(1)}, bf16[256,2048]{1,0:T(8,128)(2,1)S(1)}, u32[]{:S(2)}, u32[]{:S(2)}) collective-permute-start(bf16[256,2048]{1,0:T(8,128)(2,1)S(1)} %pad_maximum_fusion.16), channel_id=1, source_target_pairs={{0,8},{4,12},{8,0},{12,4},{16,24},{20,28},{24,16},{28,20},{1,9},{5... | collective-permute-start | bytes 3145736 | tf_op jit(solution)/shard_map/ppermute | solution.py:486
  285.1 48.0 %collective-permute-start.32 = (bf16[256,2048]{1,0:T(8,128)(2,1)S(1)}, bf16[256,2048]{1,0:T(8,128)(2,1)S(1)}, u32[]{:S(2)}, u32[]{:S(2)}) collective-permute-start(bf16[256,2048]{1,0:T(8,128)(2,1)S(1)} %pad_maximum_fusion.17), channel_id=1, source_target_pairs={{0,16},{4,20},{8,24},{12,28},{16,0},{20,4},{24,8},{28,12},{1,17},{... | collective-permute-start | bytes 3145736 | tf_op jit(solution)/shard_map/ppermute | solution.py:486
  285.6 63.3 %collective-permute-start.33 = (bf16[512,1536]{1,0:T(8,128)(2,1)}, bf16[512,1536]{1,0:T(8,128)(2,1)}, u32[]{:S(2)}, u32[]{:S(2)}) collective-permute-start(bf16[512,1536]{1,0:T(8,128)(2,1)} %pack.5), channel_id=1, source_target_pairs={{0,1},{1,2},{2,3},{3,0},{4,5},{5,6},{6,7},{7,4},{8,9},{9,10},{10,1... | collective-permute-start | bytes 4718600 | tf_op jit(solution)/shard_map/ppermute | solution.py:489
  349.0 71.2 %collective-permute-start.34 = (bf16[512,2048]{1,0:T(8,128)(2,1)}, bf16[512,2048]{1,0:T(8,128)(2,1)}, u32[]{:S(2)}, u32[]{:S(2)}) collective-permute-start(bf16[512,2048]{1,0:T(8,128)(2,1)} %pad_maximum_fusion.5), channel_id=1, source_target_pairs={{0,16},{4,20},{8,24},{12,28},{16,0},{20,4},{24,8},{28,12},{1,17},{... | collective-permute-start | bytes 6291464 | tf_op jit(solution)/shard_map/ppermute | solution.py:486
  350.2 69.9 %collective-permute-start.37 = (bf16[512,1536]{1,0:T(8,128)(2,1)}, bf16[512,1536]{1,0:T(8,128)(2,1)}, u32[]{:S(2)}, u32[]{:S(2)}) collective-permute-start(bf16[512,1536]{1,0:T(8,128)(2,1)} %pack.7), channel_id=1, source_target_pairs={{0,3},{1,0},{2,1},{3,2},{4,7},{5,4},{6,5},{7,6},{8,11},{9,8},{10,9... | collective-permute-start | bytes 4718600 | tf_op jit(solution)/shard_map/ppermute | solution.py:489
  352.8 64.7 %collective-permute-start.36 = (bf16[256,1536]{1,0:T(8,128)(2,1)}, bf16[256,1536]{1,0:T(8,128)(2,1)}, u32[]{:S(2)}, u32[]{:S(2)}) collective-permute-start(bf16[256,1536]{1,0:T(8,128)(2,1)} %get-tuple-element.164), channel_id=1, source_target_pairs={{0,2},{1,3},{2,0},{3,1},{4,6},{5,7},{6,4},{7,5},{8,10},{9,11},{10,... | collective-permute-start | bytes 2359304 | tf_op jit(solution)/shard_map/ppermute | solution.py:489
  352.8 79.9 %collective-permute-start.35 = (bf16[512,2048]{1,0:T(8,128)(2,1)}, bf16[512,2048]{1,0:T(8,128)(2,1)}, u32[]{:S(2)}, u32[]{:S(2)}) collective-permute-start(bf16[512,2048]{1,0:T(8,128)(2,1)} %pad_maximum_fusion.6), channel_id=1, source_target_pairs={{0,8},{4,12},{8,0},{12,4},{16,24},{20,28},{24,16},{28,20},{1,9},{5... | collective-permute-start | bytes 6291464 | tf_op jit(solution)/shard_map/ppermute | solution.py:486
  528.9 53.5 %collective-permute-start.44 = (bf16[2,512,1536]{2,1,0:T(8,128)(2,1)}, bf16[2,512,1536]{2,1,0:T(8,128)(2,1)S(1)}, u32[]{:S(2)}, u32[]{:S(2)}) collective-permute-start(bf16[2,512,1536]{2,1,0:T(8,128)(2,1)} %get-tuple-element.175), channel_id=1, source_target_pairs={{0,4},{4,0},{8,12},{12,8},{16,20},{20,16},{24,28},{28,24},{1,5},{5... | collective-permute-start | bytes 9437192 | tf_op jit(solution)/shard_map/ppermute | solution.py:486
  534.1 47.9 %collective-permute-start.42 = (bf16[512,2048]{1,0:T(8,128)(2,1)}, bf16[512,2048]{1,0:T(8,128)(2,1)}, u32[]{:S(2)}, u32[]{:S(2)}) collective-permute-start(bf16[512,2048]{1,0:T(8,128)(2,1)} %get-tuple-element.314), channel_id=1, source_target_pairs={{0,16},{4,20},{8,24},{12,28},{16,0},{20,4},{24,8},{28,12},{1,17},{... | collective-permute-start | bytes 6291464 | tf_op jit(solution)/shard_map/ppermute | solution.py:486
  534.7 47.6 %collective-permute-start.43 = (bf16[512,2048]{1,0:T(8,128)(2,1)}, bf16[512,2048]{1,0:T(8,128)(2,1)}, u32[]{:S(2)}, u32[]{:S(2)}) collective-permute-start(bf16[512,2048]{1,0:T(8,128)(2,1)} %get-tuple-element.313), channel_id=1, source_target_pairs={{0,8},{4,12},{8,0},{12,4},{16,24},{20,28},{24,16},{28,20},{1,9},{5... | collective-permute-start | bytes 6291464 | tf_op jit(solution)/shard_map/ppermute | solution.py:486
  547.7 37.8 %collective-permute-start.46 = (bf16[512,1536]{1,0:T(8,128)(2,1)}, bf16[512,1536]{1,0:T(8,128)(2,1)S(1)}, u32[]{:S(2)}, u32[]{:S(2)}) collective-permute-start(bf16[512,1536]{1,0:T(8,128)(2,1)} %fusion.3), channel_id=1, source_target_pairs={{0,1},{1,2},{2,3},{3,0},{4,5},{5,6},{6,7},{7,4},{8,9},{9,10},{10,1... | collective-permute-start | bytes 4718600 | tf_op jit(solution)/shard_map/ppermute | solution.py:489
  617.1 309.0 %reduce-scatter.5.cloned.1.call-start = ((), (), s32[]{:S(2)}) async-start(), calls=%async_computation.3 | async-start | bytes 2621440 | tf_op jit(solution)/shard_map/reduce_scatter | solution.py:911
  620.2 42.2 %collective-permute-start.51 = (bf16[128,2048]{1,0:T(8,128)(2,1)S(1)}, bf16[128,2048]{1,0:T(8,128)(2,1)S(1)}, u32[]{:S(2)}, u32[]{:S(2)}) collective-permute-start(bf16[128,2048]{1,0:T(8,128)(2,1)S(1)} %get-tuple-element.355), channel_id=1, source_target_pairs={{0,2},{1,3},{2,0},{3,1},{4,6},{5,7},{6,4},{7,5},{8,10},{9,11},{10,... | collective-permute-start | bytes 1572872 | tf_op jit(solution)/shard_map/ppermute | solution.py:505
  620.2 42.1 %collective-permute-start.50 = (bf16[128,2048]{1,0:T(8,128)(2,1)S(1)}, bf16[128,2048]{1,0:T(8,128)(2,1)S(1)}, u32[]{:S(2)}, u32[]{:S(2)}) collective-permute-start(bf16[128,2048]{1,0:T(8,128)(2,1)S(1)} %broadcast_select_fusion.2), channel_id=1, source_target_pairs={{0,1},{1,0},{2,3},{3,2},{4,5},{5,4},{6,7},{7,6},{8,9},{9,8},{10,11... | collective-permute-start | bytes 1572872 | tf_op jit(solution)/shard_map/ppermute | solution.py:505
  734.5 43.0 %collective-permute-start.61 = (bf16[128,2048]{1,0:T(8,128)(2,1)}, bf16[128,2048]{1,0:T(8,128)(2,1)S(1)}, u32[]{:S(2)}, u32[]{:S(2)}) collective-permute-start(bf16[128,2048]{1,0:T(8,128)(2,1)} %get-tuple-element.333), channel_id=1, source_target_pairs={{0,2},{1,3},{2,0},{3,1},{4,6},{5,7},{6,4},{7,5},{8,10},{9,11},{10,... | collective-permute-start | bytes 1572872 | tf_op jit(solution)/shard_map/ppermute | solution.py:489
  734.5 43.8 %collective-permute-start.60 = (bf16[128,2048]{1,0:T(8,128)(2,1)S(1)}, bf16[128,2048]{1,0:T(8,128)(2,1)}, u32[]{:S(2)}, u32[]{:S(2)}) collective-permute-start(bf16[128,2048]{1,0:T(8,128)(2,1)S(1)} %get-tuple-element.331), channel_id=1, source_target_pairs={{0,1},{1,2},{2,3},{3,0},{4,5},{5,6},{6,7},{7,4},{8,9},{9,10},{10,1... | collective-permute-start | bytes 1572872 | tf_op jit(solution)/shard_map/ppermute | solution.py:489
  799.7 39.7 %collective-permute-start.79 = (bf16[2,2,256,2048]{3,2,1,0:T(8,128)(2,1)}, bf16[2,2,256,2048]{3,2,1,0:T(8,128)(2,1)}, u32[]{:S(2)}, u32[]{:S(2)}) collective-permute-start(bf16[2,2,256,2048]{3,2,1,0:T(8,128)(2,1)} %dynamic-slice_bitcast_fusion), channel_id=1, source_target_pairs={{0,4},{4,0},{8,12},{12,8},{16,20},{20,16},{24,28},{28,24},{1,5},{5... | collective-permute-start | bytes 12582920 | tf_op jit(solution)/shard_map/ppermute | solution.py:486
  823.7 91.1 %collective-permute-start.75 = (bf16[512,1536]{1,0:T(8,128)(2,1)S(1)}, bf16[512,1536]{1,0:T(8,128)(2,1)S(1)}, u32[]{:S(2)}, u32[]{:S(2)}) collective-permute-start(bf16[512,1536]{1,0:T(8,128)(2,1)S(1)} %copy-done.48), channel_id=1, source_target_pairs={{0,2},{1,3},{2,0},{3,1},{4,6},{5,7},{6,4},{7,5},{8,10},{9,11},{10,... | collective-permute-start | bytes 4718600 | tf_op jit(solution)/shard_map/ppermute | solution.py:489
  874.6 45.0 %collective-permute-start.83 = (bf16[256,1024]{1,0:T(8,128)(2,1)S(1)}, bf16[256,1024]{1,0:T(8,128)(2,1)S(1)}, u32[]{:S(2)}, u32[]{:S(2)}) collective-permute-start(bf16[256,1024]{1,0:T(8,128)(2,1)S(1)} %dynamic-slice_bitcast_fusion.5), channel_id=1, source_target_pairs={{0,8},{4,12},{8,0},{12,4},{16,24},{20,28},{24,16},{28,20},{1,9},{5... | collective-permute-start | bytes 1572872 | tf_op jit(solution)/shard_map/ppermute | solution.py:486
  876.8 42.9 %collective-permute-start.81 = (bf16[256,1024]{1,0:T(8,128)(2,1)S(1)}, bf16[256,1024]{1,0:T(8,128)(2,1)S(1)}, u32[]{:S(2)}, u32[]{:S(2)}) collective-permute-start(bf16[256,1024]{1,0:T(8,128)(2,1)S(1)} %dynamic-slice_bitcast_fusion.6), channel_id=1, source_target_pairs={{0,16},{4,20},{8,24},{12,28},{16,0},{20,4},{24,8},{28,12},{1,17},{... | collective-permute-start | bytes 1572872 | tf_op jit(solution)/shard_map/ppermute | solution.py:486
  (131 other events, 1520.4 us)
Sparse Core Ops, SparseCore 0:
  155.8 49.9 all-gather.4
  214.8 116.7 all-gather.6
  617.2 84.7 reduce-scatter.2
  804.1 69.7 reduce-scatter.4
